TPU v7x, 128 devices: a whole 4x4x4 slice. The times are simulated.
128 devices in a mesh: basis: 32 (over x, z, core), aux: 4 (over y).
Axes of the slice: x: 4, y: 4, z: 4, core: 2. Of those that a mesh axis runs over, the one named last changes fastest.
Arguments:
- factors: bfloat16 [65536, 16, 200], P('basis', 'aux'), may hold values from -0.09375 to 0.09375
- orbitals: bfloat16 [65536, 200], P('basis'), may hold values from -6 to 6
- block_slot: int32 [256], replicated, may hold values from 0 to 255, as said below
- pair_list: int32 [2048, 2], replicated, may hold values from 0 to 255, as said below
- pair_owner: int32 [2048], replicated, may hold values from -1 to 31, as said below
Outputs:
- exchange_product: bfloat16 [65536, 200], P('basis')
Inputs may be any that keep to these rules, and one draw needn't show every extreme that they name: `block_slot`: a permutation of the 256 shell blocks onto the 256 storage slots. `pair_list`: each entry names two different shell blocks, the smaller first. Over the live pairs of one owner, the blocks stored on any one index of basis number at most 2, and some owner reaches 2 from some index. `pair_owner`: each index of basis owns at most 64 live pairs, and one owns exactly 64.
All inputs are finite; a program needn't handle non-finite values.
Results may differ from a plain program's by a relative error of at most 0.0057.
Values may be sent and summed in bfloat16 or wider, within the bound.
No kernel may reach another device: no remote copies, remote signals or barrier semaphores. Data moves between devices by JAX's collectives and lax.ppermute only.
A program may use at most 256 MiB of HBM per device.

v0:
```python
import jax
import jax.numpy as jnp
from jax import lax
from jax.sharding import PartitionSpec as P

BLOCK = 256
SEND_CAP = 2
PAIR_CAP = 64


def shards(factors, orbitals, block_slot, pair_list, pair_owner):
    ndev = lax.axis_size("basis")
    me_index = lax.axis_index("basis")
    blocks_dev = factors.shape[0] // BLOCK
    aux_dev = factors.shape[1]
    width = factors.shape[2]
    stored_b = factors.reshape(blocks_dev, BLOCK * aux_dev * width)
    stored_x = orbitals.reshape(blocks_dev, BLOCK * width)
    slot_a = block_slot[pair_list[:, 0]]
    slot_b = block_slot[pair_list[:, 1]]
    live = pair_owner >= 0
    target = jnp.maximum(pair_owner, 0)
    source_a = slot_a // blocks_dev
    source_b = slot_b // blocks_dev
    local_a = slot_a % blocks_dev
    local_b_pos = slot_b % blocks_dev
    hit_a = (live & (source_a == me_index)).astype(jnp.int32)
    hit_b = (live & (source_b == me_index)).astype(jnp.int32)
    needed = jnp.zeros((ndev, blocks_dev), jnp.int32)
    needed = needed.at[target, local_a].max(hit_a).at[target, local_b_pos].max(hit_b)
    ranks = jnp.cumsum(needed, axis=1) - 1
    slot_ids = jnp.arange(SEND_CAP, dtype=jnp.int32)
    positions = jnp.arange(blocks_dev, dtype=jnp.int32)
    chosen = (needed[:, None, :] == 1) & (ranks[:, None, :] == slot_ids[None, :, None])
    send_local = jnp.sum(jnp.where(chosen, positions[None, None, :], 0), axis=2).reshape(-1)
    send_live = jnp.any(chosen, axis=2).reshape(-1)
    select_send = (send_local[:, None] == positions[None, :]).astype(jnp.bfloat16)
    send_b = jnp.dot(select_send, stored_b, preferred_element_type=jnp.float32).astype(jnp.bfloat16)
    send_b = send_b.reshape(-1, BLOCK, aux_dev * width)
    send_x = jnp.dot(select_send, stored_x, preferred_element_type=jnp.float32).astype(jnp.bfloat16)
    send_x = send_x.reshape(-1, BLOCK, width)
    recv_b, recv_x = (
        lax.all_to_all(send_b, "basis", split_axis=0, concat_axis=0, tiled=True),
        lax.all_to_all(send_x, "basis", split_axis=0, concat_axis=0, tiled=True),
    )
    recv_rows = ndev * SEND_CAP
    flat_b = recv_b.reshape(recv_rows, BLOCK * aux_dev * width)
    flat_x = recv_x.reshape(recv_rows, BLOCK * width)
    row_ids = jnp.arange(recv_rows, dtype=jnp.int32)
    mine = pair_owner == me_index
    mine_int = mine.astype(jnp.int32)
    used = (
        jnp.zeros((ndev * blocks_dev,), jnp.int32).at[slot_a].max(mine_int).at[slot_b].max(mine_int)
    )
    place = (jnp.cumsum(used.reshape(ndev, blocks_dev), axis=1) - 1).reshape(-1)
    top_row = recv_rows - 1
    index_a = jnp.clip(source_a * SEND_CAP + place[slot_a], 0, top_row)
    index_b = jnp.clip(source_b * SEND_CAP + place[slot_b], 0, top_row)
    picked = jnp.nonzero(mine, size=PAIR_CAP, fill_value=0)[0].astype(jnp.int32)
    pick_weight = mine[picked].astype(jnp.float32)
    rows_a = index_a[picked]
    rows_b = index_b[picked]
    group = 16

    def tile_step(turn, totals):
        start = turn * group
        ra = lax.dynamic_slice_in_dim(rows_a, start, group)
        rb = lax.dynamic_slice_in_dim(rows_b, start, group)
        weight = lax.dynamic_slice_in_dim(pick_weight, start, group)
        match_a = ra[:, None] == row_ids[None, :]
        match_b = rb[:, None] == row_ids[None, :]
        pick_a = match_a.astype(jnp.bfloat16)
        pick_b = match_b.astype(jnp.bfloat16)
        left = jnp.dot(pick_a, flat_b, preferred_element_type=jnp.float32).astype(jnp.bfloat16)
        right = jnp.dot(pick_b, flat_b, preferred_element_type=jnp.float32).astype(jnp.bfloat16)
        left = left.reshape(group, BLOCK, aux_dev * width)
        right = right.reshape(group, BLOCK, aux_dev * width)
        tile = jnp.einsum("gmk,gnk->gmn", left, right, preferred_element_type=jnp.float32).astype(
            jnp.bfloat16
        )
        orb_a = jnp.dot(pick_a, flat_x, preferred_element_type=jnp.float32).astype(jnp.bfloat16)
        orb_b = jnp.dot(pick_b, flat_x, preferred_element_type=jnp.float32).astype(jnp.bfloat16)
        orb_a = orb_a.reshape(group, BLOCK, width)
        orb_b = orb_b.reshape(group, BLOCK, width)
        to_a = jnp.einsum("gmn,gnj->gmj", tile, orb_b, preferred_element_type=jnp.float32)
        to_b = jnp.einsum("gmn,gmj->gnj", tile, orb_a, preferred_element_type=jnp.float32)
        moved = jnp.concatenate([to_a, to_b], axis=0).reshape(2 * group, BLOCK * width)
        places = jnp.concatenate([match_a.astype(jnp.float32), match_b.astype(jnp.float32)], axis=0)
        places = places * jnp.concatenate([weight, weight], axis=0)[:, None]
        update = jnp.dot(
            places.T, moved, preferred_element_type=jnp.float32, precision=lax.Precision.HIGHEST
        )
        return totals + update

    shares = lax.fori_loop(
        0, PAIR_CAP // group, tile_step, jnp.zeros((recv_rows, BLOCK * width), jnp.float32)
    )
    shares = shares.reshape(recv_rows, BLOCK, width)
    returned = lax.all_to_all(
        shares.astype(jnp.bfloat16), "basis", split_axis=0, concat_axis=0, tiled=True
    )
    spread = ((send_local[:, None] == positions[None, :]) & send_live[:, None]).astype(jnp.bfloat16)
    partial_sum = jnp.einsum("sj,smo->jmo", spread, returned, preferred_element_type=jnp.float32)
    total = lax.psum(partial_sum.reshape(blocks_dev * BLOCK, width), "aux")
    return total.astype(jnp.bfloat16)


def solution(mesh):
    return jax.shard_map(
        shards,
        mesh=mesh,
        in_specs=(P("basis", "aux", None), P("basis", None), P(), P(), P()),
        out_specs=P("basis", None),
        check_vma=False,
    )
```

profile of v0, /device:TPU:0, one launch (start us, length us, event | category | flops | bytes accessed | tf_op | source)
XLA Modules:
  0.0 1499.1 jit_solution(5989613569739887133)
XLA Ops:
  0.9 13.2 gather_fusion
  14.1 13.2 gather_fusion.1
  28.4 14.7 scatter_custom_fusion.3
  43.1 14.7 scatter_fusion.1
  65.7 27.3 %reshape.308 = bf16[64,256,200]{2,1,0:T(8,128)(2,1)} reshape(bf16[64,51200]{1,0:T(8,128)(2,1)} %convolution_convert_fusion.6) | data formatting | bytes 13107200 | tf_op jit(solution)/shard_map/reshape | solution.py:41
  93.0 10.4 copy.67
  103.4 8.9 all-to-all-start.1
  117.2 11.9 reshape.431
  132.2 13.7 convolution_convert_fusion.5
  145.8 47.9 %reshape.305 = bf16[64,256,800]{2,1,0:T(8,128)(2,1)} reshape(bf16[64,204800]{1,0:T(8,128)(2,1)} %convolution_convert_fusion.5) | data formatting | bytes 52428800 | tf_op jit(solution)/shard_map/reshape | solution.py:39
  193.7 37.0 %copy.64 = bf16[64,256,800]{1,2,0:T(8,128)(2,1)} copy(bf16[64,256,800]{2,1,0:T(8,128)(2,1)} %reshape.305) | data formatting | bytes 52428800 | tf_op jit(solution)/shard_map/reshape | solution.py:39
  238.4 14.7 scatter_custom_fusion
  253.1 14.7 scatter_fusion
  268.7 14.7 scatter_custom_fusion.2
  285.1 13.4 gather_fusion.2
  299.3 13.2 gather_fusion.4
  313.3 10.2 copy.68
  323.5 16.9 %reshape.309 = bf16[64,51200]{1,0:T(8,128)(2,1)} reshape(bf16[64,256,200]{2,1,0:T(8,128)(2,1)} %copy.68) | data formatting | bytes 13107200 | tf_op jit(solution)/shard_map/reshape | solution.py:48
  340.4 276.3 %all-to-all-done = bf16[64,256,800]{1,2,0:T(8,128)(2,1)} async-done(((bf16[64,256,800]{1,2,0:T(8,128)(2,1)}), bf16[64,256,800]{1,2,0:T(8,128)(2,1)}, u32[]{:S(2)}, u32[]{:S(2)}) %all-to-all-start) | async-done | bytes 26214432 | tf_op jit(solution)/shard_map/all_to_all | solution.py:43
  616.7 36.0 %copy.65 = bf16[64,256,800]{2,1,0:T(8,128)(2,1)} copy(bf16[64,256,800]{1,2,0:T(8,128)(2,1)} %all-to-all-done) | data formatting | bytes 52428800 | tf_op jit(solution)/shard_map/all_to_all | solution.py:43
  652.8 47.3 %reshape.306 = bf16[64,204800]{1,0:T(8,128)(2,1)} reshape(bf16[64,256,800]{2,1,0:T(8,128)(2,1)} %copy.65) | data formatting | bytes 52428800 | tf_op jit(solution)/shard_map/reshape | solution.py:47
  700.1 570.2 %while.15 = (s32[]{:T(128)}, f32[64,51200]{1,0:T(8,128)}, s32[64]{0:T(128)S(1)}, s32[64]{0:T(128)S(1)}, f32[64]{0:T(128)S(1)}, /*index=5*/bf16[64,204800]{1,0:T(...) while((s32[]{:T(128)}, f32[64,51200]{1,0:T(8,128)}, ...), condition=%wide.region_14.15_spmd.clone.clone, body=%wide.region_13.14_spmd.clone.clone.sunk | while | flops 4840892416 | bytes 229119248 | solution.py:95
  721.5 13.2 convolution_convert_fusion.12
  734.7 14.7 reshape.438
  749.5 13.3 convolution_convert_fusion.13
  762.8 14.8 reshape.439
  790.2 8.5 reshape.441
  807.8 8.5 reshape.440
  821.9 8.4 copy.79
  830.3 9.6 reshape.442
  840.1 15.9 %convolution_add_fusion.2 = f32[64,51200]{1,0:T(8,128)} fusion(f32[32,51200]{1,0:T(8,128)} %reshape.442, f32[64,51200]{1,0:T(8,128)} %get-tuple-element.288, pred[]{:T(512)S(6)} %compare.42, pred[16,64]{1,0:T(8,128)(4,1)S(1)} %get-tuple-element.274, pred[16,64]{1,0:T(8,128)(4,1)S(1)} %get-tuple-element.275, f32[32]{0:T(128)S(1)} %pad_maximum_fusion.5), kind=kOutput, calls=%fused_computation.15.clone.1 | convolution fusion | flops 1264848896 | bytes 32770176 | tf_op jit(solution)/shard_map/while/body/eval_jaxpr/dot_general | solution.py:90
  856.1 13.2 convolution_convert_fusion.12
  869.3 14.7 reshape.438
  884.1 13.3 convolution_convert_fusion.13
  897.4 14.8 reshape.439
  924.8 8.5 reshape.441
  942.4 8.5 reshape.440
  956.5 8.4 copy.79
  964.9 9.6 reshape.442
  974.7 17.8 %convolution_add_fusion.2 = f32[64,51200]{1,0:T(8,128)} fusion(f32[32,51200]{1,0:T(8,128)} %reshape.442, f32[64,51200]{1,0:T(8,128)} %get-tuple-element.288, pred[]{:T(512)S(6)} %compare.42, pred[16,64]{1,0:T(8,128)(4,1)S(1)} %get-tuple-element.274, pred[16,64]{1,0:T(8,128)(4,1)S(1)} %get-tuple-element.275, f32[32]{0:T(128)S(1)} %pad_maximum_fusion.5), kind=kOutput, calls=%fused_computation.15.clone.1 | convolution fusion | flops 1264848896 | bytes 32770176 | tf_op jit(solution)/shard_map/while/body/eval_jaxpr/dot_general | solution.py:90
  992.7 13.2 convolution_convert_fusion.12
  1005.9 14.7 reshape.438
  1020.7 13.3 convolution_convert_fusion.13
  1034.0 14.8 reshape.439
  1061.4 8.5 reshape.441
  1078.9 8.5 reshape.440
  1093.1 8.4 copy.79
  1101.5 9.6 reshape.442
  1111.3 17.8 %convolution_add_fusion.2 = f32[64,51200]{1,0:T(8,128)} fusion(f32[32,51200]{1,0:T(8,128)} %reshape.442, f32[64,51200]{1,0:T(8,128)} %get-tuple-element.288, pred[]{:T(512)S(6)} %compare.42, pred[16,64]{1,0:T(8,128)(4,1)S(1)} %get-tuple-element.274, pred[16,64]{1,0:T(8,128)(4,1)S(1)} %get-tuple-element.275, f32[32]{0:T(128)S(1)} %pad_maximum_fusion.5), kind=kOutput, calls=%fused_computation.15.clone.1 | convolution fusion | flops 1264848896 | bytes 32770176 | tf_op jit(solution)/shard_map/while/body/eval_jaxpr/dot_general | solution.py:90
  1129.2 13.2 convolution_convert_fusion.12
  1142.4 14.7 reshape.438
  1157.2 13.3 convolution_convert_fusion.13
  1170.5 14.8 reshape.439
  1197.9 8.5 reshape.441
  1215.5 8.5 reshape.440
  1229.6 8.4 copy.79
  1238.0 9.6 reshape.442
  1247.8 17.8 %convolution_add_fusion.2 = f32[64,51200]{1,0:T(8,128)} fusion(f32[32,51200]{1,0:T(8,128)} %reshape.442, f32[64,51200]{1,0:T(8,128)} %get-tuple-element.288, pred[]{:T(512)S(6)} %compare.42, pred[16,64]{1,0:T(8,128)(4,1)S(1)} %get-tuple-element.274, pred[16,64]{1,0:T(8,128)(4,1)S(1)} %get-tuple-element.275, f32[32]{0:T(128)S(1)} %pad_maximum_fusion.5), kind=kOutput, calls=%fused_computation.15.clone.1 | convolution fusion | flops 1264848896 | bytes 32770176 | tf_op jit(solution)/shard_map/while/body/eval_jaxpr/dot_general | solution.py:90
  1270.2 8.1 convert_element_type.89
  1278.3 27.3 %convert_element_type.90 = bf16[64,256,200]{2,1,0:T(8,128)(2,1)} reshape(bf16[64,51200]{1,0:T(8,128)(2,1)} %convert_element_type.89) | data formatting | bytes 13107200 | tf_op jit(solution)/shard_map/convert_element_type | solution.py:100
  1305.6 10.4 copy.69
  1316.0 56.5 %all-to-all-start.2 = ((bf16[64,256,200]{1,2,0:T(8,128)(2,1)}), bf16[64,256,200]{1,2,0:T(8,128)(2,1)}, u32[]{:S(2)}, u32[]{:S(2)}) async-start(bf16[64,256,200]{1,2,0:T(8,128)(2,1)} %copy.69), calls=%async_computation.2 | async-start | bytes 13107200 | tf_op jit(solution)/shard_map/all_to_all | solution.py:99
  1372.8 84.1 %all-to-all-done.2 = bf16[64,256,200]{1,2,0:T(8,128)(2,1)} async-done(((bf16[64,256,200]{1,2,0:T(8,128)(2,1)}), bf16[64,256,200]{1,2,0:T(8,128)(2,1)}, u32[]{:S(2)}, u32[]{:S(2)}) %all-to-all-start.2) | async-done | bytes 6553632 | tf_op jit(solution)/shard_map/all_to_all | solution.py:99
  1461.4 37.5 %all-reduce.1 = bf16[2048,200]{0,1:T(8,128)(2,1)} all-reduce(f32[2048,200]{0,1:T(8,128)S(1)} %bitcast.56), channel_id=1, replica_groups=mesh['basis'=32,'aux'=4] {'aux'}, use_global_device_ids=true, to_apply=%region_15.16 | all-reduce | flops 409600 | bytes 2457600 | tf_op jit(solution)/shard_map/psum | solution.py:104
  (135 shorter events, 145.4 us)
Async XLA Ops:
  0.0 0.8 copy-start
  0.8 26.5 %copy-start.7 = (s32[2048]{0:T(1024)S(1)}, s32[2048]{0:T(1024)}, u32[]{:S(2)}) copy-start(s32[2048]{0:T(1024)} %param.11) | copy-start | bytes 24580
  0.9 27.2 %copy-start.13 = (s32[2]{0:T(128)S(1)}, s32[2]{0:T(128)}, u32[]{:S(2)}) copy-start(s32[2]{0:T(128)} %constant.139) | copy-start | bytes 28
  0.9 27.4 %copy-start.12 = (s32[2]{0:T(128)S(1)}, s32[2]{0:T(128)}, u32[]{:S(2)}) copy-start(s32[2]{0:T(128)} %constant.142) | copy-start | bytes 28
  43.1 15.6 %copy-start.4 = (bf16[2048,200]{0,1:T(8,128)(2,1)S(1)}, bf16[2048,200]{0,1:T(8,128)(2,1)}, u32[]{:S(2)}) copy-start(bf16[2048,200]{0,1:T(8,128)(2,1)} %param.8) | copy-start | bytes 2457604
  57.8 0.6 copy-start.8
  58.4 34.6 %copy-start.5 = (s32[32,8]{0,1:T(8,128)}, s32[32,8]{0,1:T(8,128)S(1)}, u32[]{:S(2)}) copy-start(s32[32,8]{0,1:T(8,128)S(1)} %broadcast_add_fusion.2) | copy-start | bytes 3076
  58.7 73.5 %copy-start.10 = (s32[64]{0:T(128)}, s32[64]{0:T(128)S(1)}, u32[]{:S(2)}) copy-start(s32[64]{0:T(128)S(1)} %eq.127) | copy-start | bytes 772
  103.4 8.9 copy-start.3
  103.4 127.4 %all-to-all-start.1 = ((bf16[64,256,200]{1,2,0:T(8,128)(2,1)}), bf16[64,256,200]{1,2,0:T(8,128)(2,1)}, u32[]{:S(2)}, u32[]{:S(2)}) async-start(bf16[64,256,200]{1,2,0:T(8,128)(2,1)} %copy.67), calls=%async_computation.1 | async-start | bytes 13107200 | tf_op jit(solution)/shard_map/all_to_all | solution.py:44
  230.7 386.0 %all-to-all-start = ((bf16[64,256,800]{1,2,0:T(8,128)(2,1)}), bf16[64,256,800]{1,2,0:T(8,128)(2,1)}, u32[]{:S(2)}, u32[]{:S(2)}) async-start(bf16[64,256,800]{1,2,0:T(8,128)(2,1)} %copy.64), calls=%async_computation | async-start | bytes 52428800 | tf_op jit(solution)/shard_map/all_to_all | solution.py:43
  816.2 2.6 copy-start.2
  950.8 2.6 copy-start.2
  1087.4 2.6 copy-start.2
  1223.9 2.6 copy-start.2
  1316.0 56.5 %copy-start.6 = (s32[32,8]{0,1:T(8,128)S(1)}, s32[32,8]{0,1:T(8,128)}, u32[]{:S(2)}) copy-start(s32[32,8]{0,1:T(8,128)} %copy-done.5) | copy-start | bytes 3076
  1316.0 56.5 %copy-start.9 = (pred[32,8]{0,1:T(8,128)(4,1)S(1)}, pred[32,8]{0,1:T(8,128)(4,1)}, u32[]{:S(2)}) copy-start(pred[32,8]{0,1:T(8,128)(4,1)} %copy-done.8) | copy-start | bytes 772
  1316.0 140.8 %copy-start.11 = (s32[64]{0:T(128)S(1)}, s32[64]{0:T(128)}, u32[]{:S(2)}) copy-start(s32[64]{0:T(128)} %copy-done.10) | copy-start | bytes 772
  1316.0 140.8 %all-to-all-start.2 = ((bf16[64,256,200]{1,2,0:T(8,128)(2,1)}), bf16[64,256,200]{1,2,0:T(8,128)(2,1)}, u32[]{:S(2)}, u32[]{:S(2)}) async-start(bf16[64,256,200]{1,2,0:T(8,128)(2,1)} %copy.69), calls=%async_computation.2 | async-start | bytes 13107200 | tf_op jit(solution)/shard_map/all_to_all | solution.py:99
  1372.7 126.2 %copy-start.1 = (s32[256]{0:T(256)S(1)}, s32[256]{0:T(256)}, u32[]{:S(2)}) copy-start(s32[256]{0:T(256)} %param.9) | copy-start | bytes 3076
where the time goes:
time: 1520 us; the launch traced here: 1500 us
  local copies, waits for them, and re-layouts  609 us (40%)
  waiting for transfers between devices  360 us (24%)
  matrix products  295 us (19%)
  other arithmetic  97.8 us (6%)
  starting transfers between devices  73 us (5%)
  blocking collectives  37.5 us (2%)
  loops' own time  26 us (2%)
    all_to_all x1, waiting for transfers between devices, shards(): lax.all_to_all(send_b, 'basis', split_axis=0, concat_axis=0, tiled=True)  276 us
    reshape x2, local copies, waits for them, and re-layouts, shards(): send_b = send_b.reshape(-1, BLOCK, aux_dev * width)  84.9 us
    all_to_all x1, waiting for transfers between devices, shards(): lax.all_to_all(shares.astype(jnp.bfloat16), 'basis', split_axis=0, concat...  84.1 us
    dot_general x4, matrix products, tile_step(): jnp.dot(places.T, moved, preferred_element_type=jnp.float32, precision=la...  69.4 us
    reshape x4, local copies, waits for them, and re-layouts, tile_step(): right = right.reshape(group, BLOCK, aux_dev * width)  59.2 us
    reshape x4, local copies, waits for them, and re-layouts, tile_step(): left = left.reshape(group, BLOCK, aux_dev * width)  58.9 us
    all_to_all x1, starting transfers between devices, shards(): lax.all_to_all(shares.astype(jnp.bfloat16), 'basis', split_axis=0, concat...  56.5 us
    dot_general x4, matrix products, tile_step(): jnp.dot(pick_b, flat_b, preferred_element_type=jnp.float32)  53.2 us
  transfers between devices with their start and end apart: 3, of which 2 were waited for; matrix products, arithmetic and copies ran while one was open for 15% of the time, Pallas kernels for 0%

commit v1 on v0

v1 whole, which is shorter than its diff:
```python
import functools

import jax
import jax.numpy as jnp
from jax import lax
from jax.experimental import pallas as pl
from jax.experimental.pallas import tpu as pltpu
from jax.sharding import PartitionSpec as P

BLOCK = 256
PAIR_CAP = 64
LANES = 128
CHUNKS = ((0, 200),)
VMEM = 56 * 1024 * 1024


def plan(span, depth, ndev):
    full = depth // LANES
    rest = depth - full * LANES
    fold = LANES // rest
    group = -(-span // (fold * 8)) * 8
    rows = full * span + group
    per = -(-rows // ndev)
    return full, rest, fold, group, per


def count_kernel(slot_ref, pairs_ref, owner_ref, low_ref, high_ref, flag_ref):
    nblk = slot_ref.shape[1]
    npair = pairs_ref.shape[1]
    ids = lax.broadcasted_iota(jnp.int32, (nblk, npair), 0)
    owner = owner_ref[...]
    held = jnp.sum((owner == owner_ref[0:1, 0:1]).astype(jnp.float32), axis=1, keepdims=True)
    entry = lax.broadcasted_iota(jnp.int32, (1, npair), 1)
    weight = jnp.where(entry == 0, PAIR_CAP + 1.0 - held, 1.0)
    weight = jnp.where(owner >= 0, weight, 0.0)
    one_a = jnp.where(ids == pairs_ref[0:1, :], weight, 0.0).astype(jnp.bfloat16)
    one_b = (ids == pairs_ref[1:2, :]).astype(jnp.float32).astype(jnp.bfloat16)
    rows = lax.broadcasted_iota(jnp.int32, (nblk, nblk), 0)
    place = (rows == slot_ref[...]).astype(jnp.float32).astype(jnp.bfloat16)
    at = jnp.dot(place, one_a, preferred_element_type=jnp.float32).astype(jnp.bfloat16)
    bt = jnp.dot(place, one_b, preferred_element_type=jnp.float32).astype(jnp.bfloat16)
    dims = (((1,), (1,)), ((), ()))
    count = lax.dot_general(at, bt, dims, preferred_element_type=jnp.float32)
    count += lax.dot_general(bt, at, dims, preferred_element_type=jnp.float32)
    high = jnp.floor(count * (1.0 / 256.0)) * 256.0
    low_ref[...] = (count - high).astype(jnp.bfloat16)
    high_ref[...] = high.astype(jnp.bfloat16)
    flag_ref[0] = (jnp.max(high) > 0).astype(jnp.int32)


def pair_counts(block_slot, pair_list, pair_owner):
    nblk = block_slot.shape[0]
    square = jax.ShapeDtypeStruct((nblk, nblk), jnp.bfloat16)
    vmem = pl.BlockSpec(memory_space=pltpu.VMEM)
    return pl.pallas_call(
        count_kernel,
        out_shape=(square, square, jax.ShapeDtypeStruct((1,), jnp.int32)),
        in_specs=[vmem] * 3,
        out_specs=(vmem, vmem, pl.BlockSpec(memory_space=pltpu.SMEM)),
        compiler_params=pltpu.CompilerParams(vmem_limit_bytes=VMEM),
        name="pair_counts",
    )(block_slot[None, :], pair_list.T, pair_owner[None, :])


def pack_kernel(spans, plans, ndev, x_ref, f_ref, *refs):
    outs, scratch = refs[: len(spans)], refs[len(spans):]
    b = pl.program_id(0)
    dims = (((1,), (1,)), ((), ()))
    for (lo, hi), (full, rest, fold, group, per), stage in zip(spans, plans, scratch):
        span = hi - lo
        x = x_ref[lo:hi, :]
        for t in range(0, full, 2):
            g = lax.dot_general(
                x, f_ref[t * LANES : (t + 2) * LANES, :], dims, preferred_element_type=jnp.float32
            )
            for half in range(2):
                stage[pl.ds((t + half) * span * 8 + b, span, stride=8), :] = g[
                    :, half * LANES : (half + 1) * LANES
                ]
        g = lax.dot_general(
            x, f_ref[full * LANES :, :], dims, preferred_element_type=jnp.float32
        )
        short = fold * group - span
        if short:
            g = jnp.concatenate([g, jnp.zeros((short, rest), jnp.float32)], axis=0)
        g = jnp.concatenate([g[q * group : (q + 1) * group] for q in range(fold)], axis=1)
        stage[pl.ds(full * span * 8 + b, group, stride=8), :] = g

    @pl.when(b == pl.num_programs(0) - 1)
    def _():
        for (lo, hi), (full, rest, fold, group, per), stage, out in zip(spans, plans, scratch, outs):
            rows = full * (hi - lo) + group
            out[0:rows] = stage[...].reshape(rows, 8, LANES).astype(jnp.bfloat16)


def pack(xt, ft, spans, plans, ndev):
    depth, width = ft.shape
    blocks = width // BLOCK
    outs = [jax.ShapeDtypeStruct((ndev * p[4], blocks, LANES), jnp.bfloat16) for p in plans]
    return pl.pallas_call(
        functools.partial(pack_kernel, spans, plans, ndev),
        out_shape=outs,
        grid=(blocks,),
        in_specs=[
            pl.BlockSpec((xt.shape[0], BLOCK), lambda b: (0, b)),
            pl.BlockSpec((depth, BLOCK), lambda b: (0, b)),
        ],
        out_specs=[pl.BlockSpec(o.shape, lambda b: (0, 0, 0)) for o in outs],
        scratch_shapes=[
            pltpu.VMEM(((p[0] * (s[1] - s[0]) + p[3]) * 8, LANES), jnp.float32)
            for s, p in zip(spans, plans)
        ],
        compiler_params=pltpu.CompilerParams(vmem_limit_bytes=VMEM),
        name="pack",
    )(xt, ft)


def mix_kernel(flag_ref, low_ref, high_ref, g_ref, h_ref):
    ndev, per, blocks, lanes = g_ref.shape
    nblk = ndev * blocks

    def tile(t, use_high):
        g = g_ref[:, t].astype(jnp.float32).reshape(nblk, lanes).astype(jnp.bfloat16)
        h = jnp.dot(low_ref[...], g, preferred_element_type=jnp.float32)
        if use_high:
            h += jnp.dot(high_ref[...], g, preferred_element_type=jnp.float32)
        h_ref[:, t] = h.reshape(ndev, blocks, lanes).astype(jnp.bfloat16)

    @pl.when(flag_ref[0] == 0)
    def _():
        for t in range(per):
            tile(t, False)

    @pl.when(flag_ref[0] != 0)
    def _():
        for t in range(per):
            tile(t, True)


def mix(counts, g):
    low, high, flag = counts
    vmem = pl.BlockSpec(memory_space=pltpu.VMEM)
    return pl.pallas_call(
        mix_kernel,
        out_shape=jax.ShapeDtypeStruct(g.shape, jnp.bfloat16),
        in_specs=[pl.BlockSpec(memory_space=pltpu.SMEM), vmem, vmem, vmem],
        out_specs=vmem,
        compiler_params=pltpu.CompilerParams(vmem_limit_bytes=VMEM),
        name="mix",
    )(flag, low, high, g)


def apply_kernel(span, parts, h_ref, f_ref, e_ref, stage):
    full, rest, fold, group, per = parts
    a = pl.program_id(0)
    rows = full * span + group

    @pl.when(a == 0)
    def _():
        stage[...] = h_ref[0:rows].astype(jnp.float32).reshape(rows * 8, LANES)

    total = jnp.zeros((span, BLOCK), jnp.float32)
    for t in range(0, full, 2):
        left = jnp.concatenate(
            [
                stage[pl.ds((t + half) * span * 8 + a, span, stride=8), :].astype(jnp.bfloat16)
                for half in range(2)
            ],
            axis=1,
        )
        total += jnp.dot(
            left, f_ref[t * LANES : (t + 2) * LANES, :], preferred_element_type=jnp.float32
        )
    left = stage[pl.ds(full * span * 8 + a, group, stride=8), :]
    left = jnp.concatenate([left[:, q * rest : (q + 1) * rest] for q in range(fold)], axis=0)
    total += jnp.dot(
        left[0:span].astype(jnp.bfloat16), f_ref[full * LANES :, :],
        preferred_element_type=jnp.float32,
    )
    e_ref[...] = total


def apply(h, ft, span, parts):
    depth, width = ft.shape
    blocks = width // BLOCK
    rows = parts[0] * span + parts[3]
    return pl.pallas_call(
        functools.partial(apply_kernel, span, parts),
        out_shape=jax.ShapeDtypeStruct((span, width), jnp.float32),
        grid=(blocks,),
        in_specs=[
            pl.BlockSpec(h.shape, lambda a: (0, 0, 0)),
            pl.BlockSpec((depth, BLOCK), lambda a: (0, a)),
        ],
        out_specs=pl.BlockSpec((span, BLOCK), lambda a: (0, a)),
        scratch_shapes=[pltpu.VMEM((rows * 8, LANES), jnp.float32)],
        compiler_params=pltpu.CompilerParams(vmem_limit_bytes=VMEM),
        name="apply",
    )(h, ft)


def exchange(g):
    return lax.all_to_all(g, "basis", split_axis=0, concat_axis=0, tiled=True)


def shards(factors, orbitals, block_slot, pair_list, pair_owner):
    ndev = lax.axis_size("basis")
    rows, aux, width = factors.shape
    ft = factors.transpose(1, 2, 0).reshape(aux * width, rows)
    xt = orbitals.T
    plans = [plan(hi - lo, aux * width, ndev) for lo, hi in CHUNKS]
    counts = pair_counts(block_slot, pair_list, pair_owner)
    sent = pack(xt, ft, CHUNKS, plans, ndev)
    got = [exchange(g) for g in sent]
    mixed = [mix(counts, g.reshape(ndev, p[4], *g.shape[1:])) for g, p in zip(got, plans)]
    back = [exchange(h.reshape(-1, *h.shape[2:])) for h in mixed]
    parts = [apply(h, ft, hi - lo, p) for h, (lo, hi), p in zip(back, CHUNKS, plans)]
    done = [lax.psum(e, "aux").astype(jnp.bfloat16) for e in parts]
    return jnp.concatenate(done, axis=0).T


def solution(mesh):
    return jax.shard_map(
        shards,
        mesh=mesh,
        in_specs=(P("basis", "aux", None), P("basis", None), P(), P(), P()),
        out_specs=P("basis", None),
        check_vma=False,
    )
```

time: 1520 us -> 144 us (0.09); the launches traced: 1500 us -> 143 us
  local copies, waits for them, and re-layouts: 609 us -> 1.52 us
  waiting for transfers between devices: 360 us -> 31.1 us
  matrix products: 295 us -> 0 us
  other arithmetic: 97.8 us -> 0 us
  starting transfers between devices: 73 us -> 8.25 us
  blocking collectives: 37.5 us -> 76.9 us
  loops' own time: 26 us -> 0 us
  Pallas kernels: 0 us -> 25.6 us
    reshape x30 -> x0, local copies, waits for them, and re-layouts: 416 us -> none  [the longest x2 84.9 us: shards(): send_b = send_b.reshape(-1, BLOCK, aux_dev * width)]
    all_to_all x3 -> x1, waiting for transfers between devices: 360 us -> 31.1 us  [exchange(): return lax.all_to_all(g, 'basis', split_axis=0, concat_axis=0, tiled=True)]
    dot_general x35 -> x0, matrix products: 295 us -> none  [the longest x4 69.4 us: tile_step(): jnp.dot(places.T, moved, preferred_element_type=jnp.float32, precision=la...]
    all_to_all x3 -> x1, starting transfers between devices: 73 us -> 8.25 us  [exchange(): return lax.all_to_all(g, 'basis', split_axis=0, concat_axis=0, tiled=True)]
    gather x7 -> x0, local copies, waits for them, and re-layouts: 55.3 us -> none  [the longest x1 13.4 us: shards(): index_a = jnp.clip(source_a * SEND_CAP + place[slot_a], 0, top_row)]
    all_to_all x2 -> x0, local copies, waits for them, and re-layouts: 46.2 us -> none  [the longest x1 36 us: shards(): lax.all_to_all(send_b, 'basis', split_axis=0, concat_axis=0, tiled=True)]
    all_to_all x0 -> x1, blocking collectives: none -> 38.4 us  [exchange(): return lax.all_to_all(g, 'basis', split_axis=0, concat_axis=0, tiled=True)]
    convert_element_type x2 -> x0, local copies, waits for them, and re-layouts: 37.7 us -> none  [shards(): shares.astype(jnp.bfloat16)]
  transfers between devices with their start and end apart: 3 -> 1, of which waited for: 2 -> 1; matrix products, arithmetic and copies ran while one was open for 15% -> 0% of each run, Pallas kernels for 0% -> 2%
where the time goes in v1:
time: 144 us; the launch traced here: 143 us
  blocking collectives  76.9 us (53%)
  waiting for transfers between devices  31.1 us (22%)
  Pallas kernels  25.6 us (18%)
  starting transfers between devices  8.25 us (6%)
  local copies, waits for them, and re-layouts  1.52 us (1%)
    psum x1, blocking collectives, shards(): done = [lax.psum(e, 'aux').astype(jnp.bfloat16) for e in parts]  38.5 us
    all_to_all x1, blocking collectives, exchange(): return lax.all_to_all(g, 'basis', split_axis=0, concat_axis=0, tiled=True)  38.4 us
    all_to_all x1, waiting for transfers between devices, exchange(): return lax.all_to_all(g, 'basis', split_axis=0, concat_axis=0, tiled=True)  31.1 us
    pallas_call x1, Pallas kernels, apply(): pl.pallas_call(functools.partial(apply_kernel, span, parts), out_shape=ja...  8.3 us
    pallas_call x1, Pallas kernels, pack(): pl.pallas_call(functools.partial(pack_kernel, spans, plans, ndev), out_sh...  8.25 us
    all_to_all x1, starting transfers between devices, exchange(): return lax.all_to_all(g, 'basis', split_axis=0, concat_axis=0, tiled=True)  8.25 us
    pallas_call x1, Pallas kernels, mix(): pl.pallas_call(mix_kernel, out_shape=jax.ShapeDtypeStruct(g.shape, jnp.bf...  5.5 us
    pallas_call x1, Pallas kernels, pair_counts(): pl.pallas_call(count_kernel, out_shape=(square, square, jax.ShapeDtypeStr...  3.52 us
  transfers between devices with their start and end apart: 1, of which 1 were waited for; matrix products, arithmetic and copies ran while one was open for 0% of the time, Pallas kernels for 2%

profile of v1, /device:TPU:0, one launch (start us, length us, event | category | flops | bytes accessed | tf_op | source)
XLA Modules:
  0.0 143.3 jit_solution(15501923956106520728)
XLA Ops:
  0.0 8.3 %pack.1 = bf16[1280,8,128]{2,1,0:T(8,128)(2,1)} custom-call(bf16[200,2048]{1,0:T(8,128)(2,1)} %bitcast.16, bf16[800,2048]{1,0:T(8,128)(2,1)} %bitcast.12), custom_call_target="tpu_custom_call" | custom-call | tf_op jit(solution)/shard_map/pack/pallas_call | solution.py:100
  8.3 8.2 %all-to-all-start = ((bf16[1280,8,128]{2,1,0:T(8,128)(2,1)}), bf16[1280,8,128]{2,1,0:T(8,128)(2,1)S(1)}, u32[]{:S(2)}, u32[]{:S(2)}) async-start(bf16[1280,8,128]{2,1,0:T(8,128)(2,1)} %pack.1), calls=%async_computation | async-start | bytes 5242880 | tf_op jit(solution)/shard_map/all_to_all | solution.py:203
  16.5 3.5 %pair_counts.1 = (bf16[256,256]{1,0:T(8,128)(2,1)}, bf16[256,256]{1,0:T(8,128)(2,1)}, s32[1]{0:T(128)}) custom-call(s32[1,256]{1,0:T(1,128)} %bitcast.19, s32[2,2048]{1,0:T(2,128)} %bitcast.17, s32[1,2048]{1,0:T(1,128)} %bitcast.18), custom_call_target="tpu_custom_call" | custom-call | tf_op jit(solution)/shard_map/pair_counts/pallas_call | solution.py:55
  20.0 31.1 %all-to-all-done = bf16[1280,8,128]{2,1,0:T(8,128)(2,1)S(1)} async-done(((bf16[1280,8,128]{2,1,0:T(8,128)(2,1)}), bf16[1280,8,128]{2,1,0:T(8,128)(2,1)S(1)}, u32[]{:S(2)}, u32[]{:S(2)}) %all-to-all-start) | async-done | bytes 2621472 | tf_op jit(solution)/shard_map/all_to_all | solution.py:203
  51.1 0.0 copy-start
  51.1 1.5 %copy-done = bf16[1280,8,128]{2,1,0:T(8,128)(2,1)} copy-done((bf16[1280,8,128]{2,1,0:T(8,128)(2,1)}, bf16[1280,8,128]{2,1,0:T(8,128)(2,1)S(1)}, u32[]{:S(2)}) %copy-start) | copy-done | bytes 2621464
  52.7 5.5 %mix.1 = bf16[32,40,8,128]{3,2,1,0:T(8,128)(2,1)} custom-call(s32[1]{0:T(128)} %get-tuple-element.8.flag_ref, bf16[256,256]{1,0:T(8,128)(2,1)} %get-tuple-element.9.low_ref, bf16[256,256]{1,0:T(8,128)(2,1)} %get-tuple-element.10.high_ref, bf16[32,40,8,128]{3,2,1,0:T(8,128)(2,1)} %bitcast.14), custom_call_target="tpu_custom_call" | custom-call | tf_op jit(solution)/shard_map/mix/pallas_call | solution.py:143
  58.2 38.4 %all_to_all.10.h_ref = bf16[1280,8,128]{2,1,0:T(8,128)(2,1)} all-to-all(bf16[1280,8,128]{2,1,0:T(8,128)(2,1)} %bitcast.15), channel_id=1, replica_groups=mesh['basis'=32,'aux'=4] {'basis'}, dimensions={0} | all-to-all | bytes 5242880 | tf_op jit(solution)/shard_map/all_to_all | solution.py:203
  96.6 8.3 %apply.1 = f32[200,2048]{1,0:T(8,128)} custom-call(bf16[1280,8,128]{2,1,0:T(8,128)(2,1)} %all_to_all.10.h_ref, bf16[800,2048]{1,0:T(8,128)(2,1)} %bitcast.13), custom_call_target="tpu_custom_call" | custom-call | tf_op jit(solution)/shard_map/apply/pallas_call | solution.py:187
  104.9 38.5 %all-reduce.1 = bf16[200,2048]{1,0:T(8,128)(2,1)} all-reduce(f32[200,2048]{1,0:T(8,128)} %apply.1), channel_id=1, replica_groups=mesh['basis'=32,'aux'=4] {'aux'}, use_global_device_ids=true, to_apply=%region_0.0 | all-reduce | flops 409600 | bytes 2457600 | tf_op jit(solution)/shard_map/psum | solution.py:218
Async XLA Ops:
  8.3 42.9 %all-to-all-start = ((bf16[1280,8,128]{2,1,0:T(8,128)(2,1)}), bf16[1280,8,128]{2,1,0:T(8,128)(2,1)S(1)}, u32[]{:S(2)}, u32[]{:S(2)}) async-start(bf16[1280,8,128]{2,1,0:T(8,128)(2,1)} %pack.1), calls=%async_computation | async-start | bytes 5242880 | tf_op jit(solution)/shard_map/all_to_all | solution.py:203
  51.1 1.5 %copy-start = (bf16[1280,8,128]{2,1,0:T(8,128)(2,1)}, bf16[1280,8,128]{2,1,0:T(8,128)(2,1)S(1)}, u32[]{:S(2)}) copy-start(bf16[1280,8,128]{2,1,0:T(8,128)(2,1)S(1)} %all-to-all-done) | copy-start | bytes 7864324

commit v2 on v1

v2 whole, which is shorter than its diff:
```python
import functools

import jax
import jax.numpy as jnp
from jax import lax
from jax.experimental import pallas as pl
from jax.experimental.pallas import tpu as pltpu
from jax.sharding import PartitionSpec as P

BLOCK = 256
PAIR_CAP = 64
LANES = 128
VMEM = 56 * 1024 * 1024
NT = (((1,), (1,)), ((), ()))
F32 = jnp.float32
BF16 = jnp.bfloat16


def count_kernel(keep, slot_ref, pairs_ref, owner_ref, low_ref, high_ref, flag_ref):
    nblk = slot_ref.shape[1]
    npair = pairs_ref.shape[1]
    ids = lax.broadcasted_iota(jnp.int32, (nblk, npair), 0)
    owner = owner_ref[...]
    held = jnp.sum((owner == owner_ref[0:1, 0:1]).astype(F32), axis=1, keepdims=True)
    entry = lax.broadcasted_iota(jnp.int32, (1, npair), 1)
    weight = jnp.where(entry == 0, PAIR_CAP + 1.0 - held, 1.0)
    weight = jnp.where(owner >= 0, weight, 0.0)
    one_a = jnp.where(ids == pairs_ref[0:1, :], weight, 0.0).astype(BF16)
    one_b = (ids == pairs_ref[1:2, :]).astype(F32).astype(BF16)
    rows = lax.broadcasted_iota(jnp.int32, (nblk, nblk), 0)
    ndev = nblk // keep
    turned = (rows % ndev) * keep + rows // ndev

    def put(ids, one):
        place = (ids == slot_ref[...]).astype(F32).astype(BF16)
        return jnp.dot(place, one, preferred_element_type=F32).astype(BF16)

    count = lax.dot_general(put(turned, one_a), put(rows, one_b), NT, preferred_element_type=F32)
    count += lax.dot_general(put(turned, one_b), put(rows, one_a), NT, preferred_element_type=F32)
    high = jnp.floor(count * (1.0 / 256.0)) * 256.0
    low_ref[...] = (count - high).astype(BF16)
    high_ref[...] = high.astype(BF16)
    flag_ref[0] = (jnp.max(high) > 0).astype(jnp.int32)


def pair_counts(block_slot, pair_list, pair_owner, keep):
    nblk = block_slot.shape[0]
    square = jax.ShapeDtypeStruct((nblk, nblk), BF16)
    vmem = pl.BlockSpec(memory_space=pltpu.VMEM)
    return pl.pallas_call(
        functools.partial(count_kernel, keep),
        out_shape=(square, square, jax.ShapeDtypeStruct((1,), jnp.int32)),
        in_specs=[vmem] * 3,
        out_specs=(vmem, vmem, pl.BlockSpec(memory_space=pltpu.SMEM)),
        compiler_params=pltpu.CompilerParams(vmem_limit_bytes=VMEM),
        name="pair_counts",
    )(block_slot[None, :], pair_list.T, pair_owner[None, :])


def pack_kernel(per, x_hbm, f_hbm, out_hbm, x_ref, f_ref, out_ref, sems, out_sems):
    span, depth = x_ref.shape[0], f_ref.shape[0]
    full = depth // LANES
    rest = depth - full * LANES
    fold = LANES // rest
    group = -(-span // (fold * 8)) * 8
    step = span // per
    tail = out_ref.shape[0] - full * step
    pairs = f_ref.shape[1] // (2 * BLOCK)

    def fetch(p):
        cols = slice(p * 2 * BLOCK, (p + 1) * 2 * BLOCK)
        return [
            pltpu.make_async_copy(src.at[:, cols], dst.at[:, cols], sems.at[k, p])
            for k, (src, dst) in enumerate(((x_hbm, x_ref), (f_hbm, f_ref)))
        ]

    def send(p):
        rows = slice(p * 2 * per, (p + 1) * 2 * per)
        return pltpu.make_async_copy(out_ref.at[:, rows], out_hbm.at[:, rows], out_sems.at[p])

    for p in range(pairs):
        for copy in fetch(p):
            copy.start()
    for p in range(pairs):
        for copy in fetch(p):
            copy.wait()

        def product(k, lo, hi):
            cols = slice((2 * p + k) * BLOCK, (2 * p + k + 1) * BLOCK)
            return lax.dot_general(
                x_ref[:, cols], f_ref[lo:hi, cols], NT, preferred_element_type=F32
            )

        place = slice(p * 2 * per, (p + 1) * 2 * per)
        for t in range(0, full, 2):
            gs = [product(k, t * LANES, (t + 2) * LANES) for k in range(2)]
            for half in range(2):
                lanes = slice(half * LANES, (half + 1) * LANES)
                rows = [g[:, lanes].reshape(step, per, LANES) for g in gs]
                first = (t + half) * step
                out_ref[first : first + step, place] = jnp.concatenate(rows, axis=1).astype(BF16)
        rows = []
        for k in range(2):
            g = product(k, full * LANES, depth)
            g = jnp.concatenate([g, jnp.zeros((fold * group - span, rest), F32)], axis=0)
            g = jnp.concatenate([g[q * group : (q + 1) * group] for q in range(fold)], axis=1)
            g = jnp.concatenate([g, jnp.zeros((tail * per - group, LANES), F32)], axis=0)
            rows.append(g.reshape(tail, per, LANES))
        out_ref[full * step :, place] = jnp.concatenate(rows, axis=1).astype(BF16)
        send(p).start()
    for p in range(pairs):
        send(p).wait()


def pack(xt, ft, ndev, per):
    depth, width = ft.shape
    blocks = width // BLOCK
    return pl.pallas_call(
        functools.partial(pack_kernel, per),
        out_shape=jax.ShapeDtypeStruct((ndev, blocks * per, LANES), BF16),
        in_specs=[pl.BlockSpec(memory_space=pltpu.HBM)] * 2,
        out_specs=pl.BlockSpec(memory_space=pltpu.HBM),
        scratch_shapes=[
            pltpu.VMEM(xt.shape, BF16),
            pltpu.VMEM(ft.shape, BF16),
            pltpu.VMEM((ndev, blocks * per, LANES), BF16),
            pltpu.SemaphoreType.DMA((2, blocks // 2)),
            pltpu.SemaphoreType.DMA((blocks // 2,)),
        ],
        compiler_params=pltpu.CompilerParams(vmem_limit_bytes=VMEM),
        name="pack",
    )(xt, ft)


def mix_kernel(
    per, flag_ref, low_hbm, high_hbm, g_ref, h_hbm, low_ref, high_ref, stage, turned, h_ref, sems, out_sems
):
    ndev, height, lanes = g_ref.shape
    blocks = height // per
    nblk = low_ref.shape[0]
    pitch = per + 1
    far = blocks * per + 1
    matrices = [
        pltpu.make_async_copy(low_hbm, low_ref, sems.at[0]),
        pltpu.make_async_copy(high_hbm, high_ref, sems.at[1]),
    ]
    for copy in matrices:
        copy.start()
    for c in range(ndev):
        v = g_ref[c].astype(F32)
        for b in range(blocks):
            stage[pl.ds((c * blocks + b) * pitch, per), :] = v[b * per : (b + 1) * per]
    for copy in matrices:
        copy.wait()

    def tiles(use_high):
        for t in range(0, per, 2):
            g = [stage[pl.ds(t + k, nblk, stride=pitch), :].astype(BF16) for k in range(2)]
            g = jnp.concatenate(g, axis=1)
            h = jnp.dot(low_ref[...], g, preferred_element_type=F32)
            if use_high:
                h += jnp.dot(high_ref[...], g, preferred_element_type=F32)
            for k in range(2):
                for a in range(blocks):
                    turned[pl.ds(a * per + t + k, ndev, stride=far), :] = h[
                        a * ndev : (a + 1) * ndev, k * lanes : (k + 1) * lanes
                    ]

    pl.when(flag_ref[0] == 0)(lambda: tiles(False))
    pl.when(flag_ref[0] != 0)(lambda: tiles(True))
    sends = out_sems.shape[0]
    group = ndev // sends

    def send(p):
        cut = slice(p * group, (p + 1) * group)
        return pltpu.make_async_copy(h_ref.at[cut], h_hbm.at[cut], out_sems.at[p])

    for p in range(sends):
        for i in range(p * group, (p + 1) * group):
            h_ref[i] = turned[i * far : i * far + height, :].astype(BF16)
        send(p).start()
    for p in range(sends):
        send(p).wait()


def mix(counts, g, per):
    low, high, flag = counts
    ndev, height, lanes = g.shape
    blocks = height // per
    vmem = pl.BlockSpec(memory_space=pltpu.VMEM)
    hbm = pl.BlockSpec(memory_space=pltpu.HBM)
    return pl.pallas_call(
        functools.partial(mix_kernel, per),
        out_shape=jax.ShapeDtypeStruct(g.shape, BF16),
        in_specs=[
            pl.BlockSpec(memory_space=pltpu.SMEM),
            hbm,
            hbm,
            vmem,
        ],
        out_specs=hbm,
        scratch_shapes=[
            pltpu.VMEM(low.shape, BF16),
            pltpu.VMEM(low.shape, BF16),
            pltpu.VMEM((ndev * blocks * (per + 1), lanes), F32),
            pltpu.VMEM((ndev * (height + 1), lanes), F32),
            pltpu.VMEM(g.shape, BF16),
            pltpu.SemaphoreType.DMA((2,)),
            pltpu.SemaphoreType.DMA((8,)),
        ],
        compiler_params=pltpu.CompilerParams(vmem_limit_bytes=VMEM),
        name="mix",
    )(flag, low, high, g)


def apply_kernel(per, me_ref, h_ref, f_hbm, *refs):
    outs, f_ref, sems = refs[:-2], *refs[-2:]
    ndev, height, lanes = h_ref.shape
    span = outs[0].shape[0]
    depth = f_hbm.shape[0]
    aux, _, width = f_ref.shape
    keep = width // BLOCK
    full = depth // LANES
    rest = depth - full * LANES
    fold = LANES // rest
    group = -(-span // (fold * 8)) * 8
    step = span // per

    def fetch(d):
        start = pl.multiple_of(lax.rem(me_ref[0] + d, aux) * width, width)
        return pltpu.make_async_copy(f_hbm.at[:, pl.ds(start, width)], f_ref.at[d], sems.at[d])

    order = list(range(1, aux)) + [0]
    for d in order:
        fetch(d).start()
    for d in order:
        fetch(d).wait()
        chunk = keep * per
        first = pl.multiple_of(lax.rem(me_ref[0] + d, aux) * chunk, chunk)

        def take(lo, hi):
            return h_ref[lo:hi, pl.ds(first, chunk)].astype(F32)

        tiles = [take(t * step, (t + 1) * step) for t in range(full)]
        tail = take(full * step, ndev)
        for a in range(keep):
            rows = slice(a * per, (a + 1) * per)
            left = [v[:, rows].reshape(span, lanes).astype(BF16) for v in tiles]
            last = tail[:, rows].reshape(-1, lanes)[:group]
            last = [last[:, q * rest : (q + 1) * rest] for q in range(fold)]
            last = jnp.concatenate(last, axis=0)[:span].astype(BF16)
            left = jnp.concatenate(left + [last], axis=1)
            cols = slice(a * BLOCK, (a + 1) * BLOCK)
            total = jnp.dot(left, f_ref[d, :, cols], preferred_element_type=F32)
            out = outs[a * aux + d]
            out[...] = total.astype(out.dtype)


def apply(me, h, ft, span, per, aux):
    depth, rows = ft.shape
    width = rows // aux
    vmem = pl.BlockSpec(memory_space=pltpu.VMEM)
    return pl.pallas_call(
        functools.partial(apply_kernel, per),
        out_shape=[
            pltpu.VMEM((span, BLOCK), BF16 if d else F32)
            for a in range(width // BLOCK)
            for d in range(aux)
        ],
        in_specs=[
            pl.BlockSpec(memory_space=pltpu.SMEM),
            vmem,
            pl.BlockSpec(memory_space=pltpu.HBM),
        ],
        out_specs=[vmem] * (rows // BLOCK),
        scratch_shapes=[
            pltpu.VMEM((aux, depth, width), BF16),
            pltpu.SemaphoreType.DMA((aux,)),
        ],
        compiler_params=pltpu.CompilerParams(vmem_limit_bytes=VMEM),
        name="apply",
    )(me, h, ft)


def place_kernel(aux, me_ref, *refs):
    pieces, out_ref = refs[:-1], refs[-1]
    keep = len(pieces) // aux
    for d in range(aux):
        h = lax.rem(me_ref[0] + aux - d, aux)
        for a in range(keep):
            start = pl.multiple_of((h * keep + a) * BLOCK, BLOCK)
            out_ref[:, pl.ds(start, BLOCK)] = pieces[a * aux + d][...]


def place(me, pieces, aux):
    span, width = pieces[0].shape
    vmem = pl.BlockSpec(memory_space=pltpu.VMEM)
    return pl.pallas_call(
        functools.partial(place_kernel, aux),
        out_shape=jax.ShapeDtypeStruct((span, width * len(pieces)), BF16),
        in_specs=[pl.BlockSpec(memory_space=pltpu.SMEM)] + [vmem] * len(pieces),
        out_specs=vmem,
        compiler_params=pltpu.CompilerParams(vmem_limit_bytes=VMEM),
        name="place",
    )(me, *pieces)


def exchange(v):
    v = lax.all_to_all(v, "basis", split_axis=0, concat_axis=0, tiled=True)
    return pltpu.with_memory_space_constraint(v, pltpu.VMEM)


def shards(factors, orbitals, block_slot, pair_list, pair_owner):
    ndev, aux = lax.axis_size("basis"), lax.axis_size("aux")
    me = lax.axis_index("aux").astype(jnp.int32)
    rows, aux_dev, width = factors.shape
    ft = factors.transpose(1, 2, 0).reshape(aux_dev * width, rows)
    xt = orbitals.T
    blocks = rows // BLOCK
    per = -(-(aux_dev * width * width) // (LANES * ndev * 8)) * 8
    got = exchange(pack(xt, ft, ndev, per))
    counts = pair_counts(block_slot, pair_list, pair_owner, blocks)
    back = exchange(mix(counts, got, per))
    parts = apply(me[None], back, ft, width, per, aux)

    def turn(v, d, last):
        v = lax.ppermute(v, "aux", [(k, (k + d) % aux) for k in range(aux)])
        return pltpu.with_memory_space_constraint(v, pltpu.VMEM) if last else v

    pieces = []
    for a in range(blocks // aux):
        total = parts[a * aux]
        for d in range(1, aux):
            total += turn(parts[a * aux + d], d, False).astype(F32)
        total = total.astype(BF16)
        pieces += [turn(total, d, True) if d else total for d in range(aux)]
    return place(me[None], pieces, aux).T


def solution(mesh):
    return jax.shard_map(
        shards,
        mesh=mesh,
        in_specs=(P("basis", "aux", None), P("basis", None), P(), P(), P()),
        out_specs=P("basis", None),
        check_vma=False,
    )
```

time: 144 us -> 120 us (0.83)
  blocking collectives: 76.9 us -> 0 us
  waiting for transfers between devices: 31.1 us -> 70.9 us
  starting transfers between devices: 8.25 us -> 30.6 us
  Pallas kernels: 25.6 us -> 17.6 us
  local copies, waits for them, and re-layouts: 1.52 us -> 0.01 us
    psum x1 -> x0, blocking collectives: 38.5 us -> none  [shards(): done = [lax.psum(e, 'aux').astype(jnp.bfloat16) for e in parts]]
    all_to_all x1 -> x0, blocking collectives: 38.4 us -> none  [exchange(): return lax.all_to_all(g, 'basis', split_axis=0, concat_axis=0, tiled=True)]
    all_to_all x1 -> x2, waiting for transfers between devices: 31.1 us -> 64.8 us  [exchange(): v = lax.all_to_all(v, 'basis', split_axis=0, concat_axis=0, tiled=True)]
    ppermute x0 -> x12, starting transfers between devices: none -> 18.2 us  [turn(): v = lax.ppermute(v, 'aux', [(k, (k + d) % aux) for k in range(aux)])]
    pallas_call x4 -> x5, Pallas kernels: 25.6 us -> 17.6 us  [the longest x1 4.46 us: pack(): pl.pallas_call(functools.partial(pack_kernel, per), out_shape=jax.ShapeDt...]
    ppermute x0 -> x12, waiting for transfers between devices: none -> 6.05 us  [turn(): v = lax.ppermute(v, 'aux', [(k, (k + d) % aux) for k in range(aux)])]
    all_to_all x1 -> x2, starting transfers between devices: 8.25 us -> 12.3 us  [exchange(): v = lax.all_to_all(v, 'basis', split_axis=0, concat_axis=0, tiled=True)]
    unnamed x2 -> x4, local copies, waits for them, and re-layouts: 1.52 us -> 0.01 us
  transfers between devices with their start and end apart: 1 -> 14, of which waited for: 1 -> 9; matrix products, arithmetic and copies ran while one was open for 0% -> 0% of each run, Pallas kernels for 2% -> 4%
where the time goes in v2:
time: 120 us; the launch traced here: 119 us
  waiting for transfers between devices  70.9 us (59%)
  starting transfers between devices  30.6 us (26%)
  Pallas kernels  17.6 us (15%)
    all_to_all x2, waiting for transfers between devices, exchange(): v = lax.all_to_all(v, 'basis', split_axis=0, concat_axis=0, tiled=True)  64.8 us
    ppermute x12, starting transfers between devices, turn(): v = lax.ppermute(v, 'aux', [(k, (k + d) % aux) for k in range(aux)])  18.2 us
    all_to_all x2, starting transfers between devices, exchange(): v = lax.all_to_all(v, 'basis', split_axis=0, concat_axis=0, tiled=True)  12.3 us
    ppermute x12, waiting for transfers between devices, turn(): v = lax.ppermute(v, 'aux', [(k, (k + d) % aux) for k in range(aux)])  6.05 us
    pallas_call x1, Pallas kernels, pack(): pl.pallas_call(functools.partial(pack_kernel, per), out_shape=jax.ShapeDt...  4.46 us
    pallas_call x1, Pallas kernels, pair_counts(): pl.pallas_call(functools.partial(count_kernel, keep), out_shape=(square,...  4.41 us
    pallas_call x1, Pallas kernels, mix(): pl.pallas_call(functools.partial(mix_kernel, per), out_shape=jax.ShapeDty...  4.01 us
    pallas_call x1, Pallas kernels, apply(): pl.pallas_call(functools.partial(apply_kernel, per), out_shape=[pltpu.VME...  2.77 us
  transfers between devices with their start and end apart: 14, of which 9 were waited for; matrix products, arithmetic and copies ran while one was open for 0% of the time, Pallas kernels for 4%

profile of v2, /device:TPU:0, one launch (start us, length us, event | category | flops | bytes accessed | tf_op | source)
XLA Modules:
  0.0 119.3 jit_solution(7407443650525799396)
XLA Ops:
  0.0 4.5 %pack.1 = bf16[32,320,128]{2,1,0:T(8,128)(2,1)} custom-call(bf16[200,2048]{1,0:T(8,128)(2,1)} %bitcast.11, bf16[800,2048]{1,0:T(8,128)(2,1)} %bitcast.9), custom_call_target="tpu_custom_call" | custom-call | tf_op jit(solution)/shard_map/pack/pallas_call | solution.py:118
  4.5 8.3 %all-to-all-start = ((bf16[32,320,128]{2,1,0:T(8,128)(2,1)}), bf16[32,320,128]{2,1,0:T(8,128)(2,1)S(1)}, u32[]{:S(2)}, u32[]{:S(2)}) async-start(bf16[32,320,128]{2,1,0:T(8,128)(2,1)} %pack.1), calls=%async_computation | async-start | bytes 5242880 | tf_op jit(solution)/shard_map/all_to_all | solution.py:309
  12.7 4.4 %pair_counts.1 = (bf16[256,256]{1,0:T(8,128)(2,1)}, bf16[256,256]{1,0:T(8,128)(2,1)}, s32[1]{0:T(128)}) custom-call(s32[1,256]{1,0:T(1,128)} %bitcast.14, s32[2,2048]{1,0:T(2,128)} %bitcast.12, s32[1,2048]{1,0:T(1,128)} %bitcast.13), custom_call_target="tpu_custom_call" | custom-call | tf_op jit(solution)/shard_map/pair_counts/pallas_call | solution.py:50
  17.2 30.2 %all-to-all-done.g_ref = bf16[32,320,128]{2,1,0:T(8,128)(2,1)S(1)} async-done(((bf16[32,320,128]{2,1,0:T(8,128)(2,1)}), bf16[32,320,128]{2,1,0:T(8,128)(2,1)S(1)}, u32[]{:S(2)}, u32[]{:S(2)}) %all-to-all-start) | async-done | bytes 2621472 | tf_op jit(solution)/shard_map/all_to_all | solution.py:309
  47.4 4.0 %mix.1 = bf16[32,320,128]{2,1,0:T(8,128)(2,1)} custom-call(s32[1]{0:T(128)} %get-tuple-element.16.flag_ref, bf16[256,256]{1,0:T(8,128)(2,1)} %get-tuple-element.17.low_hbm, bf16[256,256]{1,0:T(8,128)(2,1)} %get-tuple-element.18.high_hbm, bf16[32,320,128]{2,1,0:T(8,128)(2,1)S(1)} %all-to-all-done.g_ref), custom_call_target="tpu_custom_call" | custom-call | tf_op jit(solution)/shard_map/mix/pallas_call | solution.py:192
  51.4 4.1 %all-to-all-start.1 = ((bf16[32,320,128]{2,1,0:T(8,128)(2,1)}), bf16[32,320,128]{2,1,0:T(8,128)(2,1)S(1)}, u32[]{:S(2)}, u32[]{:S(2)}) async-start(bf16[32,320,128]{2,1,0:T(8,128)(2,1)} %mix.1), calls=%async_computation.1 | async-start | bytes 5242880 | tf_op jit(solution)/shard_map/all_to_all | solution.py:309
  55.5 34.6 %all-to-all-done.1.h_ref = bf16[32,320,128]{2,1,0:T(8,128)(2,1)S(1)} async-done(((bf16[32,320,128]{2,1,0:T(8,128)(2,1)}), bf16[32,320,128]{2,1,0:T(8,128)(2,1)S(1)}, u32[]{:S(2)}, u32[]{:S(2)}) %all-to-all-start.1) | async-done | bytes 2621472 | tf_op jit(solution)/shard_map/all_to_all | solution.py:309
  90.1 2.8 %apply.1 = (f32[200,256]{1,0:T(8,128)S(1)}, bf16[200,256]{1,0:T(8,128)(2,1)S(1)}, bf16[200,256]{1,0:T(8,128)(2,1)S(1)}, bf16[200,256]{1,0:T(8,128)(2,1)S(1)}, f3...) custom-call(s32[1]{0:T(128)} %bitcast.me_ref, ...), custom_call_target="tpu_custom_call" | custom-call | tf_op jit(solution)/shard_map/apply/pallas_call | solution.py:263
  92.9 1.7 %collective-permute-start.6 = (bf16[200,256]{1,0:T(8,128)(2,1)S(1)}, bf16[200,256]{1,0:T(8,128)(2,1)S(1)}, u32[]{:S(2)}, u32[]{:S(2)}) collective-permute-start(bf16[200,256]{1,0:T(8,128)(2,1)S(1)} %get-tuple-element.24), channel_id=1, source_target_pairs={{0,1},{1,2},{2,3},{3,0},{4,5},{5,6},{6,7},{7,4},{8,9},{9,10},{10,1... | collective-permute-start | bytes 307208 | tf_op jit(solution)/shard_map/ppermute | solution.py:327
  94.5 2.9 %collective-permute-start.7 = (bf16[200,256]{1,0:T(8,128)(2,1)S(1)}, bf16[200,256]{1,0:T(8,128)(2,1)S(1)}, u32[]{:S(2)}, u32[]{:S(2)}) collective-permute-start(bf16[200,256]{1,0:T(8,128)(2,1)S(1)} %get-tuple-element.25), channel_id=1, source_target_pairs={{0,2},{1,3},{2,0},{3,1},{4,6},{5,7},{6,4},{7,5},{8,10},{9,11},{10,... | collective-permute-start | bytes 307208 | tf_op jit(solution)/shard_map/ppermute | solution.py:327
  97.4 1.3 %collective-permute-start.8 = (bf16[200,256]{1,0:T(8,128)(2,1)S(1)}, bf16[200,256]{1,0:T(8,128)(2,1)S(1)}, u32[]{:S(2)}, u32[]{:S(2)}) collective-permute-start(bf16[200,256]{1,0:T(8,128)(2,1)S(1)} %get-tuple-element.26), channel_id=1, source_target_pairs={{0,3},{1,0},{2,1},{3,2},{4,7},{5,4},{6,5},{7,6},{8,11},{9,8},{10,9... | collective-permute-start | bytes 307208 | tf_op jit(solution)/shard_map/ppermute | solution.py:327
  98.8 0.7 collective-permute-start
  99.5 0.8 collective-permute-start.1
  100.2 0.0 collective-permute-done.6
  100.2 1.9 %collective-permute-start.2 = (bf16[200,256]{1,0:T(8,128)(2,1)S(1)}, bf16[200,256]{1,0:T(8,128)(2,1)S(1)}, u32[]{:S(2)}, u32[]{:S(2)}) collective-permute-start(bf16[200,256]{1,0:T(8,128)(2,1)S(1)} %get-tuple-element.22), channel_id=1, source_target_pairs={{0,3},{1,0},{2,1},{3,2},{4,7},{5,4},{6,5},{7,6},{8,11},{9,8},{10,9... | collective-permute-start | bytes 307208 | tf_op jit(solution)/shard_map/ppermute | solution.py:327
  102.1 1.3 %collective-permute-done.7 = bf16[200,256]{1,0:T(8,128)(2,1)S(1)} collective-permute-done((bf16[200,256]{1,0:T(8,128)(2,1)S(1)}, bf16[200,256]{1,0:T(8,128)(2,1)S(1)}, u32[]{:S(2)}, u32[]{:S(2)}) %collective-permute-start.7) | collective-permute-done | bytes 102432 | tf_op jit(solution)/shard_map/ppermute | solution.py:327
  103.5 0.0 collective-permute-done.8
  103.5 0.1 add_convert_fusion.refs_4_
  103.5 0.0 copy-start
  103.5 2.7 %collective-permute-start.10 = (bf16[200,256]{1,0:T(8,128)(2,1)S(1)}, bf16[200,256]{1,0:T(8,128)(2,1)S(1)}, u32[]{:S(2)}, u32[]{:S(2)}) collective-permute-start(bf16[200,256]{1,0:T(8,128)(2,1)S(1)} %add_convert_fusion.refs_4_), channel_id=1, source_target_pairs={{0,2},{1,3},{2,0},{3,1},{4,6},{5,7},{6,4},{7,5},{8,10},{9,11},{10,... | collective-permute-start | bytes 307208 | tf_op jit(solution)/shard_map/ppermute | solution.py:327
  106.3 0.8 collective-permute-start.11
  107.1 0.7 collective-permute-done
  107.8 0.5 collective-permute-start.9
  108.3 0.0 collective-permute-done.1
  108.3 0.2 collective-permute-done.2
  108.5 0.1 add_convert_fusion.1.refs_0_
  108.5 0.0 copy-start.1
  108.5 2.2 %collective-permute-start.3 = (bf16[200,256]{1,0:T(8,128)(2,1)S(1)}, bf16[200,256]{1,0:T(8,128)(2,1)S(1)}, u32[]{:S(2)}, u32[]{:S(2)}) collective-permute-start(bf16[200,256]{1,0:T(8,128)(2,1)S(1)} %add_convert_fusion.1.refs_0_), channel_id=1, source_target_pairs={{0,1},{1,2},{2,3},{3,0},{4,5},{5,6},{6,7},{7,4},{8,9},{9,10},{10,1... | collective-permute-start | bytes 307208 | tf_op jit(solution)/shard_map/ppermute | solution.py:327
  110.7 1.9 %collective-permute-start.4 = (bf16[200,256]{1,0:T(8,128)(2,1)S(1)}, bf16[200,256]{1,0:T(8,128)(2,1)S(1)}, u32[]{:S(2)}, u32[]{:S(2)}) collective-permute-start(bf16[200,256]{1,0:T(8,128)(2,1)S(1)} %add_convert_fusion.1.refs_0_), channel_id=1, source_target_pairs={{0,2},{1,3},{2,0},{3,1},{4,6},{5,7},{6,4},{7,5},{8,10},{9,11},{10,... | collective-permute-start | bytes 307208 | tf_op jit(solution)/shard_map/ppermute | solution.py:327
  112.7 0.0 collective-permute-done.10.refs_6_
  112.7 0.8 collective-permute-start.5
  113.5 0.0 collective-permute-done.11.refs_7_
  113.5 0.8 collective-permute-done.9.refs_5_
  114.3 1.1 collective-permute-done.3.refs_1_
  115.4 1.5 %collective-permute-done.4.refs_2_ = bf16[200,256]{1,0:T(8,128)(2,1)S(1)} collective-permute-done((bf16[200,256]{1,0:T(8,128)(2,1)S(1)}, bf16[200,256]{1,0:T(8,128)(2,1)S(1)}, u32[]{:S(2)}, u32[]{:S(2)}) %collective-permute-start.4) | collective-permute-done | bytes 102432 | tf_op jit(solution)/shard_map/ppermute | solution.py:327
  116.9 0.4 collective-permute-done.5.refs_3_
  117.3 0.0 copy-done
  117.3 0.0 copy-done.1
  117.3 1.9 %place.1 = bf16[200,2048]{1,0:T(8,128)(2,1)} custom-call(s32[1]{0:T(128)} %bitcast.me_ref, bf16[200,256]{1,0:T(8,128)(2,1)} %copy-done.1, bf16[200,256]{1,0:T(8,128)(2,1)S(1)} %collective-permute-done.3.refs_1_, bf16[200,256]{1,0:T(8,128)(2,1)S(1)} %collective-permute-done.4.refs_2_, bf16[200,256]{1,0:T(8,128)(2,1)S(1)} %collective-permute-done.5.refs_3_, ...), custom_call_target="tpu_custom_call" | custom-call | tf_op jit(solution)/shard_map/place/pallas_call | solution.py:298
Async XLA Ops:
  4.5 42.9 %all-to-all-start = ((bf16[32,320,128]{2,1,0:T(8,128)(2,1)}), bf16[32,320,128]{2,1,0:T(8,128)(2,1)S(1)}, u32[]{:S(2)}, u32[]{:S(2)}) async-start(bf16[32,320,128]{2,1,0:T(8,128)(2,1)} %pack.1), calls=%async_computation | async-start | bytes 5242880 | tf_op jit(solution)/shard_map/all_to_all | solution.py:309
  51.4 38.7 %all-to-all-start.1 = ((bf16[32,320,128]{2,1,0:T(8,128)(2,1)}), bf16[32,320,128]{2,1,0:T(8,128)(2,1)S(1)}, u32[]{:S(2)}, u32[]{:S(2)}) async-start(bf16[32,320,128]{2,1,0:T(8,128)(2,1)} %mix.1), calls=%async_computation.1 | async-start | bytes 5242880 | tf_op jit(solution)/shard_map/all_to_all | solution.py:309
  92.9 7.4 %collective-permute-start.6 = (bf16[200,256]{1,0:T(8,128)(2,1)S(1)}, bf16[200,256]{1,0:T(8,128)(2,1)S(1)}, u32[]{:S(2)}, u32[]{:S(2)}) collective-permute-start(bf16[200,256]{1,0:T(8,128)(2,1)S(1)} %get-tuple-element.24), channel_id=1, source_target_pairs={{0,1},{1,2},{2,3},{3,0},{4,5},{5,6},{6,7},{7,4},{8,9},{9,10},{10,1... | collective-permute-start | bytes 307208 | tf_op jit(solution)/shard_map/ppermute | solution.py:327
  94.5 8.9 %collective-permute-start.7 = (bf16[200,256]{1,0:T(8,128)(2,1)S(1)}, bf16[200,256]{1,0:T(8,128)(2,1)S(1)}, u32[]{:S(2)}, u32[]{:S(2)}) collective-permute-start(bf16[200,256]{1,0:T(8,128)(2,1)S(1)} %get-tuple-element.25), channel_id=1, source_target_pairs={{0,2},{1,3},{2,0},{3,1},{4,6},{5,7},{6,4},{7,5},{8,10},{9,11},{10,... | collective-permute-start | bytes 307208 | tf_op jit(solution)/shard_map/ppermute | solution.py:327
  97.4 6.0 %collective-permute-start.8 = (bf16[200,256]{1,0:T(8,128)(2,1)S(1)}, bf16[200,256]{1,0:T(8,128)(2,1)S(1)}, u32[]{:S(2)}, u32[]{:S(2)}) collective-permute-start(bf16[200,256]{1,0:T(8,128)(2,1)S(1)} %get-tuple-element.26), channel_id=1, source_target_pairs={{0,3},{1,0},{2,1},{3,2},{4,7},{5,4},{6,5},{7,6},{8,11},{9,8},{10,9... | collective-permute-start | bytes 307208 | tf_op jit(solution)/shard_map/ppermute | solution.py:327
  98.8 9.0 %collective-permute-start = (bf16[200,256]{1,0:T(8,128)(2,1)S(1)}, bf16[200,256]{1,0:T(8,128)(2,1)S(1)}, u32[]{:S(2)}, u32[]{:S(2)}) collective-permute-start(bf16[200,256]{1,0:T(8,128)(2,1)S(1)} %get-tuple-element.20), channel_id=1, source_target_pairs={{0,1},{1,2},{2,3},{3,0},{4,5},{5,6},{6,7},{7,4},{8,9},{9,10},{10,1... | collective-permute-start | bytes 307208 | tf_op jit(solution)/shard_map/ppermute | solution.py:327
  99.5 8.8 %collective-permute-start.1 = (bf16[200,256]{1,0:T(8,128)(2,1)S(1)}, bf16[200,256]{1,0:T(8,128)(2,1)S(1)}, u32[]{:S(2)}, u32[]{:S(2)}) collective-permute-start(bf16[200,256]{1,0:T(8,128)(2,1)S(1)} %get-tuple-element.21), channel_id=1, source_target_pairs={{0,2},{1,3},{2,0},{3,1},{4,6},{5,7},{6,4},{7,5},{8,10},{9,11},{10,... | collective-permute-start | bytes 307208 | tf_op jit(solution)/shard_map/ppermute | solution.py:327
  100.2 8.2 %collective-permute-start.2 = (bf16[200,256]{1,0:T(8,128)(2,1)S(1)}, bf16[200,256]{1,0:T(8,128)(2,1)S(1)}, u32[]{:S(2)}, u32[]{:S(2)}) collective-permute-start(bf16[200,256]{1,0:T(8,128)(2,1)S(1)} %get-tuple-element.22), channel_id=1, source_target_pairs={{0,3},{1,0},{2,1},{3,2},{4,7},{5,4},{6,5},{7,6},{8,11},{9,8},{10,9... | collective-permute-start | bytes 307208 | tf_op jit(solution)/shard_map/ppermute | solution.py:327
  103.5 13.8 %copy-start = (bf16[200,256]{1,0:T(8,128)(2,1)}, bf16[200,256]{1,0:T(8,128)(2,1)S(1)}, u32[]{:S(2)}) copy-start(bf16[200,256]{1,0:T(8,128)(2,1)S(1)} %add_convert_fusion.refs_4_) | copy-start | bytes 307204
  103.5 9.1 %collective-permute-start.10 = (bf16[200,256]{1,0:T(8,128)(2,1)S(1)}, bf16[200,256]{1,0:T(8,128)(2,1)S(1)}, u32[]{:S(2)}, u32[]{:S(2)}) collective-permute-start(bf16[200,256]{1,0:T(8,128)(2,1)S(1)} %add_convert_fusion.refs_4_), channel_id=1, source_target_pairs={{0,2},{1,3},{2,0},{3,1},{4,6},{5,7},{6,4},{7,5},{8,10},{9,11},{10,... | collective-permute-start | bytes 307208 | tf_op jit(solution)/shard_map/ppermute | solution.py:327
  106.3 7.3 %collective-permute-start.11 = (bf16[200,256]{1,0:T(8,128)(2,1)S(1)}, bf16[200,256]{1,0:T(8,128)(2,1)S(1)}, u32[]{:S(2)}, u32[]{:S(2)}) collective-permute-start(bf16[200,256]{1,0:T(8,128)(2,1)S(1)} %add_convert_fusion.refs_4_), channel_id=1, source_target_pairs={{0,3},{1,0},{2,1},{3,2},{4,7},{5,4},{6,5},{7,6},{8,11},{9,8},{10,9... | collective-permute-start | bytes 307208 | tf_op jit(solution)/shard_map/ppermute | solution.py:327
  107.8 6.5 %collective-permute-start.9 = (bf16[200,256]{1,0:T(8,128)(2,1)S(1)}, bf16[200,256]{1,0:T(8,128)(2,1)S(1)}, u32[]{:S(2)}, u32[]{:S(2)}) collective-permute-start(bf16[200,256]{1,0:T(8,128)(2,1)S(1)} %add_convert_fusion.refs_4_), channel_id=1, source_target_pairs={{0,1},{1,2},{2,3},{3,0},{4,5},{5,6},{6,7},{7,4},{8,9},{9,10},{10,1... | collective-permute-start | bytes 307208 | tf_op jit(solution)/shard_map/ppermute | solution.py:327
  108.5 8.8 %copy-start.1 = (bf16[200,256]{1,0:T(8,128)(2,1)}, bf16[200,256]{1,0:T(8,128)(2,1)S(1)}, u32[]{:S(2)}) copy-start(bf16[200,256]{1,0:T(8,128)(2,1)S(1)} %add_convert_fusion.1.refs_0_) | copy-start | bytes 307204
  108.5 6.9 %collective-permute-start.3 = (bf16[200,256]{1,0:T(8,128)(2,1)S(1)}, bf16[200,256]{1,0:T(8,128)(2,1)S(1)}, u32[]{:S(2)}, u32[]{:S(2)}) collective-permute-start(bf16[200,256]{1,0:T(8,128)(2,1)S(1)} %add_convert_fusion.1.refs_0_), channel_id=1, source_target_pairs={{0,1},{1,2},{2,3},{3,0},{4,5},{5,6},{6,7},{7,4},{8,9},{9,10},{10,1... | collective-permute-start | bytes 307208 | tf_op jit(solution)/shard_map/ppermute | solution.py:327
  110.7 6.2 %collective-permute-start.4 = (bf16[200,256]{1,0:T(8,128)(2,1)S(1)}, bf16[200,256]{1,0:T(8,128)(2,1)S(1)}, u32[]{:S(2)}, u32[]{:S(2)}) collective-permute-start(bf16[200,256]{1,0:T(8,128)(2,1)S(1)} %add_convert_fusion.1.refs_0_), channel_id=1, source_target_pairs={{0,2},{1,3},{2,0},{3,1},{4,6},{5,7},{6,4},{7,5},{8,10},{9,11},{10,... | collective-permute-start | bytes 307208 | tf_op jit(solution)/shard_map/ppermute | solution.py:327
  112.7 4.7 %collective-permute-start.5 = (bf16[200,256]{1,0:T(8,128)(2,1)S(1)}, bf16[200,256]{1,0:T(8,128)(2,1)S(1)}, u32[]{:S(2)}, u32[]{:S(2)}) collective-permute-start(bf16[200,256]{1,0:T(8,128)(2,1)S(1)} %add_convert_fusion.1.refs_0_), channel_id=1, source_target_pairs={{0,3},{1,0},{2,1},{3,2},{4,7},{5,4},{6,5},{7,6},{8,11},{9,8},{10,9... | collective-permute-start | bytes 307208 | tf_op jit(solution)/shard_map/ppermute | solution.py:327

commit v3 on v2

--- a/solution.py
+++ b/solution.py
@@ -57,79 +57,97 @@
     )(block_slot[None, :], pair_list.T, pair_owner[None, :])
 
 
-def pack_kernel(per, x_hbm, f_hbm, out_hbm, x_ref, f_ref, out_ref, sems, out_sems):
-    span, depth = x_ref.shape[0], f_ref.shape[0]
+def pack_kernel(per, me_ref, x_hbm, f_hbm, out_hbm, *refs):
+    f_out, (x_ref, f_ref, out_ref, sems, out_sems, f_sems) = refs[:-6], refs[-6:]
+    aux, span, width = x_ref.shape
+    depth = f_ref.shape[1]
+    keep = width // BLOCK
     full = depth // LANES
     rest = depth - full * LANES
     fold = LANES // rest
     group = -(-span // (fold * 8)) * 8
     step = span // per
     tail = out_ref.shape[0] - full * step
-    pairs = f_ref.shape[1] // (2 * BLOCK)
-
-    def fetch(p):
-        cols = slice(p * 2 * BLOCK, (p + 1) * 2 * BLOCK)
+
+    def at(d, size):
+        return pl.ds(pl.multiple_of(lax.rem(me_ref[0] + d, aux) * size, size), size)
+
+    def fetch(d):
         return [
-            pltpu.make_async_copy(src.at[:, cols], dst.at[:, cols], sems.at[k, p])
+            pltpu.make_async_copy(src.at[:, at(d, width)], dst.at[d], sems.at[k, d])
             for k, (src, dst) in enumerate(((x_hbm, x_ref), (f_hbm, f_ref)))
         ]
 
-    def send(p):
-        rows = slice(p * 2 * per, (p + 1) * 2 * per)
-        return pltpu.make_async_copy(out_ref.at[:, rows], out_hbm.at[:, rows], out_sems.at[p])
-
-    for p in range(pairs):
-        for copy in fetch(p):
+    def send(d):
+        rows = at(d, keep * per)
+        copies = [pltpu.make_async_copy(out_ref.at[:, rows], out_hbm.at[:, rows], out_sems.at[d])]
+        for a in range(keep if d else 0):
+            k = (d - 1) * keep + a
+            cols = slice(a * BLOCK, (a + 1) * BLOCK)
+            copies.append(pltpu.make_async_copy(f_ref.at[d, :, cols], f_out[k], f_sems.at[k]))
+        return copies
+
+    order = list(range(1, aux)) + [0]
+    for d in order:
+        for copy in fetch(d):
             copy.start()
-    for p in range(pairs):
-        for copy in fetch(p):
+    for d in order:
+        for copy in fetch(d):
             copy.wait()
 
         def product(k, lo, hi):
-            cols = slice((2 * p + k) * BLOCK, (2 * p + k + 1) * BLOCK)
+            cols = slice(k * BLOCK, (k + 1) * BLOCK)
             return lax.dot_general(
-                x_ref[:, cols], f_ref[lo:hi, cols], NT, preferred_element_type=F32
+                x_ref[d, :, cols], f_ref[d, lo:hi, cols], NT, preferred_element_type=F32
             )
 
-        place = slice(p * 2 * per, (p + 1) * 2 * per)
+        place = at(d, keep * per)
         for t in range(0, full, 2):
-            gs = [product(k, t * LANES, (t + 2) * LANES) for k in range(2)]
+            gs = [product(k, t * LANES, (t + 2) * LANES) for k in range(keep)]
             for half in range(2):
                 lanes = slice(half * LANES, (half + 1) * LANES)
                 rows = [g[:, lanes].reshape(step, per, LANES) for g in gs]
                 first = (t + half) * step
                 out_ref[first : first + step, place] = jnp.concatenate(rows, axis=1).astype(BF16)
         rows = []
-        for k in range(2):
+        for k in range(keep):
             g = product(k, full * LANES, depth)
             g = jnp.concatenate([g, jnp.zeros((fold * group - span, rest), F32)], axis=0)
             g = jnp.concatenate([g[q * group : (q + 1) * group] for q in range(fold)], axis=1)
             g = jnp.concatenate([g, jnp.zeros((tail * per - group, LANES), F32)], axis=0)
             rows.append(g.reshape(tail, per, LANES))
         out_ref[full * step :, place] = jnp.concatenate(rows, axis=1).astype(BF16)
-        send(p).start()
-    for p in range(pairs):
-        send(p).wait()
-
-
-def pack(xt, ft, ndev, per):
-    depth, width = ft.shape
-    blocks = width // BLOCK
+        for copy in send(d):
+            copy.start()
+    for d in order:
+        for copy in send(d):
+            copy.wait()
+
+
+def pack(me, xt, ft, ndev, aux, per):
+    depth, rows = ft.shape
+    blocks = rows // BLOCK
+    width = rows // aux
+    count = (aux - 1) * (width // BLOCK)
+    hbm = pl.BlockSpec(memory_space=pltpu.HBM)
+    shape = jax.ShapeDtypeStruct((ndev, blocks * per, LANES), BF16)
+    piece = jax.ShapeDtypeStruct((depth, BLOCK), BF16)
     return pl.pallas_call(
         functools.partial(pack_kernel, per),
-        out_shape=jax.ShapeDtypeStruct((ndev, blocks * per, LANES), BF16),
-        in_specs=[pl.BlockSpec(memory_space=pltpu.HBM)] * 2,
-        out_specs=pl.BlockSpec(memory_space=pltpu.HBM),
+        out_shape=[shape] + [piece] * count,
+        in_specs=[pl.BlockSpec(memory_space=pltpu.SMEM), hbm, hbm],
+        out_specs=[hbm] * (1 + count),
         scratch_shapes=[
-            pltpu.VMEM(xt.shape, BF16),
-            pltpu.VMEM(ft.shape, BF16),
-            pltpu.VMEM((ndev, blocks * per, LANES), BF16),
-            pltpu.SemaphoreType.DMA((2, blocks // 2)),
-            pltpu.SemaphoreType.DMA((blocks // 2,)),
+            pltpu.VMEM((aux, xt.shape[0], width), BF16),
+            pltpu.VMEM((aux, depth, width), BF16),
+            pltpu.VMEM(shape.shape, BF16),
+            pltpu.SemaphoreType.DMA((2, aux)),
+            pltpu.SemaphoreType.DMA((aux,)),
+            pltpu.SemaphoreType.DMA((count,)),
         ],
         compiler_params=pltpu.CompilerParams(vmem_limit_bytes=VMEM),
         name="pack",
-    )(xt, ft)
+    )(me, xt, ft)
 
 
 def mix_kernel(
@@ -213,83 +231,71 @@
     )(flag, low, high, g)
 
 
-def apply_kernel(per, me_ref, h_ref, f_hbm, *refs):
-    outs, f_ref, sems = refs[:-2], *refs[-2:]
-    ndev, height, lanes = h_ref.shape
-    span = outs[0].shape[0]
-    depth = f_hbm.shape[0]
-    aux, _, width = f_ref.shape
-    keep = width // BLOCK
+def apply_kernel(per, a, count, me_ref, h_ref, *refs):
+    f_hbm, e_ref, f_ref, f_sems = refs[:count], *refs[count:]
+    ndev, aux, height, lanes = h_ref.shape
+    span = e_ref.shape[0]
+    depth = f_ref.shape[1]
     full = depth // LANES
     rest = depth - full * LANES
     fold = LANES // rest
     group = -(-span // (fold * 8)) * 8
     step = span // per
-
-    def fetch(d):
-        start = pl.multiple_of(lax.rem(me_ref[0] + d, aux) * width, width)
-        return pltpu.make_async_copy(f_hbm.at[:, pl.ds(start, width)], f_ref.at[d], sems.at[d])
-
-    order = list(range(1, aux)) + [0]
-    for d in order:
-        fetch(d).start()
-    for d in order:
-        fetch(d).wait()
-        chunk = keep * per
-        first = pl.multiple_of(lax.rem(me_ref[0] + d, aux) * chunk, chunk)
+    rows = slice(a * per, (a + 1) * per)
+    start = pl.multiple_of((me_ref[0] * (height // per) + a) * BLOCK, BLOCK)
+    sources = [f_hbm[0].at[:, pl.ds(start, BLOCK)], *f_hbm[1:]]
+    copies = [pltpu.make_async_copy(sources[d], f_ref.at[d], f_sems.at[d]) for d in range(aux)]
+    for copy in copies:
+        copy.start()
+    total = jnp.zeros((span, BLOCK), F32)
+    for d in range(aux):
+        h = lax.rem(me_ref[0] + aux - d, aux)
 
         def take(lo, hi):
-            return h_ref[lo:hi, pl.ds(first, chunk)].astype(F32)
-
-        tiles = [take(t * step, (t + 1) * step) for t in range(full)]
-        tail = take(full * step, ndev)
-        for a in range(keep):
-            rows = slice(a * per, (a + 1) * per)
-            left = [v[:, rows].reshape(span, lanes).astype(BF16) for v in tiles]
-            last = tail[:, rows].reshape(-1, lanes)[:group]
-            last = [last[:, q * rest : (q + 1) * rest] for q in range(fold)]
-            last = jnp.concatenate(last, axis=0)[:span].astype(BF16)
-            left = jnp.concatenate(left + [last], axis=1)
-            cols = slice(a * BLOCK, (a + 1) * BLOCK)
-            total = jnp.dot(left, f_ref[d, :, cols], preferred_element_type=F32)
-            out = outs[a * aux + d]
-            out[...] = total.astype(out.dtype)
-
-
-def apply(me, h, ft, span, per, aux):
-    depth, rows = ft.shape
-    width = rows // aux
+            v = h_ref[lo:hi, pl.ds(h, 1)].reshape(hi - lo, height, lanes).astype(F32)
+            return v[:, rows].reshape(-1, lanes)
+
+        left = [take(t * step, (t + 1) * step).astype(BF16) for t in range(full)]
+        last = take(full * step, ndev)[:group]
+        last = [last[:, q * rest : (q + 1) * rest] for q in range(fold)]
+        last = jnp.concatenate(last, axis=0)[:span].astype(BF16)
+        left = jnp.concatenate(left + [last], axis=1)
+        copies[d].wait()
+        total += jnp.dot(left, f_ref[d], preferred_element_type=F32)
+    e_ref[...] = total.astype(BF16)
+
+
+def apply(me, h, fs, spaces, a, span, per):
+    depth, width = fs[1].shape
+    aux = h.shape[1]
     vmem = pl.BlockSpec(memory_space=pltpu.VMEM)
     return pl.pallas_call(
-        functools.partial(apply_kernel, per),
-        out_shape=[
-            pltpu.VMEM((span, BLOCK), BF16 if d else F32)
-            for a in range(width // BLOCK)
-            for d in range(aux)
-        ],
-        in_specs=[
-            pl.BlockSpec(memory_space=pltpu.SMEM),
-            vmem,
-            pl.BlockSpec(memory_space=pltpu.HBM),
-        ],
-        out_specs=[vmem] * (rows // BLOCK),
+        functools.partial(apply_kernel, per, a, len(fs)),
+        out_shape=pltpu.VMEM((span, width), BF16),
+        in_specs=[pl.BlockSpec(memory_space=pltpu.SMEM), vmem]
+        + [pl.BlockSpec(memory_space=space) for space in spaces],
+        out_specs=vmem,
         scratch_shapes=[
             pltpu.VMEM((aux, depth, width), BF16),
             pltpu.SemaphoreType.DMA((aux,)),
         ],
         compiler_params=pltpu.CompilerParams(vmem_limit_bytes=VMEM),
         name="apply",
-    )(me, h, ft)
+    )(me, h, *fs)
 
 
 def place_kernel(aux, me_ref, *refs):
-    pieces, out_ref = refs[:-1], refs[-1]
+    pieces, out_hbm, sems = refs[:-2], refs[-2], refs[-1]
     keep = len(pieces) // aux
-    for d in range(aux):
-        h = lax.rem(me_ref[0] + aux - d, aux)
-        for a in range(keep):
-            start = pl.multiple_of((h * keep + a) * BLOCK, BLOCK)
-            out_ref[:, pl.ds(start, BLOCK)] = pieces[a * aux + d][...]
+    copies = []
+    for k, piece in enumerate(pieces):
+        h = lax.rem(me_ref[0] + aux - k % aux, aux)
+        start = pl.multiple_of((h * keep + k // aux) * BLOCK, BLOCK)
+        copies.append(pltpu.make_async_copy(piece, out_hbm.at[:, pl.ds(start, BLOCK)], sems.at[k]))
+    for copy in copies:
+        copy.start()
+    for copy in copies:
+        copy.wait()
 
 
 def place(me, pieces, aux):
@@ -299,15 +305,11 @@
         functools.partial(place_kernel, aux),
         out_shape=jax.ShapeDtypeStruct((span, width * len(pieces)), BF16),
         in_specs=[pl.BlockSpec(memory_space=pltpu.SMEM)] + [vmem] * len(pieces),
-        out_specs=vmem,
+        out_specs=pl.BlockSpec(memory_space=pltpu.HBM),
+        scratch_shapes=[pltpu.SemaphoreType.DMA((len(pieces),))],
         compiler_params=pltpu.CompilerParams(vmem_limit_bytes=VMEM),
         name="place",
     )(me, *pieces)
-
-
-def exchange(v):
-    v = lax.all_to_all(v, "basis", split_axis=0, concat_axis=0, tiled=True)
-    return pltpu.with_memory_space_constraint(v, pltpu.VMEM)
 
 
 def shards(factors, orbitals, block_slot, pair_list, pair_owner):
@@ -317,24 +319,38 @@
     ft = factors.transpose(1, 2, 0).reshape(aux_dev * width, rows)
     xt = orbitals.T
     blocks = rows // BLOCK
+    keep = blocks // aux
     per = -(-(aux_dev * width * width) // (LANES * ndev * 8)) * 8
-    got = exchange(pack(xt, ft, ndev, per))
+
+    def turn(v, d):
+        return lax.ppermute(v, "aux", [(k, (k + d) % aux) for k in range(aux)])
+
+    sent, *pieces = pack(me[None], xt, ft, ndev, aux, per)
+    got = lax.all_to_all(sent, "basis", split_axis=0, concat_axis=0, tiled=True)
     counts = pair_counts(block_slot, pair_list, pair_owner, blocks)
-    back = exchange(mix(counts, got, per))
-    parts = apply(me[None], back, ft, width, per, aux)
-
-    def turn(v, d, last):
-        v = lax.ppermute(v, "aux", [(k, (k + d) % aux) for k in range(aux)])
-        return pltpu.with_memory_space_constraint(v, pltpu.VMEM) if last else v
-
-    pieces = []
-    for a in range(blocks // aux):
-        total = parts[a * aux]
+    far = aux // 2
+    fs = {(d, a): turn(pieces[(d - 1) * keep + a], d) for d in range(1, aux) for a in range(keep)}
+    early = {k: v for k, v in fs.items() if k != (far, 0)}
+    got, early = lax.optimization_barrier((got, early))
+    fs.update(early)
+    spaces = {k: pltpu.HBM if k in early else pltpu.VMEM for k in fs}
+    fs = {k: pltpu.with_memory_space_constraint(v, spaces[k]) for k, v in fs.items()}
+    fs.update({(0, a): ft for a in range(keep)})
+    got = pltpu.with_memory_space_constraint(got, pltpu.VMEM)
+    mixed = mix(counts, got, per)
+    mixed = mixed.reshape(ndev * aux, -1, LANES)
+    back = lax.all_to_all(mixed, ("basis", "aux"), split_axis=0, concat_axis=0, tiled=True)
+    back = back.reshape(ndev, aux, *back.shape[1:])
+    back = pltpu.with_memory_space_constraint(back, pltpu.VMEM)
+    done = {}
+    for a in range(keep):
+        kinds = [spaces.get((d, a), pltpu.HBM) for d in range(aux)]
+        mine = apply(me[None], back, [fs[d, a] for d in range(aux)], kinds, a, width, per)
         for d in range(1, aux):
-            total += turn(parts[a * aux + d], d, False).astype(F32)
-        total = total.astype(BF16)
-        pieces += [turn(total, d, True) if d else total for d in range(aux)]
-    return place(me[None], pieces, aux).T
+            done[d, a] = pltpu.with_memory_space_constraint(turn(mine, d), pltpu.VMEM)
+        done[0, a] = mine
+    done = [done[d, a] for a in range(keep) for d in range(aux)]
+    return place(me[None], done, aux).T
 
 
 def solution(mesh):

time: 120 us -> 115 us (0.958)
  waiting for transfers between devices: 70.9 us -> 59.9 us
  starting transfers between devices: 30.6 us -> 34.4 us
  Pallas kernels: 17.6 us -> 19.7 us
    all_to_all x2, waiting for transfers between devices: 64.8 us -> 35.2 us  [the longest x1 33.2 us: shards(): lax.all_to_all(mixed, ('basis', 'aux'), split_axis=0, concat_axis=0, tile...]
    ppermute x12, waiting for transfers between devices: 6.05 us -> 24.7 us  [turn(): return lax.ppermute(v, 'aux', [(k, (k + d) % aux) for k in range(aux)])]
    all_to_all x2, starting transfers between devices: 12.3 us -> 16.2 us  [the longest x1 8.25 us: shards(): got = lax.all_to_all(sent, 'basis', split_axis=0, concat_axis=0, tiled=True)]
    pallas_call x2 -> x3, Pallas kernels: 7.23 us -> 9.2 us  [the longest x2 4.7 us: apply(): pl.pallas_call(functools.partial(apply_kernel, per, a, len(fs)), out_shap...]
  transfers between devices with their start and end apart: 14 -> 14, of which waited for: 9 -> 8; matrix products, arithmetic and copies ran while one was open for 0% -> 0% of each run, Pallas kernels for 4% -> 8%
where the time goes in v3:
time: 115 us
  waiting for transfers between devices  59.9 us (52%)
  starting transfers between devices  34.4 us (30%)
  Pallas kernels  19.7 us (17%)
    all_to_all x1, waiting for transfers between devices, shards(): lax.all_to_all(mixed, ('basis', 'aux'), split_axis=0, concat_axis=0, tile...  33.2 us
    ppermute x12, waiting for transfers between devices, turn(): return lax.ppermute(v, 'aux', [(k, (k + d) % aux) for k in range(aux)])  24.7 us
    ppermute x12, starting transfers between devices, turn(): return lax.ppermute(v, 'aux', [(k, (k + d) % aux) for k in range(aux)])  18.2 us
    all_to_all x1, starting transfers between devices, shards(): got = lax.all_to_all(sent, 'basis', split_axis=0, concat_axis=0, tiled=True)  8.25 us
    all_to_all x1, starting transfers between devices, shards(): lax.all_to_all(mixed, ('basis', 'aux'), split_axis=0, concat_axis=0, tile...  7.95 us
    pallas_call x2, Pallas kernels, apply(): pl.pallas_call(functools.partial(apply_kernel, per, a, len(fs)), out_shap...  4.7 us
    pallas_call x1, Pallas kernels, pack(): pl.pallas_call(functools.partial(pack_kernel, per), out_shape=[shape] + [...  4.5 us
    pallas_call x1, Pallas kernels, pair_counts(): pl.pallas_call(functools.partial(count_kernel, keep), out_shape=(square,...  4.43 us
  transfers between devices with their start and end apart: 14, of which 8 were waited for; matrix products, arithmetic and copies ran while one was open for 0% of the time, Pallas kernels for 8%

profile of v3, /device:TPU:0, one launch (start us, length us, event | category | flops | bytes accessed | tf_op | source)
XLA Modules:
  0.0 114.8 jit_solution(15802459342120575867)
XLA Ops:
  0.0 4.5 %pack.1 = (bf16[32,320,128]{2,1,0:T(8,128)(2,1)}, bf16[800,256]{1,0:T(8,128)(2,1)}, bf16[800,256]{1,0:T(8,128)(2,1)}, bf16[800,256]{1,0:T(8,128)(2,1)}, bf16[800...) custom-call(s32[1]{0:T(128)} %bitcast.me_ref, bf16[200,2048]{1,0:T(8,128)(2,1)} %bitcast.17, ...), custom_call_target="tpu_custom_call" | custom-call | tf_op jit(solution)/shard_map/pack/pallas_call | solution.py:135
  4.5 8.3 %all-to-all-start = ((bf16[32,320,128]{2,1,0:T(8,128)(2,1)}), bf16[32,320,128]{2,1,0:T(8,128)(2,1)S(1)}, u32[]{:S(2)}, u32[]{:S(2)}) async-start(bf16[32,320,128]{2,1,0:T(8,128)(2,1)} %get-tuple-element.24), calls=%async_computation | async-start | bytes 5242880 | tf_op jit(solution)/shard_map/all_to_all | solution.py:329
  12.8 1.6 %collective-permute-start = (bf16[800,256]{1,0:T(8,128)(2,1)}, bf16[800,256]{1,0:T(8,128)(2,1)S(1)}, u32[]{:S(2)}, u32[]{:S(2)}) collective-permute-start(bf16[800,256]{1,0:T(8,128)(2,1)} %get-tuple-element.25), channel_id=1, source_target_pairs={{0,1},{1,2},{2,3},{3,0},{4,5},{5,6},{6,7},{7,4},{8,9},{9,10},{10,1... | collective-permute-start | bytes 1228808 | tf_op jit(solution)/shard_map/ppermute | solution.py:326
  14.4 1.6 %collective-permute-start.1 = (bf16[800,256]{1,0:T(8,128)(2,1)}, bf16[800,256]{1,0:T(8,128)(2,1)S(1)}, u32[]{:S(2)}, u32[]{:S(2)}) collective-permute-start(bf16[800,256]{1,0:T(8,128)(2,1)} %get-tuple-element.26), channel_id=1, source_target_pairs={{0,1},{1,2},{2,3},{3,0},{4,5},{5,6},{6,7},{7,4},{8,9},{9,10},{10,1... | collective-permute-start | bytes 1228808 | tf_op jit(solution)/shard_map/ppermute | solution.py:326
  15.9 1.6 %collective-permute-start.2 = (bf16[800,256]{1,0:T(8,128)(2,1)}, bf16[800,256]{1,0:T(8,128)(2,1)S(1)}, u32[]{:S(2)}, u32[]{:S(2)}) collective-permute-start(bf16[800,256]{1,0:T(8,128)(2,1)} %get-tuple-element.27), channel_id=1, source_target_pairs={{0,2},{1,3},{2,0},{3,1},{4,6},{5,7},{6,4},{7,5},{8,10},{9,11},{10,... | collective-permute-start | bytes 1228808 | tf_op jit(solution)/shard_map/ppermute | solution.py:326
  17.5 2.4 %collective-permute-start.3 = (bf16[800,256]{1,0:T(8,128)(2,1)}, bf16[800,256]{1,0:T(8,128)(2,1)S(1)}, u32[]{:S(2)}, u32[]{:S(2)}) collective-permute-start(bf16[800,256]{1,0:T(8,128)(2,1)} %get-tuple-element.28), channel_id=1, source_target_pairs={{0,3},{1,0},{2,1},{3,2},{4,7},{5,4},{6,5},{7,6},{8,11},{9,8},{10,9... | collective-permute-start | bytes 1228808 | tf_op jit(solution)/shard_map/ppermute | solution.py:326
  19.9 0.1 collective-permute-start.4
  20.0 4.4 %pair_counts.1 = (bf16[256,256]{1,0:T(8,128)(2,1)}, bf16[256,256]{1,0:T(8,128)(2,1)}, s32[1]{0:T(128)}) custom-call(s32[1,256]{1,0:T(1,128)} %bitcast.20, s32[2,2048]{1,0:T(2,128)} %bitcast.18, s32[1,2048]{1,0:T(1,128)} %bitcast.19), custom_call_target="tpu_custom_call" | custom-call | tf_op jit(solution)/shard_map/pair_counts/pallas_call | solution.py:50
  24.5 2.1 %collective-permute-done.refs_1_ = bf16[800,256]{1,0:T(8,128)(2,1)S(1)} collective-permute-done((bf16[800,256]{1,0:T(8,128)(2,1)}, bf16[800,256]{1,0:T(8,128)(2,1)S(1)}, u32[]{:S(2)}, u32[]{:S(2)}) %collective-permute-start) | collective-permute-done | bytes 409632 | tf_op jit(solution)/shard_map/ppermute | solution.py:326
  26.5 0.0 copy-start.2
  26.5 8.2 %collective-permute-done.1.refs_1_ = bf16[800,256]{1,0:T(8,128)(2,1)S(1)} collective-permute-done((bf16[800,256]{1,0:T(8,128)(2,1)}, bf16[800,256]{1,0:T(8,128)(2,1)S(1)}, u32[]{:S(2)}, u32[]{:S(2)}) %collective-permute-start.1) | collective-permute-done | bytes 409632 | tf_op jit(solution)/shard_map/ppermute | solution.py:326
  34.7 0.0 copy-start.4
  34.7 10.0 %collective-permute-done.2.refs_2_ = bf16[800,256]{1,0:T(8,128)(2,1)S(1)} collective-permute-done((bf16[800,256]{1,0:T(8,128)(2,1)}, bf16[800,256]{1,0:T(8,128)(2,1)S(1)}, u32[]{:S(2)}, u32[]{:S(2)}) %collective-permute-start.2) | collective-permute-done | bytes 409632 | tf_op jit(solution)/shard_map/ppermute | solution.py:326
  44.7 0.0 copy-start.5
  44.7 0.0 collective-permute-done.3.refs_3_
  44.7 0.0 copy-done.4
  44.7 0.7 copy-done.5
  45.5 0.0 copy-start.3
  45.5 0.0 collective-permute-done.4.refs_3_
  45.5 1.9 %all-to-all-done.g_ref = bf16[32,320,128]{2,1,0:T(8,128)(2,1)S(1)} async-done(((bf16[32,320,128]{2,1,0:T(8,128)(2,1)}), bf16[32,320,128]{2,1,0:T(8,128)(2,1)S(1)}, u32[]{:S(2)}, u32[]{:S(2)}) %all-to-all-start) | async-done | bytes 2621472 | tf_op jit(solution)/shard_map/all_to_all | solution.py:329
  47.4 4.1 %mix.1 = bf16[32,320,128]{2,1,0:T(8,128)(2,1)} custom-call(s32[1]{0:T(128)} %get-tuple-element.21.flag_ref, bf16[256,256]{1,0:T(8,128)(2,1)} %get-tuple-element.22.low_hbm, bf16[256,256]{1,0:T(8,128)(2,1)} %get-tuple-element.23.high_hbm, bf16[32,320,128]{2,1,0:T(8,128)(2,1)S(1)} %all-to-all-done.g_ref), custom_call_target="tpu_custom_call" | custom-call | tf_op jit(solution)/shard_map/mix/pallas_call | solution.py:210
  51.5 0.0 copy-done.2
  51.6 0.0 copy-done.3
  51.6 0.0 copy-start.6
  51.6 8.0 %all-to-all-start.1 = ((bf16[128,80,128]{2,1,0:T(8,128)(2,1)}), bf16[128,80,128]{2,1,0:T(8,128)(2,1)S(1)}, u32[]{:S(2)}, u32[]{:S(2)}) async-start(bf16[128,80,128]{2,1,0:T(8,128)(2,1)} %bitcast.16), calls=%async_computation.1 | async-start | bytes 5242880 | tf_op jit(solution)/shard_map/all_to_all | solution.py:342
  59.5 0.0 copy-done.6
  59.5 2.5 %collective-permute-start.5 = (bf16[800,256]{1,0:T(8,128)(2,1)S(1)}, bf16[800,256]{1,0:T(8,128)(2,1)S(1)}, u32[]{:S(2)}, u32[]{:S(2)}) collective-permute-start(bf16[800,256]{1,0:T(8,128)(2,1)S(1)} %copy-done.6), channel_id=1, source_target_pairs={{0,2},{1,3},{2,0},{3,1},{4,6},{5,7},{6,4},{7,5},{8,10},{9,11},{10,... | collective-permute-start | bytes 1228808 | tf_op jit(solution)/shard_map/ppermute | solution.py:326
  62.1 33.2 %all-to-all-done.1 = bf16[128,80,128]{2,1,0:T(8,128)(2,1)S(1)} async-done(((bf16[128,80,128]{2,1,0:T(8,128)(2,1)}), bf16[128,80,128]{2,1,0:T(8,128)(2,1)S(1)}, u32[]{:S(2)}, u32[]{:S(2)}) %all-to-all-start.1) | async-done | bytes 2621472 | tf_op jit(solution)/shard_map/all_to_all | solution.py:342
  95.3 2.4 %apply.3.refs_4_ = bf16[200,256]{1,0:T(8,128)(2,1)S(1)} custom-call(s32[1]{0:T(128)} %bitcast.me_ref, bf16[32,4,80,128]{3,2,1,0:T(8,128)(2,1)S(1)} %bitcast.11, bf16[800,2048]{1,0:T(8,128)(2,1)} %bitcast.14, bf16[800,256]{1,0:T(8,128)(2,1)} %copy-done.4, bf16[800,256]{1,0:T(8,128)(2,1)} %copy-done.5, bf16[800,256]{1,0:T(8,128)(2,1)} %collective-permute-done.4.refs_3_), custom_call_target="tpu_custom_call" | custom-call | tf_op jit(solution)/shard_map/apply/pallas_call | solution.py:272
  97.7 0.0 copy-start
  97.7 1.1 collective-permute-start.10
  98.8 2.4 %collective-permute-start.11 = (bf16[200,256]{1,0:T(8,128)(2,1)S(1)}, bf16[200,256]{1,0:T(8,128)(2,1)S(1)}, u32[]{:S(2)}, u32[]{:S(2)}) collective-permute-start(bf16[200,256]{1,0:T(8,128)(2,1)S(1)} %apply.3.refs_4_), channel_id=1, source_target_pairs={{0,3},{1,0},{2,1},{3,2},{4,7},{5,4},{6,5},{7,6},{8,11},{9,8},{10,9... | collective-permute-start | bytes 307208 | tf_op jit(solution)/shard_map/ppermute | solution.py:326
  101.1 0.0 collective-permute-start.9
  101.1 0.0 collective-permute-done.5.refs_2_
  101.1 2.3 %apply.2.refs_0_ = bf16[200,256]{1,0:T(8,128)(2,1)S(1)} custom-call(s32[1]{0:T(128)} %bitcast.me_ref, bf16[32,4,80,128]{3,2,1,0:T(8,128)(2,1)S(1)} %bitcast.12, bf16[800,2048]{1,0:T(8,128)(2,1)} %bitcast.15, bf16[800,256]{1,0:T(8,128)(2,1)} %copy-done.2, bf16[800,256]{1,0:T(8,128)(2,1)S(1)} %collective-permute-done.5.refs_2_, bf16[800,256]{1,0:T(8,128)(2,1)} %copy-done.3), custom_call_target="tpu_custom_call" | custom-call | tf_op jit(solution)/shard_map/apply/pallas_call | solution.py:272
  103.5 0.0 copy-done
  103.5 0.0 copy-start.1
  103.5 1.2 %collective-permute-start.6 = (bf16[200,256]{1,0:T(8,128)(2,1)S(1)}, bf16[200,256]{1,0:T(8,128)(2,1)S(1)}, u32[]{:S(2)}, u32[]{:S(2)}) collective-permute-start(bf16[200,256]{1,0:T(8,128)(2,1)S(1)} %apply.2.refs_0_), channel_id=1, source_target_pairs={{0,1},{1,2},{2,3},{3,0},{4,5},{5,6},{6,7},{7,4},{8,9},{9,10},{10,1... | collective-permute-start | bytes 307208 | tf_op jit(solution)/shard_map/ppermute | solution.py:326
  104.6 3.6 %collective-permute-start.7 = (bf16[200,256]{1,0:T(8,128)(2,1)S(1)}, bf16[200,256]{1,0:T(8,128)(2,1)S(1)}, u32[]{:S(2)}, u32[]{:S(2)}) collective-permute-start(bf16[200,256]{1,0:T(8,128)(2,1)S(1)} %apply.2.refs_0_), channel_id=1, source_target_pairs={{0,2},{1,3},{2,0},{3,1},{4,6},{5,7},{6,4},{7,5},{8,10},{9,11},{10,... | collective-permute-start | bytes 307208 | tf_op jit(solution)/shard_map/ppermute | solution.py:326
  108.3 0.0 collective-permute-done.10.refs_6_
  108.3 0.2 collective-permute-start.8
  108.4 0.0 collective-permute-done.11.refs_7_
  108.4 0.0 collective-permute-done.9.refs_5_
  108.4 1.7 %collective-permute-done.6.refs_1_ = bf16[200,256]{1,0:T(8,128)(2,1)S(1)} collective-permute-done((bf16[200,256]{1,0:T(8,128)(2,1)S(1)}, bf16[200,256]{1,0:T(8,128)(2,1)S(1)}, u32[]{:S(2)}, u32[]{:S(2)}) %collective-permute-start.6) | collective-permute-done | bytes 102432 | tf_op jit(solution)/shard_map/ppermute | solution.py:326
  110.1 2.5 %collective-permute-done.7.refs_2_ = bf16[200,256]{1,0:T(8,128)(2,1)S(1)} collective-permute-done((bf16[200,256]{1,0:T(8,128)(2,1)S(1)}, bf16[200,256]{1,0:T(8,128)(2,1)S(1)}, u32[]{:S(2)}, u32[]{:S(2)}) %collective-permute-start.7) | collective-permute-done | bytes 102432 | tf_op jit(solution)/shard_map/ppermute | solution.py:326
  112.6 0.3 collective-permute-done.8.refs_3_
  112.9 0.0 copy-done.1
  112.9 1.9 %place.1 = bf16[200,2048]{1,0:T(8,128)(2,1)} custom-call(s32[1]{0:T(128)} %bitcast.me_ref, bf16[200,256]{1,0:T(8,128)(2,1)} %copy-done.1, bf16[200,256]{1,0:T(8,128)(2,1)S(1)} %collective-permute-done.6.refs_1_, bf16[200,256]{1,0:T(8,128)(2,1)S(1)} %collective-permute-done.7.refs_2_, bf16[200,256]{1,0:T(8,128)(2,1)S(1)} %collective-permute-done.8.refs_3_, ...), custom_call_target="tpu_custom_call" | custom-call | tf_op jit(solution)/shard_map/place/pallas_call | solution.py:304
Async XLA Ops:
  4.5 42.9 %all-to-all-start = ((bf16[32,320,128]{2,1,0:T(8,128)(2,1)}), bf16[32,320,128]{2,1,0:T(8,128)(2,1)S(1)}, u32[]{:S(2)}, u32[]{:S(2)}) async-start(bf16[32,320,128]{2,1,0:T(8,128)(2,1)} %get-tuple-element.24), calls=%async_computation | async-start | bytes 5242880 | tf_op jit(solution)/shard_map/all_to_all | solution.py:329
  12.8 13.8 %collective-permute-start = (bf16[800,256]{1,0:T(8,128)(2,1)}, bf16[800,256]{1,0:T(8,128)(2,1)S(1)}, u32[]{:S(2)}, u32[]{:S(2)}) collective-permute-start(bf16[800,256]{1,0:T(8,128)(2,1)} %get-tuple-element.25), channel_id=1, source_target_pairs={{0,1},{1,2},{2,3},{3,0},{4,5},{5,6},{6,7},{7,4},{8,9},{9,10},{10,1... | collective-permute-start | bytes 1228808 | tf_op jit(solution)/shard_map/ppermute | solution.py:326
  14.4 20.4 %collective-permute-start.1 = (bf16[800,256]{1,0:T(8,128)(2,1)}, bf16[800,256]{1,0:T(8,128)(2,1)S(1)}, u32[]{:S(2)}, u32[]{:S(2)}) collective-permute-start(bf16[800,256]{1,0:T(8,128)(2,1)} %get-tuple-element.26), channel_id=1, source_target_pairs={{0,1},{1,2},{2,3},{3,0},{4,5},{5,6},{6,7},{7,4},{8,9},{9,10},{10,1... | collective-permute-start | bytes 1228808 | tf_op jit(solution)/shard_map/ppermute | solution.py:326
  15.9 28.8 %collective-permute-start.2 = (bf16[800,256]{1,0:T(8,128)(2,1)}, bf16[800,256]{1,0:T(8,128)(2,1)S(1)}, u32[]{:S(2)}, u32[]{:S(2)}) collective-permute-start(bf16[800,256]{1,0:T(8,128)(2,1)} %get-tuple-element.27), channel_id=1, source_target_pairs={{0,2},{1,3},{2,0},{3,1},{4,6},{5,7},{6,4},{7,5},{8,10},{9,11},{10,... | collective-permute-start | bytes 1228808 | tf_op jit(solution)/shard_map/ppermute | solution.py:326
  17.5 27.2 %collective-permute-start.3 = (bf16[800,256]{1,0:T(8,128)(2,1)}, bf16[800,256]{1,0:T(8,128)(2,1)S(1)}, u32[]{:S(2)}, u32[]{:S(2)}) collective-permute-start(bf16[800,256]{1,0:T(8,128)(2,1)} %get-tuple-element.28), channel_id=1, source_target_pairs={{0,3},{1,0},{2,1},{3,2},{4,7},{5,4},{6,5},{7,6},{8,11},{9,8},{10,9... | collective-permute-start | bytes 1228808 | tf_op jit(solution)/shard_map/ppermute | solution.py:326
  19.9 25.5 %collective-permute-start.4 = (bf16[800,256]{1,0:T(8,128)(2,1)}, bf16[800,256]{1,0:T(8,128)(2,1)}, u32[]{:S(2)}, u32[]{:S(2)}) collective-permute-start(bf16[800,256]{1,0:T(8,128)(2,1)} %get-tuple-element.29), channel_id=1, source_target_pairs={{0,3},{1,0},{2,1},{3,2},{4,7},{5,4},{6,5},{7,6},{8,11},{9,8},{10,9... | collective-permute-start | bytes 1228808 | tf_op jit(solution)/shard_map/ppermute | solution.py:326
  26.5 25.0 %copy-start.2 = (bf16[800,256]{1,0:T(8,128)(2,1)}, bf16[800,256]{1,0:T(8,128)(2,1)S(1)}, u32[]{:S(2)}) copy-start(bf16[800,256]{1,0:T(8,128)(2,1)S(1)} %collective-permute-done.refs_1_) | copy-start | bytes 1228804
  34.7 10.0 %copy-start.4 = (bf16[800,256]{1,0:T(8,128)(2,1)}, bf16[800,256]{1,0:T(8,128)(2,1)S(1)}, u32[]{:S(2)}) copy-start(bf16[800,256]{1,0:T(8,128)(2,1)S(1)} %collective-permute-done.1.refs_1_) | copy-start | bytes 1228804
  44.7 0.8 copy-start.5
  45.5 6.1 %copy-start.3 = (bf16[800,256]{1,0:T(8,128)(2,1)}, bf16[800,256]{1,0:T(8,128)(2,1)S(1)}, u32[]{:S(2)}) copy-start(bf16[800,256]{1,0:T(8,128)(2,1)S(1)} %collective-permute-done.3.refs_3_) | copy-start | bytes 1228804
  51.6 8.0 %copy-start.6 = (bf16[800,256]{1,0:T(8,128)(2,1)S(1)}, bf16[800,256]{1,0:T(8,128)(2,1)}, u32[]{:S(2)}) copy-start(bf16[800,256]{1,0:T(8,128)(2,1)} %get-tuple-element.32) | copy-start | bytes 1228804
  51.6 43.7 %all-to-all-start.1 = ((bf16[128,80,128]{2,1,0:T(8,128)(2,1)}), bf16[128,80,128]{2,1,0:T(8,128)(2,1)S(1)}, u32[]{:S(2)}, u32[]{:S(2)}) async-start(bf16[128,80,128]{2,1,0:T(8,128)(2,1)} %bitcast.16), calls=%async_computation.1 | async-start | bytes 5242880 | tf_op jit(solution)/shard_map/all_to_all | solution.py:342
  59.5 41.6 %collective-permute-start.5 = (bf16[800,256]{1,0:T(8,128)(2,1)S(1)}, bf16[800,256]{1,0:T(8,128)(2,1)S(1)}, u32[]{:S(2)}, u32[]{:S(2)}) collective-permute-start(bf16[800,256]{1,0:T(8,128)(2,1)S(1)} %copy-done.6), channel_id=1, source_target_pairs={{0,2},{1,3},{2,0},{3,1},{4,6},{5,7},{6,4},{7,5},{8,10},{9,11},{10,... | collective-permute-start | bytes 1228808 | tf_op jit(solution)/shard_map/ppermute | solution.py:326
  97.7 5.8 %copy-start = (bf16[200,256]{1,0:T(8,128)(2,1)}, bf16[200,256]{1,0:T(8,128)(2,1)S(1)}, u32[]{:S(2)}) copy-start(bf16[200,256]{1,0:T(8,128)(2,1)S(1)} %apply.3.refs_4_) | copy-start | bytes 307204
  97.7 10.6 %collective-permute-start.10 = (bf16[200,256]{1,0:T(8,128)(2,1)S(1)}, bf16[200,256]{1,0:T(8,128)(2,1)S(1)}, u32[]{:S(2)}, u32[]{:S(2)}) collective-permute-start(bf16[200,256]{1,0:T(8,128)(2,1)S(1)} %apply.3.refs_4_), channel_id=1, source_target_pairs={{0,2},{1,3},{2,0},{3,1},{4,6},{5,7},{6,4},{7,5},{8,10},{9,11},{10,... | collective-permute-start | bytes 307208 | tf_op jit(solution)/shard_map/ppermute | solution.py:326
  98.8 9.7 %collective-permute-start.11 = (bf16[200,256]{1,0:T(8,128)(2,1)S(1)}, bf16[200,256]{1,0:T(8,128)(2,1)S(1)}, u32[]{:S(2)}, u32[]{:S(2)}) collective-permute-start(bf16[200,256]{1,0:T(8,128)(2,1)S(1)} %apply.3.refs_4_), channel_id=1, source_target_pairs={{0,3},{1,0},{2,1},{3,2},{4,7},{5,4},{6,5},{7,6},{8,11},{9,8},{10,9... | collective-permute-start | bytes 307208 | tf_op jit(solution)/shard_map/ppermute | solution.py:326
  101.1 7.3 %collective-permute-start.9 = (bf16[200,256]{1,0:T(8,128)(2,1)S(1)}, bf16[200,256]{1,0:T(8,128)(2,1)S(1)}, u32[]{:S(2)}, u32[]{:S(2)}) collective-permute-start(bf16[200,256]{1,0:T(8,128)(2,1)S(1)} %apply.3.refs_4_), channel_id=1, source_target_pairs={{0,1},{1,2},{2,3},{3,0},{4,5},{5,6},{6,7},{7,4},{8,9},{9,10},{10,1... | collective-permute-start | bytes 307208 | tf_op jit(solution)/shard_map/ppermute | solution.py:326
  103.5 9.4 %copy-start.1 = (bf16[200,256]{1,0:T(8,128)(2,1)}, bf16[200,256]{1,0:T(8,128)(2,1)S(1)}, u32[]{:S(2)}) copy-start(bf16[200,256]{1,0:T(8,128)(2,1)S(1)} %apply.2.refs_0_) | copy-start | bytes 307204
  103.5 6.6 %collective-permute-start.6 = (bf16[200,256]{1,0:T(8,128)(2,1)S(1)}, bf16[200,256]{1,0:T(8,128)(2,1)S(1)}, u32[]{:S(2)}, u32[]{:S(2)}) collective-permute-start(bf16[200,256]{1,0:T(8,128)(2,1)S(1)} %apply.2.refs_0_), channel_id=1, source_target_pairs={{0,1},{1,2},{2,3},{3,0},{4,5},{5,6},{6,7},{7,4},{8,9},{9,10},{10,1... | collective-permute-start | bytes 307208 | tf_op jit(solution)/shard_map/ppermute | solution.py:326
  104.6 8.0 %collective-permute-start.7 = (bf16[200,256]{1,0:T(8,128)(2,1)S(1)}, bf16[200,256]{1,0:T(8,128)(2,1)S(1)}, u32[]{:S(2)}, u32[]{:S(2)}) collective-permute-start(bf16[200,256]{1,0:T(8,128)(2,1)S(1)} %apply.2.refs_0_), channel_id=1, source_target_pairs={{0,2},{1,3},{2,0},{3,1},{4,6},{5,7},{6,4},{7,5},{8,10},{9,11},{10,... | collective-permute-start | bytes 307208 | tf_op jit(solution)/shard_map/ppermute | solution.py:326
  108.3 4.7 %collective-permute-start.8 = (bf16[200,256]{1,0:T(8,128)(2,1)S(1)}, bf16[200,256]{1,0:T(8,128)(2,1)S(1)}, u32[]{:S(2)}, u32[]{:S(2)}) collective-permute-start(bf16[200,256]{1,0:T(8,128)(2,1)S(1)} %apply.2.refs_0_), channel_id=1, source_target_pairs={{0,3},{1,0},{2,1},{3,2},{4,7},{5,4},{6,5},{7,6},{8,11},{9,8},{10,9... | collective-permute-start | bytes 307208 | tf_op jit(solution)/shard_map/ppermute | solution.py:326

commit v4 on v3

--- a/solution.py
+++ b/solution.py
@@ -80,7 +80,10 @@
 
     def send(d):
         rows = at(d, keep * per)
-        copies = [pltpu.make_async_copy(out_ref.at[:, rows], out_hbm.at[:, rows], out_sems.at[d])]
+        return pltpu.make_async_copy(out_ref.at[:, rows], out_hbm.at[:, rows], out_sems.at[d])
+
+    def pass_on(d):
+        copies = []
         for a in range(keep if d else 0):
             k = (d - 1) * keep + a
             cols = slice(a * BLOCK, (a + 1) * BLOCK)
@@ -94,6 +97,8 @@
     for d in order:
         for copy in fetch(d):
             copy.wait()
+        for copy in pass_on(d):
+            copy.start()
 
         def product(k, lo, hi):
             cols = slice(k * BLOCK, (k + 1) * BLOCK)
@@ -117,10 +122,9 @@
             g = jnp.concatenate([g, jnp.zeros((tail * per - group, LANES), F32)], axis=0)
             rows.append(g.reshape(tail, per, LANES))
         out_ref[full * step :, place] = jnp.concatenate(rows, axis=1).astype(BF16)
-        for copy in send(d):
-            copy.start()
+        send(d).start()
     for d in order:
-        for copy in send(d):
+        for copy in (*pass_on(d), send(d)):
             copy.wait()
 
 

time: 115 us -> 115 us (level)
  no operation moved by 1% of the time
where the time goes in v4:
time: 115 us
  waiting for transfers between devices  59.9 us (52%)
  starting transfers between devices  34.4 us (30%)
  Pallas kernels  19.7 us (17%)
    all_to_all x1, waiting for transfers between devices, shards(): lax.all_to_all(mixed, ('basis', 'aux'), split_axis=0, concat_axis=0, tile...  33.2 us
    ppermute x12, waiting for transfers between devices, turn(): return lax.ppermute(v, 'aux', [(k, (k + d) % aux) for k in range(aux)])  24.7 us
    ppermute x12, starting transfers between devices, turn(): return lax.ppermute(v, 'aux', [(k, (k + d) % aux) for k in range(aux)])  18.2 us
    all_to_all x1, starting transfers between devices, shards(): got = lax.all_to_all(sent, 'basis', split_axis=0, concat_axis=0, tiled=True)  8.25 us
    all_to_all x1, starting transfers between devices, shards(): lax.all_to_all(mixed, ('basis', 'aux'), split_axis=0, concat_axis=0, tile...  7.95 us
    pallas_call x2, Pallas kernels, apply(): pl.pallas_call(functools.partial(apply_kernel, per, a, len(fs)), out_shap...  4.7 us
    pallas_call x1, Pallas kernels, pack(): pl.pallas_call(functools.partial(pack_kernel, per), out_shape=[shape] + [...  4.5 us
    pallas_call x1, Pallas kernels, pair_counts(): pl.pallas_call(functools.partial(count_kernel, keep), out_shape=(square,...  4.43 us
  transfers between devices with their start and end apart: 14, of which 8 were waited for; matrix products, arithmetic and copies ran while one was open for 0% of the time, Pallas kernels for 8%

profile of v4, /device:TPU:0, one launch (start us, length us, event | category | flops | bytes accessed | tf_op | source)
XLA Modules:
  0.0 114.8 jit_solution(7576175514303433086)
XLA Ops:
  0.0 4.5 %pack.1 = (bf16[32,320,128]{2,1,0:T(8,128)(2,1)}, bf16[800,256]{1,0:T(8,128)(2,1)}, bf16[800,256]{1,0:T(8,128)(2,1)}, bf16[800,256]{1,0:T(8,128)(2,1)}, bf16[800...) custom-call(s32[1]{0:T(128)} %bitcast.me_ref, bf16[200,2048]{1,0:T(8,128)(2,1)} %bitcast.17, ...), custom_call_target="tpu_custom_call" | custom-call | tf_op jit(solution)/shard_map/pack/pallas_call | solution.py:139
  4.5 8.3 %all-to-all-start = ((bf16[32,320,128]{2,1,0:T(8,128)(2,1)}), bf16[32,320,128]{2,1,0:T(8,128)(2,1)S(1)}, u32[]{:S(2)}, u32[]{:S(2)}) async-start(bf16[32,320,128]{2,1,0:T(8,128)(2,1)} %get-tuple-element.24), calls=%async_computation | async-start | bytes 5242880 | tf_op jit(solution)/shard_map/all_to_all | solution.py:333
  12.8 1.6 %collective-permute-start = (bf16[800,256]{1,0:T(8,128)(2,1)}, bf16[800,256]{1,0:T(8,128)(2,1)S(1)}, u32[]{:S(2)}, u32[]{:S(2)}) collective-permute-start(bf16[800,256]{1,0:T(8,128)(2,1)} %get-tuple-element.25), channel_id=1, source_target_pairs={{0,1},{1,2},{2,3},{3,0},{4,5},{5,6},{6,7},{7,4},{8,9},{9,10},{10,1... | collective-permute-start | bytes 1228808 | tf_op jit(solution)/shard_map/ppermute | solution.py:330
  14.4 1.6 %collective-permute-start.1 = (bf16[800,256]{1,0:T(8,128)(2,1)}, bf16[800,256]{1,0:T(8,128)(2,1)S(1)}, u32[]{:S(2)}, u32[]{:S(2)}) collective-permute-start(bf16[800,256]{1,0:T(8,128)(2,1)} %get-tuple-element.26), channel_id=1, source_target_pairs={{0,1},{1,2},{2,3},{3,0},{4,5},{5,6},{6,7},{7,4},{8,9},{9,10},{10,1... | collective-permute-start | bytes 1228808 | tf_op jit(solution)/shard_map/ppermute | solution.py:330
  15.9 1.6 %collective-permute-start.2 = (bf16[800,256]{1,0:T(8,128)(2,1)}, bf16[800,256]{1,0:T(8,128)(2,1)S(1)}, u32[]{:S(2)}, u32[]{:S(2)}) collective-permute-start(bf16[800,256]{1,0:T(8,128)(2,1)} %get-tuple-element.27), channel_id=1, source_target_pairs={{0,2},{1,3},{2,0},{3,1},{4,6},{5,7},{6,4},{7,5},{8,10},{9,11},{10,... | collective-permute-start | bytes 1228808 | tf_op jit(solution)/shard_map/ppermute | solution.py:330
  17.5 2.4 %collective-permute-start.3 = (bf16[800,256]{1,0:T(8,128)(2,1)}, bf16[800,256]{1,0:T(8,128)(2,1)S(1)}, u32[]{:S(2)}, u32[]{:S(2)}) collective-permute-start(bf16[800,256]{1,0:T(8,128)(2,1)} %get-tuple-element.28), channel_id=1, source_target_pairs={{0,3},{1,0},{2,1},{3,2},{4,7},{5,4},{6,5},{7,6},{8,11},{9,8},{10,9... | collective-permute-start | bytes 1228808 | tf_op jit(solution)/shard_map/ppermute | solution.py:330
  19.9 0.1 collective-permute-start.4
  20.0 4.4 %pair_counts.1 = (bf16[256,256]{1,0:T(8,128)(2,1)}, bf16[256,256]{1,0:T(8,128)(2,1)}, s32[1]{0:T(128)}) custom-call(s32[1,256]{1,0:T(1,128)} %bitcast.20, s32[2,2048]{1,0:T(2,128)} %bitcast.18, s32[1,2048]{1,0:T(1,128)} %bitcast.19), custom_call_target="tpu_custom_call" | custom-call | tf_op jit(solution)/shard_map/pair_counts/pallas_call | solution.py:50
  24.5 2.1 %collective-permute-done.refs_1_ = bf16[800,256]{1,0:T(8,128)(2,1)S(1)} collective-permute-done((bf16[800,256]{1,0:T(8,128)(2,1)}, bf16[800,256]{1,0:T(8,128)(2,1)S(1)}, u32[]{:S(2)}, u32[]{:S(2)}) %collective-permute-start) | collective-permute-done | bytes 409632 | tf_op jit(solution)/shard_map/ppermute | solution.py:330
  26.5 0.0 copy-start.2
  26.5 8.2 %collective-permute-done.1.refs_1_ = bf16[800,256]{1,0:T(8,128)(2,1)S(1)} collective-permute-done((bf16[800,256]{1,0:T(8,128)(2,1)}, bf16[800,256]{1,0:T(8,128)(2,1)S(1)}, u32[]{:S(2)}, u32[]{:S(2)}) %collective-permute-start.1) | collective-permute-done | bytes 409632 | tf_op jit(solution)/shard_map/ppermute | solution.py:330
  34.7 0.0 copy-start.4
  34.7 10.0 %collective-permute-done.2.refs_2_ = bf16[800,256]{1,0:T(8,128)(2,1)S(1)} collective-permute-done((bf16[800,256]{1,0:T(8,128)(2,1)}, bf16[800,256]{1,0:T(8,128)(2,1)S(1)}, u32[]{:S(2)}, u32[]{:S(2)}) %collective-permute-start.2) | collective-permute-done | bytes 409632 | tf_op jit(solution)/shard_map/ppermute | solution.py:330
  44.7 0.0 copy-start.5
  44.7 0.0 collective-permute-done.3.refs_3_
  44.7 0.0 copy-done.4
  44.7 0.7 copy-done.5
  45.5 0.0 copy-start.3
  45.5 0.0 collective-permute-done.4.refs_3_
  45.5 1.9 %all-to-all-done.g_ref = bf16[32,320,128]{2,1,0:T(8,128)(2,1)S(1)} async-done(((bf16[32,320,128]{2,1,0:T(8,128)(2,1)}), bf16[32,320,128]{2,1,0:T(8,128)(2,1)S(1)}, u32[]{:S(2)}, u32[]{:S(2)}) %all-to-all-start) | async-done | bytes 2621472 | tf_op jit(solution)/shard_map/all_to_all | solution.py:333
  47.4 4.1 %mix.1 = bf16[32,320,128]{2,1,0:T(8,128)(2,1)} custom-call(s32[1]{0:T(128)} %get-tuple-element.21.flag_ref, bf16[256,256]{1,0:T(8,128)(2,1)} %get-tuple-element.22.low_hbm, bf16[256,256]{1,0:T(8,128)(2,1)} %get-tuple-element.23.high_hbm, bf16[32,320,128]{2,1,0:T(8,128)(2,1)S(1)} %all-to-all-done.g_ref), custom_call_target="tpu_custom_call" | custom-call | tf_op jit(solution)/shard_map/mix/pallas_call | solution.py:214
  51.5 0.0 copy-done.2
  51.6 0.0 copy-done.3
  51.6 0.0 copy-start.6
  51.6 8.0 %all-to-all-start.1 = ((bf16[128,80,128]{2,1,0:T(8,128)(2,1)}), bf16[128,80,128]{2,1,0:T(8,128)(2,1)S(1)}, u32[]{:S(2)}, u32[]{:S(2)}) async-start(bf16[128,80,128]{2,1,0:T(8,128)(2,1)} %bitcast.16), calls=%async_computation.1 | async-start | bytes 5242880 | tf_op jit(solution)/shard_map/all_to_all | solution.py:346
  59.5 0.0 copy-done.6
  59.5 2.5 %collective-permute-start.5 = (bf16[800,256]{1,0:T(8,128)(2,1)S(1)}, bf16[800,256]{1,0:T(8,128)(2,1)S(1)}, u32[]{:S(2)}, u32[]{:S(2)}) collective-permute-start(bf16[800,256]{1,0:T(8,128)(2,1)S(1)} %copy-done.6), channel_id=1, source_target_pairs={{0,2},{1,3},{2,0},{3,1},{4,6},{5,7},{6,4},{7,5},{8,10},{9,11},{10,... | collective-permute-start | bytes 1228808 | tf_op jit(solution)/shard_map/ppermute | solution.py:330
  62.1 33.2 %all-to-all-done.1 = bf16[128,80,128]{2,1,0:T(8,128)(2,1)S(1)} async-done(((bf16[128,80,128]{2,1,0:T(8,128)(2,1)}), bf16[128,80,128]{2,1,0:T(8,128)(2,1)S(1)}, u32[]{:S(2)}, u32[]{:S(2)}) %all-to-all-start.1) | async-done | bytes 2621472 | tf_op jit(solution)/shard_map/all_to_all | solution.py:346
  95.3 2.4 %apply.3.refs_4_ = bf16[200,256]{1,0:T(8,128)(2,1)S(1)} custom-call(s32[1]{0:T(128)} %bitcast.me_ref, bf16[32,4,80,128]{3,2,1,0:T(8,128)(2,1)S(1)} %bitcast.11, bf16[800,2048]{1,0:T(8,128)(2,1)} %bitcast.14, bf16[800,256]{1,0:T(8,128)(2,1)} %copy-done.4, bf16[800,256]{1,0:T(8,128)(2,1)} %copy-done.5, bf16[800,256]{1,0:T(8,128)(2,1)} %collective-permute-done.4.refs_3_), custom_call_target="tpu_custom_call" | custom-call | tf_op jit(solution)/shard_map/apply/pallas_call | solution.py:276
  97.7 0.0 copy-start
  97.7 1.1 collective-permute-start.10
  98.8 2.4 %collective-permute-start.11 = (bf16[200,256]{1,0:T(8,128)(2,1)S(1)}, bf16[200,256]{1,0:T(8,128)(2,1)S(1)}, u32[]{:S(2)}, u32[]{:S(2)}) collective-permute-start(bf16[200,256]{1,0:T(8,128)(2,1)S(1)} %apply.3.refs_4_), channel_id=1, source_target_pairs={{0,3},{1,0},{2,1},{3,2},{4,7},{5,4},{6,5},{7,6},{8,11},{9,8},{10,9... | collective-permute-start | bytes 307208 | tf_op jit(solution)/shard_map/ppermute | solution.py:330
  101.1 0.0 collective-permute-start.9
  101.1 0.0 collective-permute-done.5.refs_2_
  101.1 2.3 %apply.2.refs_0_ = bf16[200,256]{1,0:T(8,128)(2,1)S(1)} custom-call(s32[1]{0:T(128)} %bitcast.me_ref, bf16[32,4,80,128]{3,2,1,0:T(8,128)(2,1)S(1)} %bitcast.12, bf16[800,2048]{1,0:T(8,128)(2,1)} %bitcast.15, bf16[800,256]{1,0:T(8,128)(2,1)} %copy-done.2, bf16[800,256]{1,0:T(8,128)(2,1)S(1)} %collective-permute-done.5.refs_2_, bf16[800,256]{1,0:T(8,128)(2,1)} %copy-done.3), custom_call_target="tpu_custom_call" | custom-call | tf_op jit(solution)/shard_map/apply/pallas_call | solution.py:276
  103.5 0.0 copy-done
  103.5 0.0 copy-start.1
  103.5 1.2 %collective-permute-start.6 = (bf16[200,256]{1,0:T(8,128)(2,1)S(1)}, bf16[200,256]{1,0:T(8,128)(2,1)S(1)}, u32[]{:S(2)}, u32[]{:S(2)}) collective-permute-start(bf16[200,256]{1,0:T(8,128)(2,1)S(1)} %apply.2.refs_0_), channel_id=1, source_target_pairs={{0,1},{1,2},{2,3},{3,0},{4,5},{5,6},{6,7},{7,4},{8,9},{9,10},{10,1... | collective-permute-start | bytes 307208 | tf_op jit(solution)/shard_map/ppermute | solution.py:330
  104.6 3.6 %collective-permute-start.7 = (bf16[200,256]{1,0:T(8,128)(2,1)S(1)}, bf16[200,256]{1,0:T(8,128)(2,1)S(1)}, u32[]{:S(2)}, u32[]{:S(2)}) collective-permute-start(bf16[200,256]{1,0:T(8,128)(2,1)S(1)} %apply.2.refs_0_), channel_id=1, source_target_pairs={{0,2},{1,3},{2,0},{3,1},{4,6},{5,7},{6,4},{7,5},{8,10},{9,11},{10,... | collective-permute-start | bytes 307208 | tf_op jit(solution)/shard_map/ppermute | solution.py:330
  108.3 0.0 collective-permute-done.10.refs_6_
  108.3 0.2 collective-permute-start.8
  108.4 0.0 collective-permute-done.11.refs_7_
  108.4 0.0 collective-permute-done.9.refs_5_
  108.4 1.7 %collective-permute-done.6.refs_1_ = bf16[200,256]{1,0:T(8,128)(2,1)S(1)} collective-permute-done((bf16[200,256]{1,0:T(8,128)(2,1)S(1)}, bf16[200,256]{1,0:T(8,128)(2,1)S(1)}, u32[]{:S(2)}, u32[]{:S(2)}) %collective-permute-start.6) | collective-permute-done | bytes 102432 | tf_op jit(solution)/shard_map/ppermute | solution.py:330
  110.1 2.5 %collective-permute-done.7.refs_2_ = bf16[200,256]{1,0:T(8,128)(2,1)S(1)} collective-permute-done((bf16[200,256]{1,0:T(8,128)(2,1)S(1)}, bf16[200,256]{1,0:T(8,128)(2,1)S(1)}, u32[]{:S(2)}, u32[]{:S(2)}) %collective-permute-start.7) | collective-permute-done | bytes 102432 | tf_op jit(solution)/shard_map/ppermute | solution.py:330
  112.6 0.3 collective-permute-done.8.refs_3_
  112.9 0.0 copy-done.1
  112.9 1.9 %place.1 = bf16[200,2048]{1,0:T(8,128)(2,1)} custom-call(s32[1]{0:T(128)} %bitcast.me_ref, bf16[200,256]{1,0:T(8,128)(2,1)} %copy-done.1, bf16[200,256]{1,0:T(8,128)(2,1)S(1)} %collective-permute-done.6.refs_1_, bf16[200,256]{1,0:T(8,128)(2,1)S(1)} %collective-permute-done.7.refs_2_, bf16[200,256]{1,0:T(8,128)(2,1)S(1)} %collective-permute-done.8.refs_3_, ...), custom_call_target="tpu_custom_call" | custom-call | tf_op jit(solution)/shard_map/place/pallas_call | solution.py:308
Async XLA Ops:
  4.5 42.9 %all-to-all-start = ((bf16[32,320,128]{2,1,0:T(8,128)(2,1)}), bf16[32,320,128]{2,1,0:T(8,128)(2,1)S(1)}, u32[]{:S(2)}, u32[]{:S(2)}) async-start(bf16[32,320,128]{2,1,0:T(8,128)(2,1)} %get-tuple-element.24), calls=%async_computation | async-start | bytes 5242880 | tf_op jit(solution)/shard_map/all_to_all | solution.py:333
  12.8 13.8 %collective-permute-start = (bf16[800,256]{1,0:T(8,128)(2,1)}, bf16[800,256]{1,0:T(8,128)(2,1)S(1)}, u32[]{:S(2)}, u32[]{:S(2)}) collective-permute-start(bf16[800,256]{1,0:T(8,128)(2,1)} %get-tuple-element.25), channel_id=1, source_target_pairs={{0,1},{1,2},{2,3},{3,0},{4,5},{5,6},{6,7},{7,4},{8,9},{9,10},{10,1... | collective-permute-start | bytes 1228808 | tf_op jit(solution)/shard_map/ppermute | solution.py:330
  14.4 20.4 %collective-permute-start.1 = (bf16[800,256]{1,0:T(8,128)(2,1)}, bf16[800,256]{1,0:T(8,128)(2,1)S(1)}, u32[]{:S(2)}, u32[]{:S(2)}) collective-permute-start(bf16[800,256]{1,0:T(8,128)(2,1)} %get-tuple-element.26), channel_id=1, source_target_pairs={{0,1},{1,2},{2,3},{3,0},{4,5},{5,6},{6,7},{7,4},{8,9},{9,10},{10,1... | collective-permute-start | bytes 1228808 | tf_op jit(solution)/shard_map/ppermute | solution.py:330
  15.9 28.8 %collective-permute-start.2 = (bf16[800,256]{1,0:T(8,128)(2,1)}, bf16[800,256]{1,0:T(8,128)(2,1)S(1)}, u32[]{:S(2)}, u32[]{:S(2)}) collective-permute-start(bf16[800,256]{1,0:T(8,128)(2,1)} %get-tuple-element.27), channel_id=1, source_target_pairs={{0,2},{1,3},{2,0},{3,1},{4,6},{5,7},{6,4},{7,5},{8,10},{9,11},{10,... | collective-permute-start | bytes 1228808 | tf_op jit(solution)/shard_map/ppermute | solution.py:330
  17.5 27.2 %collective-permute-start.3 = (bf16[800,256]{1,0:T(8,128)(2,1)}, bf16[800,256]{1,0:T(8,128)(2,1)S(1)}, u32[]{:S(2)}, u32[]{:S(2)}) collective-permute-start(bf16[800,256]{1,0:T(8,128)(2,1)} %get-tuple-element.28), channel_id=1, source_target_pairs={{0,3},{1,0},{2,1},{3,2},{4,7},{5,4},{6,5},{7,6},{8,11},{9,8},{10,9... | collective-permute-start | bytes 1228808 | tf_op jit(solution)/shard_map/ppermute | solution.py:330
  19.9 25.5 %collective-permute-start.4 = (bf16[800,256]{1,0:T(8,128)(2,1)}, bf16[800,256]{1,0:T(8,128)(2,1)}, u32[]{:S(2)}, u32[]{:S(2)}) collective-permute-start(bf16[800,256]{1,0:T(8,128)(2,1)} %get-tuple-element.29), channel_id=1, source_target_pairs={{0,3},{1,0},{2,1},{3,2},{4,7},{5,4},{6,5},{7,6},{8,11},{9,8},{10,9... | collective-permute-start | bytes 1228808 | tf_op jit(solution)/shard_map/ppermute | solution.py:330
  26.5 25.0 %copy-start.2 = (bf16[800,256]{1,0:T(8,128)(2,1)}, bf16[800,256]{1,0:T(8,128)(2,1)S(1)}, u32[]{:S(2)}) copy-start(bf16[800,256]{1,0:T(8,128)(2,1)S(1)} %collective-permute-done.refs_1_) | copy-start | bytes 1228804
  34.7 10.0 %copy-start.4 = (bf16[800,256]{1,0:T(8,128)(2,1)}, bf16[800,256]{1,0:T(8,128)(2,1)S(1)}, u32[]{:S(2)}) copy-start(bf16[800,256]{1,0:T(8,128)(2,1)S(1)} %collective-permute-done.1.refs_1_) | copy-start | bytes 1228804
  44.7 0.8 copy-start.5
  45.5 6.1 %copy-start.3 = (bf16[800,256]{1,0:T(8,128)(2,1)}, bf16[800,256]{1,0:T(8,128)(2,1)S(1)}, u32[]{:S(2)}) copy-start(bf16[800,256]{1,0:T(8,128)(2,1)S(1)} %collective-permute-done.3.refs_3_) | copy-start | bytes 1228804
  51.6 8.0 %copy-start.6 = (bf16[800,256]{1,0:T(8,128)(2,1)S(1)}, bf16[800,256]{1,0:T(8,128)(2,1)}, u32[]{:S(2)}) copy-start(bf16[800,256]{1,0:T(8,128)(2,1)} %get-tuple-element.32) | copy-start | bytes 1228804
  51.6 43.7 %all-to-all-start.1 = ((bf16[128,80,128]{2,1,0:T(8,128)(2,1)}), bf16[128,80,128]{2,1,0:T(8,128)(2,1)S(1)}, u32[]{:S(2)}, u32[]{:S(2)}) async-start(bf16[128,80,128]{2,1,0:T(8,128)(2,1)} %bitcast.16), calls=%async_computation.1 | async-start | bytes 5242880 | tf_op jit(solution)/shard_map/all_to_all | solution.py:346
  59.5 41.6 %collective-permute-start.5 = (bf16[800,256]{1,0:T(8,128)(2,1)S(1)}, bf16[800,256]{1,0:T(8,128)(2,1)S(1)}, u32[]{:S(2)}, u32[]{:S(2)}) collective-permute-start(bf16[800,256]{1,0:T(8,128)(2,1)S(1)} %copy-done.6), channel_id=1, source_target_pairs={{0,2},{1,3},{2,0},{3,1},{4,6},{5,7},{6,4},{7,5},{8,10},{9,11},{10,... | collective-permute-start | bytes 1228808 | tf_op jit(solution)/shard_map/ppermute | solution.py:330
  97.7 5.8 %copy-start = (bf16[200,256]{1,0:T(8,128)(2,1)}, bf16[200,256]{1,0:T(8,128)(2,1)S(1)}, u32[]{:S(2)}) copy-start(bf16[200,256]{1,0:T(8,128)(2,1)S(1)} %apply.3.refs_4_) | copy-start | bytes 307204
  97.7 10.6 %collective-permute-start.10 = (bf16[200,256]{1,0:T(8,128)(2,1)S(1)}, bf16[200,256]{1,0:T(8,128)(2,1)S(1)}, u32[]{:S(2)}, u32[]{:S(2)}) collective-permute-start(bf16[200,256]{1,0:T(8,128)(2,1)S(1)} %apply.3.refs_4_), channel_id=1, source_target_pairs={{0,2},{1,3},{2,0},{3,1},{4,6},{5,7},{6,4},{7,5},{8,10},{9,11},{10,... | collective-permute-start | bytes 307208 | tf_op jit(solution)/shard_map/ppermute | solution.py:330
  98.8 9.7 %collective-permute-start.11 = (bf16[200,256]{1,0:T(8,128)(2,1)S(1)}, bf16[200,256]{1,0:T(8,128)(2,1)S(1)}, u32[]{:S(2)}, u32[]{:S(2)}) collective-permute-start(bf16[200,256]{1,0:T(8,128)(2,1)S(1)} %apply.3.refs_4_), channel_id=1, source_target_pairs={{0,3},{1,0},{2,1},{3,2},{4,7},{5,4},{6,5},{7,6},{8,11},{9,8},{10,9... | collective-permute-start | bytes 307208 | tf_op jit(solution)/shard_map/ppermute | solution.py:330
  101.1 7.3 %collective-permute-start.9 = (bf16[200,256]{1,0:T(8,128)(2,1)S(1)}, bf16[200,256]{1,0:T(8,128)(2,1)S(1)}, u32[]{:S(2)}, u32[]{:S(2)}) collective-permute-start(bf16[200,256]{1,0:T(8,128)(2,1)S(1)} %apply.3.refs_4_), channel_id=1, source_target_pairs={{0,1},{1,2},{2,3},{3,0},{4,5},{5,6},{6,7},{7,4},{8,9},{9,10},{10,1... | collective-permute-start | bytes 307208 | tf_op jit(solution)/shard_map/ppermute | solution.py:330
  103.5 9.4 %copy-start.1 = (bf16[200,256]{1,0:T(8,128)(2,1)}, bf16[200,256]{1,0:T(8,128)(2,1)S(1)}, u32[]{:S(2)}) copy-start(bf16[200,256]{1,0:T(8,128)(2,1)S(1)} %apply.2.refs_0_) | copy-start | bytes 307204
  103.5 6.6 %collective-permute-start.6 = (bf16[200,256]{1,0:T(8,128)(2,1)S(1)}, bf16[200,256]{1,0:T(8,128)(2,1)S(1)}, u32[]{:S(2)}, u32[]{:S(2)}) collective-permute-start(bf16[200,256]{1,0:T(8,128)(2,1)S(1)} %apply.2.refs_0_), channel_id=1, source_target_pairs={{0,1},{1,2},{2,3},{3,0},{4,5},{5,6},{6,7},{7,4},{8,9},{9,10},{10,1... | collective-permute-start | bytes 307208 | tf_op jit(solution)/shard_map/ppermute | solution.py:330
  104.6 8.0 %collective-permute-start.7 = (bf16[200,256]{1,0:T(8,128)(2,1)S(1)}, bf16[200,256]{1,0:T(8,128)(2,1)S(1)}, u32[]{:S(2)}, u32[]{:S(2)}) collective-permute-start(bf16[200,256]{1,0:T(8,128)(2,1)S(1)} %apply.2.refs_0_), channel_id=1, source_target_pairs={{0,2},{1,3},{2,0},{3,1},{4,6},{5,7},{6,4},{7,5},{8,10},{9,11},{10,... | collective-permute-start | bytes 307208 | tf_op jit(solution)/shard_map/ppermute | solution.py:330
  108.3 4.7 %collective-permute-start.8 = (bf16[200,256]{1,0:T(8,128)(2,1)S(1)}, bf16[200,256]{1,0:T(8,128)(2,1)S(1)}, u32[]{:S(2)}, u32[]{:S(2)}) collective-permute-start(bf16[200,256]{1,0:T(8,128)(2,1)S(1)} %apply.2.refs_0_), channel_id=1, source_target_pairs={{0,3},{1,0},{2,1},{3,2},{4,7},{5,4},{6,5},{7,6},{8,11},{9,8},{10,9... | collective-permute-start | bytes 307208 | tf_op jit(solution)/shard_map/ppermute | solution.py:330

commit v5 on v4

--- a/solution.py
+++ b/solution.py
@@ -84,8 +84,8 @@
 
     def pass_on(d):
         copies = []
-        for a in range(keep if d else 0):
-            k = (d - 1) * keep + a
+        for a in range(keep):
+            k = d * keep + a
             cols = slice(a * BLOCK, (a + 1) * BLOCK)
             copies.append(pltpu.make_async_copy(f_ref.at[d, :, cols], f_out[k], f_sems.at[k]))
         return copies
@@ -132,7 +132,7 @@
     depth, rows = ft.shape
     blocks = rows // BLOCK
     width = rows // aux
-    count = (aux - 1) * (width // BLOCK)
+    count = aux * (width // BLOCK)
     hbm = pl.BlockSpec(memory_space=pltpu.HBM)
     shape = jax.ShapeDtypeStruct((ndev, blocks * per, LANES), BF16)
     piece = jax.ShapeDtypeStruct((depth, BLOCK), BF16)
@@ -235,22 +235,17 @@
     )(flag, low, high, g)
 
 
-def apply_kernel(per, a, count, me_ref, h_ref, *refs):
-    f_hbm, e_ref, f_ref, f_sems = refs[:count], *refs[count:]
+def apply_kernel(per, a, me_ref, h_ref, *refs):
+    f_refs, e_ref = refs[:-1], refs[-1]
     ndev, aux, height, lanes = h_ref.shape
     span = e_ref.shape[0]
-    depth = f_ref.shape[1]
+    depth = f_refs[0].shape[0]
     full = depth // LANES
     rest = depth - full * LANES
     fold = LANES // rest
     group = -(-span // (fold * 8)) * 8
     step = span // per
     rows = slice(a * per, (a + 1) * per)
-    start = pl.multiple_of((me_ref[0] * (height // per) + a) * BLOCK, BLOCK)
-    sources = [f_hbm[0].at[:, pl.ds(start, BLOCK)], *f_hbm[1:]]
-    copies = [pltpu.make_async_copy(sources[d], f_ref.at[d], f_sems.at[d]) for d in range(aux)]
-    for copy in copies:
-        copy.start()
     total = jnp.zeros((span, BLOCK), F32)
     for d in range(aux):
         h = lax.rem(me_ref[0] + aux - d, aux)
@@ -264,25 +259,17 @@
         last = [last[:, q * rest : (q + 1) * rest] for q in range(fold)]
         last = jnp.concatenate(last, axis=0)[:span].astype(BF16)
         left = jnp.concatenate(left + [last], axis=1)
-        copies[d].wait()
-        total += jnp.dot(left, f_ref[d], preferred_element_type=F32)
+        total += jnp.dot(left, f_refs[d][...], preferred_element_type=F32)
     e_ref[...] = total.astype(BF16)
 
 
-def apply(me, h, fs, spaces, a, span, per):
-    depth, width = fs[1].shape
-    aux = h.shape[1]
+def apply(me, h, fs, a, span, per):
     vmem = pl.BlockSpec(memory_space=pltpu.VMEM)
     return pl.pallas_call(
-        functools.partial(apply_kernel, per, a, len(fs)),
-        out_shape=pltpu.VMEM((span, width), BF16),
-        in_specs=[pl.BlockSpec(memory_space=pltpu.SMEM), vmem]
-        + [pl.BlockSpec(memory_space=space) for space in spaces],
+        functools.partial(apply_kernel, per, a),
+        out_shape=pltpu.VMEM((span, BLOCK), BF16),
+        in_specs=[pl.BlockSpec(memory_space=pltpu.SMEM)] + [vmem] * (1 + len(fs)),
         out_specs=vmem,
-        scratch_shapes=[
-            pltpu.VMEM((aux, depth, width), BF16),
-            pltpu.SemaphoreType.DMA((aux,)),
-        ],
         compiler_params=pltpu.CompilerParams(vmem_limit_bytes=VMEM),
         name="apply",
     )(me, h, *fs)
@@ -333,13 +320,13 @@
     got = lax.all_to_all(sent, "basis", split_axis=0, concat_axis=0, tiled=True)
     counts = pair_counts(block_slot, pair_list, pair_owner, blocks)
     far = aux // 2
-    fs = {(d, a): turn(pieces[(d - 1) * keep + a], d) for d in range(1, aux) for a in range(keep)}
+    fs = {(d, a): turn(pieces[d * keep + a], d) for d in range(1, aux) for a in range(keep)}
     early = {k: v for k, v in fs.items() if k != (far, 0)}
     got, early = lax.optimization_barrier((got, early))
     fs.update(early)
     spaces = {k: pltpu.HBM if k in early else pltpu.VMEM for k in fs}
     fs = {k: pltpu.with_memory_space_constraint(v, spaces[k]) for k, v in fs.items()}
-    fs.update({(0, a): ft for a in range(keep)})
+    fs.update({(0, a): pieces[a] for a in range(keep)})
     got = pltpu.with_memory_space_constraint(got, pltpu.VMEM)
     mixed = mix(counts, got, per)
     mixed = mixed.reshape(ndev * aux, -1, LANES)
@@ -348,8 +335,7 @@
     back = pltpu.with_memory_space_constraint(back, pltpu.VMEM)
     done = {}
     for a in range(keep):
-        kinds = [spaces.get((d, a), pltpu.HBM) for d in range(aux)]
-        mine = apply(me[None], back, [fs[d, a] for d in range(aux)], kinds, a, width, per)
+        mine = apply(me[None], back, [fs[d, a] for d in range(aux)], a, width, per)
         for d in range(1, aux):
             done[d, a] = pltpu.with_memory_space_constraint(turn(mine, d), pltpu.VMEM)
         done[0, a] = mine

time: 115 us -> 114 us (level)
  transfers between devices with their start and end apart: 14 -> 14, of which waited for: 8 -> 8; matrix products, arithmetic and copies ran while one was open for 0% -> 0% of each run, Pallas kernels for 8% -> 7%
where the time goes in v5:
time: 114 us
  waiting for transfers between devices  59.9 us (53%)
  starting transfers between devices  34.4 us (30%)
  Pallas kernels  18.8 us (16%)
    all_to_all x1, waiting for transfers between devices, shards(): lax.all_to_all(mixed, ('basis', 'aux'), split_axis=0, concat_axis=0, tile...  33.2 us
    ppermute x12, waiting for transfers between devices, turn(): return lax.ppermute(v, 'aux', [(k, (k + d) % aux) for k in range(aux)])  24.8 us
    ppermute x12, starting transfers between devices, turn(): return lax.ppermute(v, 'aux', [(k, (k + d) % aux) for k in range(aux)])  18.2 us
    all_to_all x1, starting transfers between devices, shards(): got = lax.all_to_all(sent, 'basis', split_axis=0, concat_axis=0, tiled=True)  8.25 us
    all_to_all x1, starting transfers between devices, shards(): lax.all_to_all(mixed, ('basis', 'aux'), split_axis=0, concat_axis=0, tile...  7.95 us
    pallas_call x1, Pallas kernels, pack(): pl.pallas_call(functools.partial(pack_kernel, per), out_shape=[shape] + [...  4.56 us
    pallas_call x1, Pallas kernels, pair_counts(): pl.pallas_call(functools.partial(count_kernel, keep), out_shape=(square,...  4.41 us
    pallas_call x1, Pallas kernels, mix(): pl.pallas_call(functools.partial(mix_kernel, per), out_shape=jax.ShapeDty...  4.02 us
  transfers between devices with their start and end apart: 14, of which 8 were waited for; matrix products, arithmetic and copies ran while one was open for 0% of the time, Pallas kernels for 7%

profile of v5, /device:TPU:0, one launch (start us, length us, event | category | flops | bytes accessed | tf_op | source)
XLA Modules:
  0.0 114.0 jit_solution(2373145295388280104)
XLA Ops:
  0.0 4.6 %pack.1 = (bf16[32,320,128]{2,1,0:T(8,128)(2,1)}, bf16[800,256]{1,0:T(8,128)(2,1)}, bf16[800,256]{1,0:T(8,128)(2,1)}, bf16[800,256]{1,0:T(8,128)(2,1)}, bf16[800...) custom-call(s32[1]{0:T(128)} %bitcast.me_ref, ...), custom_call_target="tpu_custom_call" | custom-call | tf_op jit(solution)/shard_map/pack/pallas_call | solution.py:139
  4.6 8.3 %all-to-all-start = ((bf16[32,320,128]{2,1,0:T(8,128)(2,1)}), bf16[32,320,128]{2,1,0:T(8,128)(2,1)S(1)}, u32[]{:S(2)}, u32[]{:S(2)}) async-start(bf16[32,320,128]{2,1,0:T(8,128)(2,1)} %get-tuple-element.26), calls=%async_computation | async-start | bytes 5242880 | tf_op jit(solution)/shard_map/all_to_all | solution.py:320
  12.8 1.6 %collective-permute-start = (bf16[800,256]{1,0:T(8,128)(2,1)}, bf16[800,256]{1,0:T(8,128)(2,1)S(1)}, u32[]{:S(2)}, u32[]{:S(2)}) collective-permute-start(bf16[800,256]{1,0:T(8,128)(2,1)} %get-tuple-element.27), channel_id=1, source_target_pairs={{0,1},{1,2},{2,3},{3,0},{4,5},{5,6},{6,7},{7,4},{8,9},{9,10},{10,1... | collective-permute-start | bytes 1228808 | tf_op jit(solution)/shard_map/ppermute | solution.py:317
  14.4 1.6 %collective-permute-start.1 = (bf16[800,256]{1,0:T(8,128)(2,1)}, bf16[800,256]{1,0:T(8,128)(2,1)S(1)}, u32[]{:S(2)}, u32[]{:S(2)}) collective-permute-start(bf16[800,256]{1,0:T(8,128)(2,1)} %get-tuple-element.28), channel_id=1, source_target_pairs={{0,1},{1,2},{2,3},{3,0},{4,5},{5,6},{6,7},{7,4},{8,9},{9,10},{10,1... | collective-permute-start | bytes 1228808 | tf_op jit(solution)/shard_map/ppermute | solution.py:317
  16.0 1.6 %collective-permute-start.2 = (bf16[800,256]{1,0:T(8,128)(2,1)}, bf16[800,256]{1,0:T(8,128)(2,1)S(1)}, u32[]{:S(2)}, u32[]{:S(2)}) collective-permute-start(bf16[800,256]{1,0:T(8,128)(2,1)} %get-tuple-element.29), channel_id=1, source_target_pairs={{0,2},{1,3},{2,0},{3,1},{4,6},{5,7},{6,4},{7,5},{8,10},{9,11},{10,... | collective-permute-start | bytes 1228808 | tf_op jit(solution)/shard_map/ppermute | solution.py:317
  17.6 2.4 %collective-permute-start.3 = (bf16[800,256]{1,0:T(8,128)(2,1)}, bf16[800,256]{1,0:T(8,128)(2,1)S(1)}, u32[]{:S(2)}, u32[]{:S(2)}) collective-permute-start(bf16[800,256]{1,0:T(8,128)(2,1)} %get-tuple-element.30), channel_id=1, source_target_pairs={{0,3},{1,0},{2,1},{3,2},{4,7},{5,4},{6,5},{7,6},{8,11},{9,8},{10,9... | collective-permute-start | bytes 1228808 | tf_op jit(solution)/shard_map/ppermute | solution.py:317
  20.0 0.1 collective-permute-start.4
  20.1 4.4 %pair_counts.1 = (bf16[256,256]{1,0:T(8,128)(2,1)}, bf16[256,256]{1,0:T(8,128)(2,1)}, s32[1]{0:T(128)}) custom-call(s32[1,256]{1,0:T(1,128)} %bitcast.18, s32[2,2048]{1,0:T(2,128)} %bitcast.16, s32[1,2048]{1,0:T(1,128)} %bitcast.17), custom_call_target="tpu_custom_call" | custom-call | tf_op jit(solution)/shard_map/pair_counts/pallas_call | solution.py:50
  24.5 2.1 %collective-permute-done.refs_1_ = bf16[800,256]{1,0:T(8,128)(2,1)S(1)} collective-permute-done((bf16[800,256]{1,0:T(8,128)(2,1)}, bf16[800,256]{1,0:T(8,128)(2,1)S(1)}, u32[]{:S(2)}, u32[]{:S(2)}) %collective-permute-start) | collective-permute-done | bytes 409632 | tf_op jit(solution)/shard_map/ppermute | solution.py:317
  26.6 0.0 copy-start.2
  26.6 8.2 %collective-permute-done.1.refs_1_ = bf16[800,256]{1,0:T(8,128)(2,1)S(1)} collective-permute-done((bf16[800,256]{1,0:T(8,128)(2,1)}, bf16[800,256]{1,0:T(8,128)(2,1)S(1)}, u32[]{:S(2)}, u32[]{:S(2)}) %collective-permute-start.1) | collective-permute-done | bytes 409632 | tf_op jit(solution)/shard_map/ppermute | solution.py:317
  34.8 0.0 copy-start.4
  34.8 10.0 %collective-permute-done.2.refs_2_ = bf16[800,256]{1,0:T(8,128)(2,1)S(1)} collective-permute-done((bf16[800,256]{1,0:T(8,128)(2,1)}, bf16[800,256]{1,0:T(8,128)(2,1)S(1)}, u32[]{:S(2)}, u32[]{:S(2)}) %collective-permute-start.2) | collective-permute-done | bytes 409632 | tf_op jit(solution)/shard_map/ppermute | solution.py:317
  44.8 0.0 copy-start.5
  44.8 0.0 collective-permute-done.3.refs_3_
  44.8 0.0 copy-done.4
  44.8 0.8 copy-done.5
  45.5 0.0 copy-start.3
  45.5 0.0 collective-permute-done.4.refs_3_
  45.5 1.9 %all-to-all-done.g_ref = bf16[32,320,128]{2,1,0:T(8,128)(2,1)S(1)} async-done(((bf16[32,320,128]{2,1,0:T(8,128)(2,1)}), bf16[32,320,128]{2,1,0:T(8,128)(2,1)S(1)}, u32[]{:S(2)}, u32[]{:S(2)}) %all-to-all-start) | async-done | bytes 2621472 | tf_op jit(solution)/shard_map/all_to_all | solution.py:320
  47.5 4.0 %mix.1 = bf16[32,320,128]{2,1,0:T(8,128)(2,1)} custom-call(s32[1]{0:T(128)} %get-tuple-element.23.flag_ref, bf16[256,256]{1,0:T(8,128)(2,1)} %get-tuple-element.24.low_hbm, bf16[256,256]{1,0:T(8,128)(2,1)} %get-tuple-element.25.high_hbm, bf16[32,320,128]{2,1,0:T(8,128)(2,1)S(1)} %all-to-all-done.g_ref), custom_call_target="tpu_custom_call" | custom-call | tf_op jit(solution)/shard_map/mix/pallas_call | solution.py:214
  51.5 0.0 copy-done.2
  51.5 0.0 copy-done.3
  51.5 0.0 copy-start.6
  51.5 7.9 %all-to-all-start.1 = ((bf16[128,80,128]{2,1,0:T(8,128)(2,1)}), bf16[128,80,128]{2,1,0:T(8,128)(2,1)S(1)}, u32[]{:S(2)}, u32[]{:S(2)}) async-start(bf16[128,80,128]{2,1,0:T(8,128)(2,1)} %bitcast.13), calls=%async_computation.1 | async-start | bytes 5242880 | tf_op jit(solution)/shard_map/all_to_all | solution.py:333
  59.5 0.0 copy-done.6
  59.5 2.5 %collective-permute-start.5 = (bf16[800,256]{1,0:T(8,128)(2,1)S(1)}, bf16[800,256]{1,0:T(8,128)(2,1)S(1)}, u32[]{:S(2)}, u32[]{:S(2)}) collective-permute-start(bf16[800,256]{1,0:T(8,128)(2,1)S(1)} %copy-done.6), channel_id=1, source_target_pairs={{0,2},{1,3},{2,0},{3,1},{4,6},{5,7},{6,4},{7,5},{8,10},{9,11},{10,... | collective-permute-start | bytes 1228808 | tf_op jit(solution)/shard_map/ppermute | solution.py:317
  62.0 33.2 %all-to-all-done.1 = bf16[128,80,128]{2,1,0:T(8,128)(2,1)S(1)} async-done(((bf16[128,80,128]{2,1,0:T(8,128)(2,1)}), bf16[128,80,128]{2,1,0:T(8,128)(2,1)S(1)}, u32[]{:S(2)}, u32[]{:S(2)}) %all-to-all-start.1) | async-done | bytes 2621472 | tf_op jit(solution)/shard_map/all_to_all | solution.py:333
  95.3 2.0 %apply.3.refs_4_ = bf16[200,256]{1,0:T(8,128)(2,1)S(1)} custom-call(s32[1]{0:T(128)} %bitcast.me_ref, bf16[32,4,80,128]{3,2,1,0:T(8,128)(2,1)S(1)} %bitcast.11, bf16[800,256]{1,0:T(8,128)(2,1)} %get-tuple-element.37.refs_0_, bf16[800,256]{1,0:T(8,128)(2,1)} %copy-done.4, bf16[800,256]{1,0:T(8,128)(2,1)} %copy-done.5, ...), custom_call_target="tpu_custom_call" | custom-call | tf_op jit(solution)/shard_map/apply/pallas_call | solution.py:268
  97.3 0.0 copy-start
  97.3 1.1 collective-permute-start.10
  98.4 2.4 %collective-permute-start.11 = (bf16[200,256]{1,0:T(8,128)(2,1)S(1)}, bf16[200,256]{1,0:T(8,128)(2,1)S(1)}, u32[]{:S(2)}, u32[]{:S(2)}) collective-permute-start(bf16[200,256]{1,0:T(8,128)(2,1)S(1)} %apply.3.refs_4_), channel_id=1, source_target_pairs={{0,3},{1,0},{2,1},{3,2},{4,7},{5,4},{6,5},{7,6},{8,11},{9,8},{10,9... | collective-permute-start | bytes 307208 | tf_op jit(solution)/shard_map/ppermute | solution.py:317
  100.7 0.0 collective-permute-start.9
  100.7 0.0 collective-permute-done.5.refs_2_
  100.7 1.9 %apply.2.refs_0_ = bf16[200,256]{1,0:T(8,128)(2,1)S(1)} custom-call(s32[1]{0:T(128)} %bitcast.me_ref, bf16[32,4,80,128]{3,2,1,0:T(8,128)(2,1)S(1)} %bitcast.12, bf16[800,256]{1,0:T(8,128)(2,1)} %get-tuple-element.33.refs_0_, bf16[800,256]{1,0:T(8,128)(2,1)} %copy-done.2, bf16[800,256]{1,0:T(8,128)(2,1)S(1)} %collective-permute-done.5.refs_2_, ...), custom_call_target="tpu_custom_call" | custom-call | tf_op jit(solution)/shard_map/apply/pallas_call | solution.py:268
  102.6 0.0 copy-start.1
  102.6 1.2 %collective-permute-start.6 = (bf16[200,256]{1,0:T(8,128)(2,1)S(1)}, bf16[200,256]{1,0:T(8,128)(2,1)S(1)}, u32[]{:S(2)}, u32[]{:S(2)}) collective-permute-start(bf16[200,256]{1,0:T(8,128)(2,1)S(1)} %apply.2.refs_0_), channel_id=1, source_target_pairs={{0,1},{1,2},{2,3},{3,0},{4,5},{5,6},{6,7},{7,4},{8,9},{9,10},{10,1... | collective-permute-start | bytes 307208 | tf_op jit(solution)/shard_map/ppermute | solution.py:317
  103.8 3.6 %collective-permute-start.7 = (bf16[200,256]{1,0:T(8,128)(2,1)S(1)}, bf16[200,256]{1,0:T(8,128)(2,1)S(1)}, u32[]{:S(2)}, u32[]{:S(2)}) collective-permute-start(bf16[200,256]{1,0:T(8,128)(2,1)S(1)} %apply.2.refs_0_), channel_id=1, source_target_pairs={{0,2},{1,3},{2,0},{3,1},{4,6},{5,7},{6,4},{7,5},{8,10},{9,11},{10,... | collective-permute-start | bytes 307208 | tf_op jit(solution)/shard_map/ppermute | solution.py:317
  107.4 0.0 collective-permute-done.10.refs_6_
  107.4 0.1 collective-permute-start.8
  107.5 0.0 collective-permute-done.11.refs_7_
  107.5 0.0 collective-permute-done.9.refs_5_
  107.6 2.1 %collective-permute-done.6.refs_1_ = bf16[200,256]{1,0:T(8,128)(2,1)S(1)} collective-permute-done((bf16[200,256]{1,0:T(8,128)(2,1)S(1)}, bf16[200,256]{1,0:T(8,128)(2,1)S(1)}, u32[]{:S(2)}, u32[]{:S(2)}) %collective-permute-start.6) | collective-permute-done | bytes 102432 | tf_op jit(solution)/shard_map/ppermute | solution.py:317
  109.7 2.1 %collective-permute-done.7.refs_2_ = bf16[200,256]{1,0:T(8,128)(2,1)S(1)} collective-permute-done((bf16[200,256]{1,0:T(8,128)(2,1)S(1)}, bf16[200,256]{1,0:T(8,128)(2,1)S(1)}, u32[]{:S(2)}, u32[]{:S(2)}) %collective-permute-start.7) | collective-permute-done | bytes 102432 | tf_op jit(solution)/shard_map/ppermute | solution.py:317
  111.7 0.3 collective-permute-done.8.refs_3_
  112.1 0.0 copy-done
  112.1 0.0 copy-done.1
  112.1 1.9 %place.1 = bf16[200,2048]{1,0:T(8,128)(2,1)} custom-call(s32[1]{0:T(128)} %bitcast.me_ref, bf16[200,256]{1,0:T(8,128)(2,1)} %copy-done.1, bf16[200,256]{1,0:T(8,128)(2,1)S(1)} %collective-permute-done.6.refs_1_, bf16[200,256]{1,0:T(8,128)(2,1)S(1)} %collective-permute-done.7.refs_2_, bf16[200,256]{1,0:T(8,128)(2,1)S(1)} %collective-permute-done.8.refs_3_, ...), custom_call_target="tpu_custom_call" | custom-call | tf_op jit(solution)/shard_map/place/pallas_call | solution.py:295
Async XLA Ops:
  4.6 42.9 %all-to-all-start = ((bf16[32,320,128]{2,1,0:T(8,128)(2,1)}), bf16[32,320,128]{2,1,0:T(8,128)(2,1)S(1)}, u32[]{:S(2)}, u32[]{:S(2)}) async-start(bf16[32,320,128]{2,1,0:T(8,128)(2,1)} %get-tuple-element.26), calls=%async_computation | async-start | bytes 5242880 | tf_op jit(solution)/shard_map/all_to_all | solution.py:320
  12.8 13.8 %collective-permute-start = (bf16[800,256]{1,0:T(8,128)(2,1)}, bf16[800,256]{1,0:T(8,128)(2,1)S(1)}, u32[]{:S(2)}, u32[]{:S(2)}) collective-permute-start(bf16[800,256]{1,0:T(8,128)(2,1)} %get-tuple-element.27), channel_id=1, source_target_pairs={{0,1},{1,2},{2,3},{3,0},{4,5},{5,6},{6,7},{7,4},{8,9},{9,10},{10,1... | collective-permute-start | bytes 1228808 | tf_op jit(solution)/shard_map/ppermute | solution.py:317
  14.4 20.4 %collective-permute-start.1 = (bf16[800,256]{1,0:T(8,128)(2,1)}, bf16[800,256]{1,0:T(8,128)(2,1)S(1)}, u32[]{:S(2)}, u32[]{:S(2)}) collective-permute-start(bf16[800,256]{1,0:T(8,128)(2,1)} %get-tuple-element.28), channel_id=1, source_target_pairs={{0,1},{1,2},{2,3},{3,0},{4,5},{5,6},{6,7},{7,4},{8,9},{9,10},{10,1... | collective-permute-start | bytes 1228808 | tf_op jit(solution)/shard_map/ppermute | solution.py:317
  16.0 28.7 %collective-permute-start.2 = (bf16[800,256]{1,0:T(8,128)(2,1)}, bf16[800,256]{1,0:T(8,128)(2,1)S(1)}, u32[]{:S(2)}, u32[]{:S(2)}) collective-permute-start(bf16[800,256]{1,0:T(8,128)(2,1)} %get-tuple-element.29), channel_id=1, source_target_pairs={{0,2},{1,3},{2,0},{3,1},{4,6},{5,7},{6,4},{7,5},{8,10},{9,11},{10,... | collective-permute-start | bytes 1228808 | tf_op jit(solution)/shard_map/ppermute | solution.py:317
  17.6 27.2 %collective-permute-start.3 = (bf16[800,256]{1,0:T(8,128)(2,1)}, bf16[800,256]{1,0:T(8,128)(2,1)S(1)}, u32[]{:S(2)}, u32[]{:S(2)}) collective-permute-start(bf16[800,256]{1,0:T(8,128)(2,1)} %get-tuple-element.30), channel_id=1, source_target_pairs={{0,3},{1,0},{2,1},{3,2},{4,7},{5,4},{6,5},{7,6},{8,11},{9,8},{10,9... | collective-permute-start | bytes 1228808 | tf_op jit(solution)/shard_map/ppermute | solution.py:317
  20.0 25.5 %collective-permute-start.4 = (bf16[800,256]{1,0:T(8,128)(2,1)}, bf16[800,256]{1,0:T(8,128)(2,1)}, u32[]{:S(2)}, u32[]{:S(2)}) collective-permute-start(bf16[800,256]{1,0:T(8,128)(2,1)} %get-tuple-element.31), channel_id=1, source_target_pairs={{0,3},{1,0},{2,1},{3,2},{4,7},{5,4},{6,5},{7,6},{8,11},{9,8},{10,9... | collective-permute-start | bytes 1228808 | tf_op jit(solution)/shard_map/ppermute | solution.py:317
  26.6 24.9 %copy-start.2 = (bf16[800,256]{1,0:T(8,128)(2,1)}, bf16[800,256]{1,0:T(8,128)(2,1)S(1)}, u32[]{:S(2)}) copy-start(bf16[800,256]{1,0:T(8,128)(2,1)S(1)} %collective-permute-done.refs_1_) | copy-start | bytes 1228804
  34.8 10.0 %copy-start.4 = (bf16[800,256]{1,0:T(8,128)(2,1)}, bf16[800,256]{1,0:T(8,128)(2,1)S(1)}, u32[]{:S(2)}) copy-start(bf16[800,256]{1,0:T(8,128)(2,1)S(1)} %collective-permute-done.1.refs_1_) | copy-start | bytes 1228804
  44.8 0.8 copy-start.5
  45.5 6.0 %copy-start.3 = (bf16[800,256]{1,0:T(8,128)(2,1)}, bf16[800,256]{1,0:T(8,128)(2,1)S(1)}, u32[]{:S(2)}) copy-start(bf16[800,256]{1,0:T(8,128)(2,1)S(1)} %collective-permute-done.3.refs_3_) | copy-start | bytes 1228804
  51.5 8.0 %copy-start.6 = (bf16[800,256]{1,0:T(8,128)(2,1)S(1)}, bf16[800,256]{1,0:T(8,128)(2,1)}, u32[]{:S(2)}) copy-start(bf16[800,256]{1,0:T(8,128)(2,1)} %get-tuple-element.35) | copy-start | bytes 1228804
  51.5 43.7 %all-to-all-start.1 = ((bf16[128,80,128]{2,1,0:T(8,128)(2,1)}), bf16[128,80,128]{2,1,0:T(8,128)(2,1)S(1)}, u32[]{:S(2)}, u32[]{:S(2)}) async-start(bf16[128,80,128]{2,1,0:T(8,128)(2,1)} %bitcast.13), calls=%async_computation.1 | async-start | bytes 5242880 | tf_op jit(solution)/shard_map/all_to_all | solution.py:333
  59.5 41.2 %collective-permute-start.5 = (bf16[800,256]{1,0:T(8,128)(2,1)S(1)}, bf16[800,256]{1,0:T(8,128)(2,1)S(1)}, u32[]{:S(2)}, u32[]{:S(2)}) collective-permute-start(bf16[800,256]{1,0:T(8,128)(2,1)S(1)} %copy-done.6), channel_id=1, source_target_pairs={{0,2},{1,3},{2,0},{3,1},{4,6},{5,7},{6,4},{7,5},{8,10},{9,11},{10,... | collective-permute-start | bytes 1228808 | tf_op jit(solution)/shard_map/ppermute | solution.py:317
  97.3 14.8 %copy-start = (bf16[200,256]{1,0:T(8,128)(2,1)}, bf16[200,256]{1,0:T(8,128)(2,1)S(1)}, u32[]{:S(2)}) copy-start(bf16[200,256]{1,0:T(8,128)(2,1)S(1)} %apply.3.refs_4_) | copy-start | bytes 307204
  97.3 10.1 %collective-permute-start.10 = (bf16[200,256]{1,0:T(8,128)(2,1)S(1)}, bf16[200,256]{1,0:T(8,128)(2,1)S(1)}, u32[]{:S(2)}, u32[]{:S(2)}) collective-permute-start(bf16[200,256]{1,0:T(8,128)(2,1)S(1)} %apply.3.refs_4_), channel_id=1, source_target_pairs={{0,2},{1,3},{2,0},{3,1},{4,6},{5,7},{6,4},{7,5},{8,10},{9,11},{10,... | collective-permute-start | bytes 307208 | tf_op jit(solution)/shard_map/ppermute | solution.py:317
  98.4 9.2 %collective-permute-start.11 = (bf16[200,256]{1,0:T(8,128)(2,1)S(1)}, bf16[200,256]{1,0:T(8,128)(2,1)S(1)}, u32[]{:S(2)}, u32[]{:S(2)}) collective-permute-start(bf16[200,256]{1,0:T(8,128)(2,1)S(1)} %apply.3.refs_4_), channel_id=1, source_target_pairs={{0,3},{1,0},{2,1},{3,2},{4,7},{5,4},{6,5},{7,6},{8,11},{9,8},{10,9... | collective-permute-start | bytes 307208 | tf_op jit(solution)/shard_map/ppermute | solution.py:317
  100.7 6.8 %collective-permute-start.9 = (bf16[200,256]{1,0:T(8,128)(2,1)S(1)}, bf16[200,256]{1,0:T(8,128)(2,1)S(1)}, u32[]{:S(2)}, u32[]{:S(2)}) collective-permute-start(bf16[200,256]{1,0:T(8,128)(2,1)S(1)} %apply.3.refs_4_), channel_id=1, source_target_pairs={{0,1},{1,2},{2,3},{3,0},{4,5},{5,6},{6,7},{7,4},{8,9},{9,10},{10,1... | collective-permute-start | bytes 307208 | tf_op jit(solution)/shard_map/ppermute | solution.py:317
  102.6 9.4 %copy-start.1 = (bf16[200,256]{1,0:T(8,128)(2,1)}, bf16[200,256]{1,0:T(8,128)(2,1)S(1)}, u32[]{:S(2)}) copy-start(bf16[200,256]{1,0:T(8,128)(2,1)S(1)} %apply.2.refs_0_) | copy-start | bytes 307204
  102.6 7.0 %collective-permute-start.6 = (bf16[200,256]{1,0:T(8,128)(2,1)S(1)}, bf16[200,256]{1,0:T(8,128)(2,1)S(1)}, u32[]{:S(2)}, u32[]{:S(2)}) collective-permute-start(bf16[200,256]{1,0:T(8,128)(2,1)S(1)} %apply.2.refs_0_), channel_id=1, source_target_pairs={{0,1},{1,2},{2,3},{3,0},{4,5},{5,6},{6,7},{7,4},{8,9},{9,10},{10,1... | collective-permute-start | bytes 307208 | tf_op jit(solution)/shard_map/ppermute | solution.py:317
  103.8 8.0 %collective-permute-start.7 = (bf16[200,256]{1,0:T(8,128)(2,1)S(1)}, bf16[200,256]{1,0:T(8,128)(2,1)S(1)}, u32[]{:S(2)}, u32[]{:S(2)}) collective-permute-start(bf16[200,256]{1,0:T(8,128)(2,1)S(1)} %apply.2.refs_0_), channel_id=1, source_target_pairs={{0,2},{1,3},{2,0},{3,1},{4,6},{5,7},{6,4},{7,5},{8,10},{9,11},{10,... | collective-permute-start | bytes 307208 | tf_op jit(solution)/shard_map/ppermute | solution.py:317
  107.4 4.7 %collective-permute-start.8 = (bf16[200,256]{1,0:T(8,128)(2,1)S(1)}, bf16[200,256]{1,0:T(8,128)(2,1)S(1)}, u32[]{:S(2)}, u32[]{:S(2)}) collective-permute-start(bf16[200,256]{1,0:T(8,128)(2,1)S(1)} %apply.2.refs_0_), channel_id=1, source_target_pairs={{0,3},{1,0},{2,1},{3,2},{4,7},{5,4},{6,5},{7,6},{8,11},{9,8},{10,9... | collective-permute-start | bytes 307208 | tf_op jit(solution)/shard_map/ppermute | solution.py:317

commit v6 on v5

--- a/solution.py
+++ b/solution.py
@@ -228,7 +228,7 @@
             pltpu.VMEM((ndev * (height + 1), lanes), F32),
             pltpu.VMEM(g.shape, BF16),
             pltpu.SemaphoreType.DMA((2,)),
-            pltpu.SemaphoreType.DMA((8,)),
+            pltpu.SemaphoreType.DMA((4,)),
         ],
         compiler_params=pltpu.CompilerParams(vmem_limit_bytes=VMEM),
         name="mix",

time: 114 us -> 114 us (level)
  no operation moved by 1% of the time
where the time goes in v6:
time: 114 us
  waiting for transfers between devices  59.9 us (53%)
  starting transfers between devices  34.4 us (30%)
  Pallas kernels  18.8 us (16%)
    all_to_all x1, waiting for transfers between devices, shards(): lax.all_to_all(mixed, ('basis', 'aux'), split_axis=0, concat_axis=0, tile...  33.2 us
    ppermute x12, waiting for transfers between devices, turn(): return lax.ppermute(v, 'aux', [(k, (k + d) % aux) for k in range(aux)])  24.7 us
    ppermute x12, starting transfers between devices, turn(): return lax.ppermute(v, 'aux', [(k, (k + d) % aux) for k in range(aux)])  18.2 us
    all_to_all x1, starting transfers between devices, shards(): got = lax.all_to_all(sent, 'basis', split_axis=0, concat_axis=0, tiled=True)  8.25 us
    all_to_all x1, starting transfers between devices, shards(): lax.all_to_all(mixed, ('basis', 'aux'), split_axis=0, concat_axis=0, tile...  7.95 us
    pallas_call x1, Pallas kernels, pack(): pl.pallas_call(functools.partial(pack_kernel, per), out_shape=[shape] + [...  4.56 us
    pallas_call x1, Pallas kernels, pair_counts(): pl.pallas_call(functools.partial(count_kernel, keep), out_shape=(square,...  4.41 us
    pallas_call x1, Pallas kernels, mix(): pl.pallas_call(functools.partial(mix_kernel, per), out_shape=jax.ShapeDty...  4.02 us
  transfers between devices with their start and end apart: 14, of which 8 were waited for; matrix products, arithmetic and copies ran while one was open for 0% of the time, Pallas kernels for 7%

profile of v6, /device:TPU:0, one launch (start us, length us, event | category | flops | bytes accessed | tf_op | source)
XLA Modules:
  0.0 114.0 jit_solution(8105759992162115220)
XLA Ops:
  0.0 4.6 %pack.1 = (bf16[32,320,128]{2,1,0:T(8,128)(2,1)}, bf16[800,256]{1,0:T(8,128)(2,1)}, bf16[800,256]{1,0:T(8,128)(2,1)}, bf16[800,256]{1,0:T(8,128)(2,1)}, bf16[800...) custom-call(s32[1]{0:T(128)} %bitcast.me_ref, ...), custom_call_target="tpu_custom_call" | custom-call | tf_op jit(solution)/shard_map/pack/pallas_call | solution.py:139
  4.6 8.3 %all-to-all-start = ((bf16[32,320,128]{2,1,0:T(8,128)(2,1)}), bf16[32,320,128]{2,1,0:T(8,128)(2,1)S(1)}, u32[]{:S(2)}, u32[]{:S(2)}) async-start(bf16[32,320,128]{2,1,0:T(8,128)(2,1)} %get-tuple-element.26), calls=%async_computation | async-start | bytes 5242880 | tf_op jit(solution)/shard_map/all_to_all | solution.py:320
  12.8 1.6 %collective-permute-start = (bf16[800,256]{1,0:T(8,128)(2,1)}, bf16[800,256]{1,0:T(8,128)(2,1)S(1)}, u32[]{:S(2)}, u32[]{:S(2)}) collective-permute-start(bf16[800,256]{1,0:T(8,128)(2,1)} %get-tuple-element.27), channel_id=1, source_target_pairs={{0,1},{1,2},{2,3},{3,0},{4,5},{5,6},{6,7},{7,4},{8,9},{9,10},{10,1... | collective-permute-start | bytes 1228808 | tf_op jit(solution)/shard_map/ppermute | solution.py:317
  14.4 1.6 %collective-permute-start.1 = (bf16[800,256]{1,0:T(8,128)(2,1)}, bf16[800,256]{1,0:T(8,128)(2,1)S(1)}, u32[]{:S(2)}, u32[]{:S(2)}) collective-permute-start(bf16[800,256]{1,0:T(8,128)(2,1)} %get-tuple-element.28), channel_id=1, source_target_pairs={{0,1},{1,2},{2,3},{3,0},{4,5},{5,6},{6,7},{7,4},{8,9},{9,10},{10,1... | collective-permute-start | bytes 1228808 | tf_op jit(solution)/shard_map/ppermute | solution.py:317
  16.0 1.6 %collective-permute-start.2 = (bf16[800,256]{1,0:T(8,128)(2,1)}, bf16[800,256]{1,0:T(8,128)(2,1)S(1)}, u32[]{:S(2)}, u32[]{:S(2)}) collective-permute-start(bf16[800,256]{1,0:T(8,128)(2,1)} %get-tuple-element.29), channel_id=1, source_target_pairs={{0,2},{1,3},{2,0},{3,1},{4,6},{5,7},{6,4},{7,5},{8,10},{9,11},{10,... | collective-permute-start | bytes 1228808 | tf_op jit(solution)/shard_map/ppermute | solution.py:317
  17.6 2.4 %collective-permute-start.3 = (bf16[800,256]{1,0:T(8,128)(2,1)}, bf16[800,256]{1,0:T(8,128)(2,1)S(1)}, u32[]{:S(2)}, u32[]{:S(2)}) collective-permute-start(bf16[800,256]{1,0:T(8,128)(2,1)} %get-tuple-element.30), channel_id=1, source_target_pairs={{0,3},{1,0},{2,1},{3,2},{4,7},{5,4},{6,5},{7,6},{8,11},{9,8},{10,9... | collective-permute-start | bytes 1228808 | tf_op jit(solution)/shard_map/ppermute | solution.py:317
  20.0 0.1 collective-permute-start.4
  20.1 4.4 %pair_counts.1 = (bf16[256,256]{1,0:T(8,128)(2,1)}, bf16[256,256]{1,0:T(8,128)(2,1)}, s32[1]{0:T(128)}) custom-call(s32[1,256]{1,0:T(1,128)} %bitcast.18, s32[2,2048]{1,0:T(2,128)} %bitcast.16, s32[1,2048]{1,0:T(1,128)} %bitcast.17), custom_call_target="tpu_custom_call" | custom-call | tf_op jit(solution)/shard_map/pair_counts/pallas_call | solution.py:50
  24.5 2.1 %collective-permute-done.refs_1_ = bf16[800,256]{1,0:T(8,128)(2,1)S(1)} collective-permute-done((bf16[800,256]{1,0:T(8,128)(2,1)}, bf16[800,256]{1,0:T(8,128)(2,1)S(1)}, u32[]{:S(2)}, u32[]{:S(2)}) %collective-permute-start) | collective-permute-done | bytes 409632 | tf_op jit(solution)/shard_map/ppermute | solution.py:317
  26.6 0.0 copy-start.2
  26.6 8.2 %collective-permute-done.1.refs_1_ = bf16[800,256]{1,0:T(8,128)(2,1)S(1)} collective-permute-done((bf16[800,256]{1,0:T(8,128)(2,1)}, bf16[800,256]{1,0:T(8,128)(2,1)S(1)}, u32[]{:S(2)}, u32[]{:S(2)}) %collective-permute-start.1) | collective-permute-done | bytes 409632 | tf_op jit(solution)/shard_map/ppermute | solution.py:317
  34.8 0.0 copy-start.4
  34.8 10.0 %collective-permute-done.2.refs_2_ = bf16[800,256]{1,0:T(8,128)(2,1)S(1)} collective-permute-done((bf16[800,256]{1,0:T(8,128)(2,1)}, bf16[800,256]{1,0:T(8,128)(2,1)S(1)}, u32[]{:S(2)}, u32[]{:S(2)}) %collective-permute-start.2) | collective-permute-done | bytes 409632 | tf_op jit(solution)/shard_map/ppermute | solution.py:317
  44.8 0.0 copy-start.5
  44.8 0.0 collective-permute-done.3.refs_3_
  44.8 0.0 copy-done.4
  44.8 0.8 copy-done.5
  45.5 0.0 copy-start.3
  45.5 0.0 collective-permute-done.4.refs_3_
  45.5 1.9 %all-to-all-done.g_ref = bf16[32,320,128]{2,1,0:T(8,128)(2,1)S(1)} async-done(((bf16[32,320,128]{2,1,0:T(8,128)(2,1)}), bf16[32,320,128]{2,1,0:T(8,128)(2,1)S(1)}, u32[]{:S(2)}, u32[]{:S(2)}) %all-to-all-start) | async-done | bytes 2621472 | tf_op jit(solution)/shard_map/all_to_all | solution.py:320
  47.5 4.0 %mix.1 = bf16[32,320,128]{2,1,0:T(8,128)(2,1)} custom-call(s32[1]{0:T(128)} %get-tuple-element.23.flag_ref, bf16[256,256]{1,0:T(8,128)(2,1)} %get-tuple-element.24.low_hbm, bf16[256,256]{1,0:T(8,128)(2,1)} %get-tuple-element.25.high_hbm, bf16[32,320,128]{2,1,0:T(8,128)(2,1)S(1)} %all-to-all-done.g_ref), custom_call_target="tpu_custom_call" | custom-call | tf_op jit(solution)/shard_map/mix/pallas_call | solution.py:214
  51.5 0.0 copy-done.2
  51.5 0.0 copy-done.3
  51.5 0.0 copy-start.6
  51.5 7.9 %all-to-all-start.1 = ((bf16[128,80,128]{2,1,0:T(8,128)(2,1)}), bf16[128,80,128]{2,1,0:T(8,128)(2,1)S(1)}, u32[]{:S(2)}, u32[]{:S(2)}) async-start(bf16[128,80,128]{2,1,0:T(8,128)(2,1)} %bitcast.13), calls=%async_computation.1 | async-start | bytes 5242880 | tf_op jit(solution)/shard_map/all_to_all | solution.py:333
  59.5 0.0 copy-done.6
  59.5 2.5 %collective-permute-start.5 = (bf16[800,256]{1,0:T(8,128)(2,1)S(1)}, bf16[800,256]{1,0:T(8,128)(2,1)S(1)}, u32[]{:S(2)}, u32[]{:S(2)}) collective-permute-start(bf16[800,256]{1,0:T(8,128)(2,1)S(1)} %copy-done.6), channel_id=1, source_target_pairs={{0,2},{1,3},{2,0},{3,1},{4,6},{5,7},{6,4},{7,5},{8,10},{9,11},{10,... | collective-permute-start | bytes 1228808 | tf_op jit(solution)/shard_map/ppermute | solution.py:317
  62.0 33.2 %all-to-all-done.1 = bf16[128,80,128]{2,1,0:T(8,128)(2,1)S(1)} async-done(((bf16[128,80,128]{2,1,0:T(8,128)(2,1)}), bf16[128,80,128]{2,1,0:T(8,128)(2,1)S(1)}, u32[]{:S(2)}, u32[]{:S(2)}) %all-to-all-start.1) | async-done | bytes 2621472 | tf_op jit(solution)/shard_map/all_to_all | solution.py:333
  95.3 2.0 %apply.3.refs_4_ = bf16[200,256]{1,0:T(8,128)(2,1)S(1)} custom-call(s32[1]{0:T(128)} %bitcast.me_ref, bf16[32,4,80,128]{3,2,1,0:T(8,128)(2,1)S(1)} %bitcast.11, bf16[800,256]{1,0:T(8,128)(2,1)} %get-tuple-element.37.refs_0_, bf16[800,256]{1,0:T(8,128)(2,1)} %copy-done.4, bf16[800,256]{1,0:T(8,128)(2,1)} %copy-done.5, ...), custom_call_target="tpu_custom_call" | custom-call | tf_op jit(solution)/shard_map/apply/pallas_call | solution.py:268
  97.3 0.0 copy-start
  97.3 1.1 collective-permute-start.10
  98.4 2.4 %collective-permute-start.11 = (bf16[200,256]{1,0:T(8,128)(2,1)S(1)}, bf16[200,256]{1,0:T(8,128)(2,1)S(1)}, u32[]{:S(2)}, u32[]{:S(2)}) collective-permute-start(bf16[200,256]{1,0:T(8,128)(2,1)S(1)} %apply.3.refs_4_), channel_id=1, source_target_pairs={{0,3},{1,0},{2,1},{3,2},{4,7},{5,4},{6,5},{7,6},{8,11},{9,8},{10,9... | collective-permute-start | bytes 307208 | tf_op jit(solution)/shard_map/ppermute | solution.py:317
  100.7 0.0 collective-permute-start.9
  100.7 0.0 collective-permute-done.5.refs_2_
  100.7 1.9 %apply.2.refs_0_ = bf16[200,256]{1,0:T(8,128)(2,1)S(1)} custom-call(s32[1]{0:T(128)} %bitcast.me_ref, bf16[32,4,80,128]{3,2,1,0:T(8,128)(2,1)S(1)} %bitcast.12, bf16[800,256]{1,0:T(8,128)(2,1)} %get-tuple-element.33.refs_0_, bf16[800,256]{1,0:T(8,128)(2,1)} %copy-done.2, bf16[800,256]{1,0:T(8,128)(2,1)S(1)} %collective-permute-done.5.refs_2_, ...), custom_call_target="tpu_custom_call" | custom-call | tf_op jit(solution)/shard_map/apply/pallas_call | solution.py:268
  102.6 0.0 copy-start.1
  102.6 1.2 %collective-permute-start.6 = (bf16[200,256]{1,0:T(8,128)(2,1)S(1)}, bf16[200,256]{1,0:T(8,128)(2,1)S(1)}, u32[]{:S(2)}, u32[]{:S(2)}) collective-permute-start(bf16[200,256]{1,0:T(8,128)(2,1)S(1)} %apply.2.refs_0_), channel_id=1, source_target_pairs={{0,1},{1,2},{2,3},{3,0},{4,5},{5,6},{6,7},{7,4},{8,9},{9,10},{10,1... | collective-permute-start | bytes 307208 | tf_op jit(solution)/shard_map/ppermute | solution.py:317
  103.8 3.6 %collective-permute-start.7 = (bf16[200,256]{1,0:T(8,128)(2,1)S(1)}, bf16[200,256]{1,0:T(8,128)(2,1)S(1)}, u32[]{:S(2)}, u32[]{:S(2)}) collective-permute-start(bf16[200,256]{1,0:T(8,128)(2,1)S(1)} %apply.2.refs_0_), channel_id=1, source_target_pairs={{0,2},{1,3},{2,0},{3,1},{4,6},{5,7},{6,4},{7,5},{8,10},{9,11},{10,... | collective-permute-start | bytes 307208 | tf_op jit(solution)/shard_map/ppermute | solution.py:317
  107.4 0.0 collective-permute-done.10.refs_6_
  107.4 0.2 collective-permute-start.8
  107.5 0.0 collective-permute-done.11.refs_7_
  107.5 0.0 collective-permute-done.9.refs_5_
  107.6 2.1 %collective-permute-done.6.refs_1_ = bf16[200,256]{1,0:T(8,128)(2,1)S(1)} collective-permute-done((bf16[200,256]{1,0:T(8,128)(2,1)S(1)}, bf16[200,256]{1,0:T(8,128)(2,1)S(1)}, u32[]{:S(2)}, u32[]{:S(2)}) %collective-permute-start.6) | collective-permute-done | bytes 102432 | tf_op jit(solution)/shard_map/ppermute | solution.py:317
  109.7 2.1 %collective-permute-done.7.refs_2_ = bf16[200,256]{1,0:T(8,128)(2,1)S(1)} collective-permute-done((bf16[200,256]{1,0:T(8,128)(2,1)S(1)}, bf16[200,256]{1,0:T(8,128)(2,1)S(1)}, u32[]{:S(2)}, u32[]{:S(2)}) %collective-permute-start.7) | collective-permute-done | bytes 102432 | tf_op jit(solution)/shard_map/ppermute | solution.py:317
  111.7 0.3 collective-permute-done.8.refs_3_
  112.1 0.0 copy-done
  112.1 0.0 copy-done.1
  112.1 1.9 %place.1 = bf16[200,2048]{1,0:T(8,128)(2,1)} custom-call(s32[1]{0:T(128)} %bitcast.me_ref, bf16[200,256]{1,0:T(8,128)(2,1)} %copy-done.1, bf16[200,256]{1,0:T(8,128)(2,1)S(1)} %collective-permute-done.6.refs_1_, bf16[200,256]{1,0:T(8,128)(2,1)S(1)} %collective-permute-done.7.refs_2_, bf16[200,256]{1,0:T(8,128)(2,1)S(1)} %collective-permute-done.8.refs_3_, ...), custom_call_target="tpu_custom_call" | custom-call | tf_op jit(solution)/shard_map/place/pallas_call | solution.py:295
Async XLA Ops:
  4.6 42.9 %all-to-all-start = ((bf16[32,320,128]{2,1,0:T(8,128)(2,1)}), bf16[32,320,128]{2,1,0:T(8,128)(2,1)S(1)}, u32[]{:S(2)}, u32[]{:S(2)}) async-start(bf16[32,320,128]{2,1,0:T(8,128)(2,1)} %get-tuple-element.26), calls=%async_computation | async-start | bytes 5242880 | tf_op jit(solution)/shard_map/all_to_all | solution.py:320
  12.8 13.8 %collective-permute-start = (bf16[800,256]{1,0:T(8,128)(2,1)}, bf16[800,256]{1,0:T(8,128)(2,1)S(1)}, u32[]{:S(2)}, u32[]{:S(2)}) collective-permute-start(bf16[800,256]{1,0:T(8,128)(2,1)} %get-tuple-element.27), channel_id=1, source_target_pairs={{0,1},{1,2},{2,3},{3,0},{4,5},{5,6},{6,7},{7,4},{8,9},{9,10},{10,1... | collective-permute-start | bytes 1228808 | tf_op jit(solution)/shard_map/ppermute | solution.py:317
  14.4 20.4 %collective-permute-start.1 = (bf16[800,256]{1,0:T(8,128)(2,1)}, bf16[800,256]{1,0:T(8,128)(2,1)S(1)}, u32[]{:S(2)}, u32[]{:S(2)}) collective-permute-start(bf16[800,256]{1,0:T(8,128)(2,1)} %get-tuple-element.28), channel_id=1, source_target_pairs={{0,1},{1,2},{2,3},{3,0},{4,5},{5,6},{6,7},{7,4},{8,9},{9,10},{10,1... | collective-permute-start | bytes 1228808 | tf_op jit(solution)/shard_map/ppermute | solution.py:317
  16.0 28.7 %collective-permute-start.2 = (bf16[800,256]{1,0:T(8,128)(2,1)}, bf16[800,256]{1,0:T(8,128)(2,1)S(1)}, u32[]{:S(2)}, u32[]{:S(2)}) collective-permute-start(bf16[800,256]{1,0:T(8,128)(2,1)} %get-tuple-element.29), channel_id=1, source_target_pairs={{0,2},{1,3},{2,0},{3,1},{4,6},{5,7},{6,4},{7,5},{8,10},{9,11},{10,... | collective-permute-start | bytes 1228808 | tf_op jit(solution)/shard_map/ppermute | solution.py:317
  17.6 27.2 %collective-permute-start.3 = (bf16[800,256]{1,0:T(8,128)(2,1)}, bf16[800,256]{1,0:T(8,128)(2,1)S(1)}, u32[]{:S(2)}, u32[]{:S(2)}) collective-permute-start(bf16[800,256]{1,0:T(8,128)(2,1)} %get-tuple-element.30), channel_id=1, source_target_pairs={{0,3},{1,0},{2,1},{3,2},{4,7},{5,4},{6,5},{7,6},{8,11},{9,8},{10,9... | collective-permute-start | bytes 1228808 | tf_op jit(solution)/shard_map/ppermute | solution.py:317
  20.0 25.5 %collective-permute-start.4 = (bf16[800,256]{1,0:T(8,128)(2,1)}, bf16[800,256]{1,0:T(8,128)(2,1)}, u32[]{:S(2)}, u32[]{:S(2)}) collective-permute-start(bf16[800,256]{1,0:T(8,128)(2,1)} %get-tuple-element.31), channel_id=1, source_target_pairs={{0,3},{1,0},{2,1},{3,2},{4,7},{5,4},{6,5},{7,6},{8,11},{9,8},{10,9... | collective-permute-start | bytes 1228808 | tf_op jit(solution)/shard_map/ppermute | solution.py:317
  26.6 24.9 %copy-start.2 = (bf16[800,256]{1,0:T(8,128)(2,1)}, bf16[800,256]{1,0:T(8,128)(2,1)S(1)}, u32[]{:S(2)}) copy-start(bf16[800,256]{1,0:T(8,128)(2,1)S(1)} %collective-permute-done.refs_1_) | copy-start | bytes 1228804
  34.8 10.0 %copy-start.4 = (bf16[800,256]{1,0:T(8,128)(2,1)}, bf16[800,256]{1,0:T(8,128)(2,1)S(1)}, u32[]{:S(2)}) copy-start(bf16[800,256]{1,0:T(8,128)(2,1)S(1)} %collective-permute-done.1.refs_1_) | copy-start | bytes 1228804
  44.8 0.8 copy-start.5
  45.5 6.0 %copy-start.3 = (bf16[800,256]{1,0:T(8,128)(2,1)}, bf16[800,256]{1,0:T(8,128)(2,1)S(1)}, u32[]{:S(2)}) copy-start(bf16[800,256]{1,0:T(8,128)(2,1)S(1)} %collective-permute-done.3.refs_3_) | copy-start | bytes 1228804
  51.5 8.0 %copy-start.6 = (bf16[800,256]{1,0:T(8,128)(2,1)S(1)}, bf16[800,256]{1,0:T(8,128)(2,1)}, u32[]{:S(2)}) copy-start(bf16[800,256]{1,0:T(8,128)(2,1)} %get-tuple-element.35) | copy-start | bytes 1228804
  51.5 43.7 %all-to-all-start.1 = ((bf16[128,80,128]{2,1,0:T(8,128)(2,1)}), bf16[128,80,128]{2,1,0:T(8,128)(2,1)S(1)}, u32[]{:S(2)}, u32[]{:S(2)}) async-start(bf16[128,80,128]{2,1,0:T(8,128)(2,1)} %bitcast.13), calls=%async_computation.1 | async-start | bytes 5242880 | tf_op jit(solution)/shard_map/all_to_all | solution.py:333
  59.5 41.2 %collective-permute-start.5 = (bf16[800,256]{1,0:T(8,128)(2,1)S(1)}, bf16[800,256]{1,0:T(8,128)(2,1)S(1)}, u32[]{:S(2)}, u32[]{:S(2)}) collective-permute-start(bf16[800,256]{1,0:T(8,128)(2,1)S(1)} %copy-done.6), channel_id=1, source_target_pairs={{0,2},{1,3},{2,0},{3,1},{4,6},{5,7},{6,4},{7,5},{8,10},{9,11},{10,... | collective-permute-start | bytes 1228808 | tf_op jit(solution)/shard_map/ppermute | solution.py:317
  97.3 14.8 %copy-start = (bf16[200,256]{1,0:T(8,128)(2,1)}, bf16[200,256]{1,0:T(8,128)(2,1)S(1)}, u32[]{:S(2)}) copy-start(bf16[200,256]{1,0:T(8,128)(2,1)S(1)} %apply.3.refs_4_) | copy-start | bytes 307204
  97.3 10.1 %collective-permute-start.10 = (bf16[200,256]{1,0:T(8,128)(2,1)S(1)}, bf16[200,256]{1,0:T(8,128)(2,1)S(1)}, u32[]{:S(2)}, u32[]{:S(2)}) collective-permute-start(bf16[200,256]{1,0:T(8,128)(2,1)S(1)} %apply.3.refs_4_), channel_id=1, source_target_pairs={{0,2},{1,3},{2,0},{3,1},{4,6},{5,7},{6,4},{7,5},{8,10},{9,11},{10,... | collective-permute-start | bytes 307208 | tf_op jit(solution)/shard_map/ppermute | solution.py:317
  98.4 9.2 %collective-permute-start.11 = (bf16[200,256]{1,0:T(8,128)(2,1)S(1)}, bf16[200,256]{1,0:T(8,128)(2,1)S(1)}, u32[]{:S(2)}, u32[]{:S(2)}) collective-permute-start(bf16[200,256]{1,0:T(8,128)(2,1)S(1)} %apply.3.refs_4_), channel_id=1, source_target_pairs={{0,3},{1,0},{2,1},{3,2},{4,7},{5,4},{6,5},{7,6},{8,11},{9,8},{10,9... | collective-permute-start | bytes 307208 | tf_op jit(solution)/shard_map/ppermute | solution.py:317
  100.7 6.8 %collective-permute-start.9 = (bf16[200,256]{1,0:T(8,128)(2,1)S(1)}, bf16[200,256]{1,0:T(8,128)(2,1)S(1)}, u32[]{:S(2)}, u32[]{:S(2)}) collective-permute-start(bf16[200,256]{1,0:T(8,128)(2,1)S(1)} %apply.3.refs_4_), channel_id=1, source_target_pairs={{0,1},{1,2},{2,3},{3,0},{4,5},{5,6},{6,7},{7,4},{8,9},{9,10},{10,1... | collective-permute-start | bytes 307208 | tf_op jit(solution)/shard_map/ppermute | solution.py:317
  102.6 9.4 %copy-start.1 = (bf16[200,256]{1,0:T(8,128)(2,1)}, bf16[200,256]{1,0:T(8,128)(2,1)S(1)}, u32[]{:S(2)}) copy-start(bf16[200,256]{1,0:T(8,128)(2,1)S(1)} %apply.2.refs_0_) | copy-start | bytes 307204
  102.6 7.0 %collective-permute-start.6 = (bf16[200,256]{1,0:T(8,128)(2,1)S(1)}, bf16[200,256]{1,0:T(8,128)(2,1)S(1)}, u32[]{:S(2)}, u32[]{:S(2)}) collective-permute-start(bf16[200,256]{1,0:T(8,128)(2,1)S(1)} %apply.2.refs_0_), channel_id=1, source_target_pairs={{0,1},{1,2},{2,3},{3,0},{4,5},{5,6},{6,7},{7,4},{8,9},{9,10},{10,1... | collective-permute-start | bytes 307208 | tf_op jit(solution)/shard_map/ppermute | solution.py:317
  103.8 8.0 %collective-permute-start.7 = (bf16[200,256]{1,0:T(8,128)(2,1)S(1)}, bf16[200,256]{1,0:T(8,128)(2,1)S(1)}, u32[]{:S(2)}, u32[]{:S(2)}) collective-permute-start(bf16[200,256]{1,0:T(8,128)(2,1)S(1)} %apply.2.refs_0_), channel_id=1, source_target_pairs={{0,2},{1,3},{2,0},{3,1},{4,6},{5,7},{6,4},{7,5},{8,10},{9,11},{10,... | collective-permute-start | bytes 307208 | tf_op jit(solution)/shard_map/ppermute | solution.py:317
  107.4 4.7 %collective-permute-start.8 = (bf16[200,256]{1,0:T(8,128)(2,1)S(1)}, bf16[200,256]{1,0:T(8,128)(2,1)S(1)}, u32[]{:S(2)}, u32[]{:S(2)}) collective-permute-start(bf16[200,256]{1,0:T(8,128)(2,1)S(1)} %apply.2.refs_0_), channel_id=1, source_target_pairs={{0,3},{1,0},{2,1},{3,2},{4,7},{5,4},{6,5},{7,6},{8,11},{9,8},{10,9... | collective-permute-start | bytes 307208 | tf_op jit(solution)/shard_map/ppermute | solution.py:317
